TPU v7x, 128 devices: a whole 4x4x4 slice. The times are simulated.
128 devices in a mesh: row: 16 (over x, y), col: 8 (over z, core).
Axes of the slice: x: 4, y: 4, z: 4, core: 2. Of those that a mesh axis runs over, the one named last changes fastest.
Arguments:
- image_student: bfloat16 [16384, 512], P(('row', 'col')), may hold values from -18 to 18
- text_student: bfloat16 [16384, 512], P(('col', 'row')), may hold values from -18 to 18
- image_teacher: bfloat16 [16384, 1280], P(('row', 'col')), may hold values from -18 to 18
- text_teacher: bfloat16 [16384, 1280], P(('col', 'row')), may hold values from -18 to 18
- sketch: bfloat16 [1280, 512], replicated, may hold values from -0.15625 to 0.15625
Outputs:
- grad_image: float32 [16384, 512], P(('row', 'col'))
- grad_text: float32 [16384, 512], P(('col', 'row'))
- mean_loss: float32 [], replicated
All inputs are finite; a program needn't handle non-finite values.
Results may differ from a plain program's by a relative error of at most 0.012.
Values may be sent and summed in bfloat16 or wider, within the bound.
No kernel may reach another device: no remote copies, remote signals or barrier semaphores. Data moves between devices by JAX's collectives and lax.ppermute only.
A program may use at most 128 MiB of HBM per device.

v0:
```python
import math

import jax
import jax.numpy as jnp
from jax import lax
from jax.experimental import pallas as pl
from jax.experimental.pallas import tpu as pltpu
from jax.sharding import PartitionSpec as P

scale = 100.0
LOG2E = math.log2(math.e)
units = scale * LOG2E
SIDE = 4
CORES = 2
AXES = ("row", "col")


def route(step):
    pairs = []
    for x in range(SIDE):
        for y in range(SIDE):
            for z in range(SIDE):
                for k in range(CORES):
                    a, b, c, d = step(x, y, z, k)
                    src = ((x * SIDE + y) * SIDE + z) * CORES + k
                    dst = ((a * SIDE + b) * SIDE + c) * CORES + d
                    pairs.append((src, dst))
    return pairs


def first(e):
    return route(lambda x, y, z, k: (x ^ e, y, z, k) if k == 0 else (x, y ^ e, z, k))


def second(e):
    return route(lambda x, y, z, k: (x, y ^ e, z, k) if k == 0 else (x ^ e, y, z, k))


def along_z(e):
    return route(lambda x, y, z, k: (x, y, z ^ e, k))


def x_or_z(e):
    return route(lambda x, y, z, k: (x ^ e, y, z, k) if k == 0 else (x, y, z ^ e, k))


def along_y(e):
    return route(lambda x, y, z, k: (x, y ^ e, z, k))


def other_core():
    return route(lambda x, y, z, k: (x, y, z, k ^ 1))


def send(x, pairs):
    return lax.ppermute(x, AXES, pairs)


BF16 = jnp.bfloat16
F32 = jnp.float32
NT = (((1,), (1,)), ((), ()))
TN = (((0,), (0,)), ((), ()))
VMEM_LIMIT = 16 * 1024 * 1024
FIRST_LIMIT = 56 * 1024 * 1024
TAIL = 16
BLOCK = 256
SHIFT = 34.0
LOWEST = -60.0


def dot(a, b, dims=(((1,), (0,)), ((), ()))):
    return lax.dot_general(a, b, dims, preferred_element_type=F32)


def call(kernel, out_shape, args, flops=0, scratch=(), hbm=0, limit=VMEM_LIMIT, scalar=None):
    size = sum(a.size * a.dtype.itemsize for a in args)
    size += sum(math.prod(o.shape) * o.dtype.itemsize for o in jax.tree.leaves(out_shape))
    return pl.pallas_call(
        kernel,
        out_shape=out_shape,
        in_specs=[pl.BlockSpec(memory_space=pltpu.HBM)] * hbm + [pl.BlockSpec(memory_space=pltpu.VMEM)] * (len(args) - hbm),
        out_specs=jax.tree.map(
            lambda o: pl.BlockSpec(memory_space=pltpu.SMEM if o is scalar else pltpu.VMEM), out_shape
        ),
        scratch_shapes=scratch,
        compiler_params=pltpu.CompilerParams(vmem_limit_bytes=limit),
        cost_estimate=pl.CostEstimate(flops=flops, bytes_accessed=size, transcendentals=0),
    )(*args)


def unit_rows(x):
    x32 = x.astype(F32)
    norms = jnp.sqrt(jnp.sum(x32 * x32, axis=-1, keepdims=True) + 1e-06)
    return (x32 / norms, norms)


def unit_block(student, teacher, sketch, out_ref):
    width = student.shape[1]
    out_ref[:, :width] = unit_rows(student)[0].astype(BF16)
    out_ref[:, width:] = unit_rows(dot(teacher, sketch))[0].astype(BF16)


def prepare_first_kernel(student_hbm, teacher_hbm, sketch_hbm, out_ref, *refs):
    *buffers, sems = refs
    copies = [
        pltpu.make_async_copy(src, dst, sems.at[n])
        for n, (src, dst) in enumerate(zip((student_hbm, teacher_hbm, sketch_hbm), buffers))
    ]
    for copy in copies:
        copy.start()
    for copy in copies:
        copy.wait()
    unit_block(*(ref[...] for ref in buffers), out_ref)


def prepare_kernel(student_ref, teacher_ref, sketch_ref, out_ref):
    unit_block(student_ref[...], teacher_ref[...], sketch_ref[...], out_ref)


def prepare(student, teacher, sketch, first_kernel):
    rows, width = student.shape
    out = jax.ShapeDtypeStruct((rows, 2 * width), BF16)
    args = (student, teacher, sketch)
    flops = 2 * rows * sketch.size
    if not first_kernel:
        return call(prepare_kernel, out, args, flops)
    scratch = [pltpu.VMEM(x.shape, x.dtype) for x in args] + [pltpu.SemaphoreType.DMA((len(args),))]
    return call(prepare_first_kernel, out, args, flops, scratch, hbm=3, limit=FIRST_LIMIT)


def lay_end_kernel(*refs):
    txt_refs, img_refs, (low_ref, high_ref, img_ref) = refs[:SIDE], refs[SIDE : 2 * SIDE], refs[2 * SIDE :]
    rows = img_refs[0].shape[0]
    for n in range(SIDE):
        img_ref[n * rows : (n + 1) * rows, :] = img_refs[n][...]
        half = low_ref if n < SIDE // 2 else high_ref
        at = n % (SIDE // 2) * rows
        half[at : at + rows, :] = txt_refs[n][...]


def lay_end(txt, img):
    rows, width = txt[0].shape
    half = jax.ShapeDtypeStruct((SIDE // 2 * rows, width), BF16)
    out = (half, half, jax.ShapeDtypeStruct((SIDE * rows, width), BF16))
    return call(lay_end_kernel, out, (*txt, *img))


def products(img, txt_refs):
    width = img.shape[1] // 2
    p = [dot(img[:, width:], ref[:, width:], NT) for ref in txt_refs]
    q = [dot(img[:, :width], ref[:, :width], NT) for ref in txt_refs]
    return jnp.concatenate(p, axis=1), jnp.concatenate(q, axis=1)


def logits(img, txt_refs):
    p, q = products(img, txt_refs)
    return units * p, units * q


def load_block(n, own_ref, other_ref, block_ref):
    half = own_ref.shape[0] // BLOCK

    @pl.when(n < half)
    def _():
        block_ref[...] = own_ref[pl.ds(pl.multiple_of(n * BLOCK, BLOCK), BLOCK), :]

    @pl.when(n >= half)
    def _():
        block_ref[...] = other_ref[pl.ds(pl.multiple_of((n - half) * BLOCK, BLOCK), BLOCK), :]


def put_rows(row_ref, n, first, second, third):
    lane = lax.broadcasted_iota(jnp.int32, (BLOCK, 128), 1)
    packed = jnp.where(lane == 0, first, jnp.where(lane == 1, second, third))
    for k in range(BLOCK // 128):
        at = pl.multiple_of(n * BLOCK + k * 128, 128)
        row_ref[:, pl.ds(at, 128)] = packed[k * 128 : (k + 1) * 128].T[:8]


def stack_rows(first, second, third, shape):
    sub = lax.broadcasted_iota(jnp.int32, shape, 0)
    return jnp.where(sub == 0, first, jnp.where(sub == 1, second, third))


def stats_kernel(has_old, own_ref, other_ref, low_ref, high_ref, *refs):
    txt_refs = (low_ref, high_ref)
    old_ref = refs[0] if has_old else None
    row_ref, col_ref, block_ref = refs[int(has_old) :]
    columns = col_ref.shape[1]
    blocks = 2 * own_ref.shape[0] // BLOCK

    def step(n, state):
        load_block(n, own_ref, other_ref, block_ref)
        p, q = products(block_ref[...], txt_refs)
        ep = jnp.exp2(units * p - SHIFT)
        eq = jnp.exp2(units * q - SHIFT)
        ed = ep * (p - q)
        put_rows(row_ref, n, *(jnp.sum(x, axis=1, keepdims=True) for x in (ep, eq, ed)))
        return tuple(s + jnp.sum(x, axis=0, keepdims=True) for s, x in zip(state, (ep, eq, ed)))

    zero = jnp.zeros((1, columns), F32)
    sp, sq, u = lax.fori_loop(0, blocks, step, (zero, zero, zero))
    rows = row_ref[...]
    lowest = jnp.minimum(jnp.min(rows[0:2, :]), jnp.min(jnp.minimum(sp, sq)))
    col_ref[...] = stack_rows(SHIFT + jnp.log2(sp), SHIFT + jnp.log2(sq), units * u / sp, col_ref.shape)
    row_ref[...] = stack_rows(SHIFT + jnp.log2(rows), SHIFT + jnp.log2(rows), units * rows / rows[0:1], rows.shape)

    @pl.when(lowest < 2.0 ** (LOWEST - SHIFT))
    def _():
        careful_stats(own_ref, other_ref, txt_refs, row_ref, col_ref, block_ref)

    if has_old:
        new, old = row_ref[...], old_ref[...]
        top = jnp.maximum(new, old)
        new_w, old_w = jnp.exp2(new - top), jnp.exp2(old - top)
        total = new_w + old_w
        mean = (new_w[0:1] * new + old_w[0:1] * old) / total[0:1]
        lse = top + jnp.log2(total)
        row_ref[...] = stack_rows(lse, lse, mean, new.shape)


def careful_stats(own_ref, other_ref, txt_refs, row_ref, col_ref, block_ref):
    columns = col_ref.shape[1]

    def step(n, state):
        load_block(n, own_ref, other_ref, block_ref)
        p, q = logits(block_ref[...], txt_refs)
        d = p - q
        mp = jnp.max(p, axis=1, keepdims=True)
        mq = jnp.max(q, axis=1, keepdims=True)
        e = jnp.exp2(p - mp)
        sp = jnp.sum(e, axis=1, keepdims=True)
        u = jnp.sum(e * d, axis=1, keepdims=True)
        sq = jnp.sum(jnp.exp2(q - mq), axis=1, keepdims=True)
        put_rows(row_ref, n, mp + jnp.log2(sp), mq + jnp.log2(sq), u / sp)
        mp = jnp.maximum(jnp.max(p, axis=0, keepdims=True), state[0])
        mq = jnp.maximum(jnp.max(q, axis=0, keepdims=True), state[3])
        e = jnp.exp2(p - mp)
        old = jnp.exp2(state[0] - mp)
        sp = jnp.sum(e, axis=0, keepdims=True) + old * state[1]
        u = jnp.sum(e * d, axis=0, keepdims=True) + old * state[2]
        sq = jnp.sum(jnp.exp2(q - mq), axis=0, keepdims=True) + jnp.exp2(state[3] - mq) * state[4]
        return (mp, sp, u, mq, sq)

    low = jnp.full((1, columns), -1e30, F32)
    zero = jnp.zeros((1, columns), F32)
    blocks = 2 * own_ref.shape[0] // BLOCK
    mp, sp, u, mq, sq = lax.fori_loop(0, blocks, step, (low, zero, zero, low, zero))
    col_ref[...] = stack_rows(mp + jnp.log2(sp), mq + jnp.log2(sq), u / sp, col_ref.shape)


def tile_stats(own, other, txt, old):
    columns = 2 * txt[0].shape[0]
    rows = 2 * own.shape[0]
    args = [own, other, *txt] + ([] if old is None else [old])
    return call(
        lambda *refs: stats_kernel(old is not None, *refs),
        (jax.ShapeDtypeStruct((8, rows), F32), jax.ShapeDtypeStruct((8, columns), F32)),
        args,
        2 * rows * columns * own.shape[1],
        scratch=[pltpu.VMEM((BLOCK, own.shape[1]), BF16)],
    )


def merge(parts):
    top = parts[0]
    for part in parts[1:]:
        top = jnp.maximum(top, part)
    weights = [jnp.exp2(part - top) for part in parts]
    total = sum(weights)
    mean = sum(pltpu.roll(w, 2, 0) * part for w, part in zip(weights, parts)) / pltpu.roll(total, 2, 0)
    sub = lax.broadcasted_iota(jnp.int32, top.shape, 0)
    return jnp.where((sub == 2) | (sub == 5), mean, top + jnp.log2(total))


def on_core(core):
    return pl.when(lax.rem(lax.axis_index("col"), CORES) == core)


def lanes(*index):
    at = 0
    for i in index:
        at = at * SIDE + i
    return slice(at * 128, (at + 1) * 128)


def rows_3(first, second):
    return jnp.concatenate([first[:3], second[:3], first[:2]], axis=0)


def local_kernel(row_ref, c0, c1, c2, c3, out_ref):
    def columns(second, first):
        half, at = divmod(first, SIDE // 2)
        if second in (0, 2):
            return (c0 if second == 0 else c3)[:, lanes(first)]
        return (c1, c2)[half][:, lanes(at + (0 if second == 1 else 2))]

    for core in range(CORES):

        @on_core(core)
        def _():
            for x in range(SIDE):
                for y in range(SIDE):
                    col = columns(y, x) if core == 0 else columns(x, y)
                    row = col
                    if x < CORES:
                        row = row_ref[:, lanes(x if core == 0 else 1 - x, y)]
                    out_ref[:, lanes(x, y)] = rows_3(col, row)


def chip_kernel(own_ref, got_ref, out_ref):
    @on_core(0)
    def _():
        out_ref[...] = rows_3(own_ref[...], got_ref[...])

    @on_core(1)
    def _():
        rows = merge([jnp.concatenate([r[3:6, :1024], r[3:6, :1024], r[:2, :1024]], axis=0) for r in (own_ref, got_ref)])
        out_ref[...] = jnp.zeros(out_ref.shape, F32)
        for z in range(SIDE):
            out_ref[:, lanes(z, 0)] = rows_3(rows[:, lanes(0, z)], rows[:, lanes(1, z)])


def line_kernel(own_ref, g1, g2, g3, out_ref):
    width = own_ref.shape[1] // SIDE
    got = (own_ref, g1, g2, g3)
    for n in range(SIDE):
        parts = [got[e][:, (n ^ e) * width : ((n ^ e) + 1) * width] for e in range(SIDE)]
        out_ref[:, n * width : (n + 1) * width] = merge(parts)


def split_kernel(own_ref, got_ref, col_ref, row_ref):
    for core in range(CORES):

        @on_core(core)
        def _():
            cols, rows = (own_ref, got_ref) if core == 0 else (got_ref, own_ref)
            col_ref[...] = rows_3(cols[3 * core :, :][:3], cols[3 * core :, :][:3])
            for k in range(CORES):
                first = 3 * (k ^ core)
                for z in range(SIDE):
                    part = rows[:, lanes(z, 0)][first : first + 3]
                    row_ref[:, lanes(k, z)] = rows_3(part, part)


def plane_kernel(own_ref, g1, g2, g3, out_ref):
    got = (own_ref, g1, g2, g3)
    for x in range(SIDE):
        for y in range(SIDE):
            part = merge([got[e][:, lanes(x, y ^ e)] for e in range(SIDE)])

            @on_core(0)
            def _():
                out_ref[:, lanes(y, x)] = part

            @on_core(1)
            def _():
                out_ref[:, lanes(x, y)] = part


def exchange(row, cols):
    out = jax.ShapeDtypeStruct((8, len(cols) * cols[0].shape[1]), F32)
    local = call(local_kernel, out, (row, *cols))
    chip = call(chip_kernel, out, (local, send(local, other_core())))
    line = call(line_kernel, out, (chip, *(send(chip, x_or_z(e)) for e in range(1, SIDE))))
    col, row = call(split_kernel, (out, jax.ShapeDtypeStruct(row.shape, F32)), (line, send(line, other_core())))
    return call(plane_kernel, out, (col, *(send(col, along_y(e)) for e in range(1, SIDE)))), row


def kl_sum(stats):
    kl = stats[2:3, :] - (stats[0:1, :] - stats[1:2, :])
    return jnp.sum(kl, axis=1, keepdims=True)


def put_tail(ref, at, value):
    shape = (TAIL, ref.shape[1])
    rest = jnp.broadcast_to(value, shape)
    sub = lax.broadcasted_iota(jnp.int32, shape, 0)
    tail = jnp.zeros(shape, F32)
    for n in range(3):
        part = rest.astype(BF16).astype(F32)
        tail = jnp.where(sub == n, part, tail)
        rest = rest - part
    ref[at : at + TAIL, :] = tail.astype(BF16)


def get_tail(ref, at):
    return jnp.sum(ref[at : at + TAIL, :].astype(F32), axis=0, keepdims=True)


def grad_kernel(piece, own_ref, other_ref, low_ref, high_ref, row_ref, col_ref, *refs):
    txt_refs = (low_ref, high_ref)
    *got, g_ref, out_ref, block_ref = refs
    columns = g_ref.shape[1]
    width = own_ref.shape[1] // 2
    half = own_ref.shape[0]
    blocks = 2 * half // BLOCK
    stats = col_ref[:, piece * columns : (piece + 1) * columns]
    lowest = jnp.minimum(jnp.min(row_ref[0:2, :]), jnp.min(stats[0:2, :]))

    def turned(n, x):
        out = []
        for k in range(BLOCK // 128):
            at = pl.multiple_of(n * BLOCK + k * 128, 128)
            out.append(jnp.concatenate([x(row_ref[:, pl.ds(at, 128)])] * 16, axis=0).T)
        out = jnp.concatenate(out, axis=0)
        return out[:, 0:1], out[:, 1:2]

    @pl.when(lowest >= LOWEST)
    def _():
        col = jnp.exp2(SHIFT - 1.0 - stats)

        def step(n, _):
            load_block(n, own_ref, other_ref, block_ref)
            rp, rq = turned(n, lambda x: jnp.exp2(SHIFT - 1.0 - x))
            p, q = logits(block_ref[...], txt_refs)
            g = jnp.exp2(q - SHIFT) * (rq + col[1:2, :]) - jnp.exp2(p - SHIFT) * (rp + col[0:1, :])
            g_ref[pl.ds(pl.multiple_of(n * BLOCK, BLOCK), BLOCK), :] = g.astype(BF16)
            return 0

        lax.fori_loop(0, blocks, step, 0)

    @pl.when(lowest < LOWEST)
    def _():
        cp = stats[0:1, :] + 1.0
        cq = stats[1:2, :] + 1.0

        def step(n, _):
            load_block(n, own_ref, other_ref, block_ref)
            rp, rq = turned(n, lambda x: x + 1.0)
            p, q = logits(block_ref[...], txt_refs)
            g = (jnp.exp2(q - rq) - jnp.exp2(p - rp)) + (jnp.exp2(q - cq) - jnp.exp2(p - cp))
            g_ref[pl.ds(pl.multiple_of(n * BLOCK, BLOCK), BLOCK), :] = g.astype(BF16)
            return 0

        lax.fori_loop(0, blocks, step, 0)

    total = dot(g_ref[:half, :], own_ref[:, :width], TN) + dot(g_ref[half:, :], other_ref[:, :width], TN)
    if got:
        out_ref[...] = total + got[0][:columns, :].astype(F32)
    else:
        out_ref[:columns, :] = total.astype(BF16)
        put_tail(out_ref, columns, kl_sum(row_ref[...]))


def tile_grad(own, other, txt, row, col, piece, got=None):
    rows = own.shape[0] + other.shape[0]
    columns, width = 2 * txt[0].shape[0], own.shape[1]
    shape = jax.ShapeDtypeStruct
    out = shape((columns + TAIL, width // 2), BF16) if got is None else shape((columns, width // 2), F32)
    return call(
        lambda *refs: grad_kernel(piece, *refs),
        (shape((rows, columns), BF16), out),
        (own, other, *txt, row, col) + (() if got is None else (got,)),
        3 * rows * columns * width,
        scratch=[pltpu.VMEM((BLOCK, width), BF16)],
    )


def image_rows(first, half, grad_refs, txt_refs, store):
    rows, width = txt_refs[0].shape
    width //= 2

    def step(n, _):
        at = pl.multiple_of(n * BLOCK, BLOCK)
        total = None
        for m, txt_ref in enumerate(txt_refs):
            at_column = m % 2 * rows
            part = dot(grad_refs[m // 2][pl.ds(first + at, BLOCK), at_column : at_column + rows], txt_ref[:, :width])
            total = part if total is None else total + part
        store(pl.ds(at, BLOCK), total)
        return 0

    lax.fori_loop(0, half // BLOCK, step, 0)


def other_images_kernel(*refs):
    grad_refs, txt_refs = refs[:SIDE], refs[SIDE : 3 * SIDE]
    stats_ref, own_ref, got_ref, out_ref, sum_ref = refs[3 * SIDE :]
    half = out_ref.shape[0] - TAIL
    sum_ref[...] = own_ref[...] + got_ref[: own_ref.shape[0], :].astype(F32)

    def store(span, value):
        out_ref[span, :] = value.astype(BF16)

    image_rows(half, half, grad_refs, txt_refs, store)
    put_tail(out_ref, half, kl_sum(stats_ref[...]))


def own_images_kernel(*refs):
    grad_refs, txt_refs = refs[:SIDE], refs[SIDE : 3 * SIDE]
    out_ref = refs[-5]
    image_rows(0, out_ref.shape[0], grad_refs, txt_refs, lambda span, value: out_ref.__setitem__((span, slice(None)), value))
    combine_kernel(2, *refs[3 * SIDE : -5], *refs[-4:])


def image_grads(grads, txts, every, row, own, got):
    rows, columns = grads[0].shape
    txts = [half for piece in txts for half in piece]
    width = txts[0].shape[1] // 2
    half = rows // 2
    shape = jax.ShapeDtypeStruct
    flops = half * columns * SIDE * width * 2
    message, own = call(
        other_images_kernel,
        (shape((half + TAIL, width), BF16), shape(own.shape, F32)),
        (*grads, *txts, every, own, got[1]),
        flops,
    )
    step = own.shape[0] // SIDE
    out = shape((step + TAIL, width), BF16)
    own_img, *texts = call(
        own_images_kernel,
        (shape((half, width), F32), shape((step + 8, width), F32), out, out, out),
        (*grads, *txts, own, row, *got),
        flops,
    )
    return message, own_img, texts


def combine_kernel(added, own_ref, stats_ref, *refs):
    count = len(refs) - SIDE
    got, (keep_ref, *out) = refs[:count], refs[count:]
    size = own_ref.shape[0]
    step = size // SIDE
    value = kl_sum(stats_ref[...]) + sum(get_tail(ref, size) for ref in got)
    for n, ref in enumerate([keep_ref, *out]):
        span = slice(n * step, (n + 1) * step)
        total = own_ref[span, :]
        for part in got[added:]:
            total = total + part[span, :].astype(F32)
        ref[:step, :] = total.astype(ref.dtype)
        if n:
            put_tail(ref, step, value)
        else:
            ref[step:, :] = jnp.broadcast_to(value, (8, value.shape[1]))


def combine(own, stats, got):
    size, width = own.shape
    step = size // SIDE
    message = jax.ShapeDtypeStruct((step + TAIL, width), BF16)
    keep = jax.ShapeDtypeStruct((step + 8, width), F32)
    out = (keep, message, message, message)
    return call(lambda *refs: combine_kernel(0, *refs), out, (own, stats, *got))


def tangent(x_ref, keep_ref, got, grad_ref):
    rows = x_ref.shape[0]
    u, n = unit_rows(x_ref[...])
    du = scale * (keep_ref[:rows, :] + sum(ref[:rows, :].astype(F32) for ref in got))
    grad_ref[...] = (du - u * jnp.sum(u * du, axis=-1, keepdims=True)) / n
    return keep_ref[rows : rows + 1, :] + sum(get_tail(ref, rows) for ref in got)


def finish_kernel(factor, *refs):
    *ins, grad_image_ref, grad_text_ref, loss_ref = refs
    each = len(ins) // 2
    value = jnp.zeros((1, grad_text_ref.shape[1]), F32)
    for n, grad_ref in enumerate((grad_image_ref, grad_text_ref)):
        x_ref, keep_ref, *got = ins[n * each : (n + 1) * each]
        value = value + tangent(x_ref, keep_ref, got, grad_ref)
    loss_ref[0, 0] = factor * jnp.max(value)


def finish(image, text, factor):
    loss = jax.ShapeDtypeStruct((1, 1), F32)
    out = tuple(jax.ShapeDtypeStruct(x.shape, F32) for x in (image[0], text[0])) + (loss,)
    return call(lambda *refs: finish_kernel(factor, *refs), out, (*image, *text), scalar=loss)


def shards(image_student, text_student, image_teacher, text_teacher, sketch):
    rows, width = image_student.shape
    txt = prepare(text_student, text_teacher, sketch, True)
    img = prepare(image_student, image_teacher, sketch, False)

    low, high, own = lay_end(
        [txt] + [send(txt, first(e)) for e in range(1, SIDE)],
        [img] + [send(img, along_z(e)) for e in range(1, SIDE)],
    )
    low_1, low_3 = send(low, second(1)), send(low, second(3))
    high_1, high_3 = send(high, second(1)), send(high, second(3))
    low_2, high_2 = send(low_3, second(1)), send(high_1, second(3))
    txt_all = [(low, high), (low_1, high_1), (low_2, high_2), (low_3, high_3)]
    other = send(own, other_core())

    row, cols = None, []
    for pair in ((low, high), (low_1, low_3), (high_1, high_3), (low_2, high_2)):
        row, col = tile_stats(own, other, pair, row)
        cols.append(col)
    col, row = exchange(row, cols)

    grads, got = [None] * SIDE, []
    for b in (2, 1, 3):
        grads[b], message = tile_grad(own, other, txt_all[b], row, col, b)
        got.append(send(message, second(b)))
    grads[0], own_txt = tile_grad(own, other, txt_all[0], row, col, 0, got[0])
    message, own_img, (keep_txt, *messages_txt) = image_grads(grads, txt_all, col, row, own_txt, got)
    keep, *messages = combine(own_img, col, [send(message, other_core())])
    image = [image_student, keep] + [send(m, along_z(e)) for e, m in enumerate(messages, 1)]
    text = [text_student, keep_txt] + [send(m, first(e)) for e, m in enumerate(messages_txt, 1)]
    pairs = rows * lax.axis_size("row") * lax.axis_size("col")
    grad_image, grad_text, mean_loss = finish(image, text, 0.5 / (LOG2E * pairs))
    return (grad_image, grad_text, mean_loss.reshape(()))


def solution(mesh):
    return jax.shard_map(
        shards,
        mesh=mesh,
        in_specs=(
            P(("row", "col"), None),
            P(("col", "row"), None),
            P(("row", "col"), None),
            P(("col", "row"), None),
            P(),
        ),
        out_specs=(P(("row", "col"), None), P(("col", "row"), None), P()),
        check_vma=False,
    )
```

profile of v0, /device:TPU:0, one launch (start us, length us, event | category | flops | bytes accessed | tf_op | source)
XLA Modules:
  0.0 112.5 jit_solution(5343630809009677990)
XLA Ops:
  0.7 2.8 %shard_map.76.refs_0_ = bf16[128,1024]{1,0:T(8,128)(2,1)} custom-call(bf16[128,512]{1,0:T(8,128)(2,1)} %refs_5_.1, bf16[128,1280]{1,0:T(8,128)(2,1)} %teacher_hbm.1, bf16[1280,512]{1,0:T(8,128)(2,1)} %sketch_ref.1), custom_call_target="tpu_custom_call" | custom-call | flops 167772160 | bytes 2031616 | tf_op jit(solution)/shard_map/pallas_call | solution.py:78
  3.4 2.9 %collective-permute-start.2 = (bf16[128,1024]{1,0:T(8,128)(2,1)}, bf16[128,1024]{1,0:T(8,128)(2,1)S(1)}, u32[]{:S(2)}, u32[]{:S(2)}) collective-permute-start(bf16[128,1024]{1,0:T(8,128)(2,1)} %shard_map.76.refs_0_), channel_id=1, source_target_pairs={{0,96},{1,25},{2,98},{3,27},{4,100},{5,29},{6,102},{7,31},{8,104},... | collective-permute-start | bytes 786440 | tf_op jit(solution)/shard_map/ppermute | solution.py:56
  6.4 0.8 collective-permute-start.1
  8.1 4.2 %collective-permute-start.5 = (bf16[128,1024]{1,0:T(8,128)(2,1)S(1)}, bf16[128,1024]{1,0:T(8,128)(2,1)S(1)}, u32[]{:S(2)}, u32[]{:S(2)}) collective-permute-start(bf16[128,1024]{1,0:T(8,128)(2,1)S(1)} %shard_map.77.refs_4_), channel_id=1, source_target_pairs={{0,6},{1,7},{2,4},{3,5},{4,2},{5,3},{6,0},{7,1},{8,14},{9,15},{10,... | collective-permute-start | bytes 786440 | tf_op jit(solution)/shard_map/ppermute | solution.py:56
  12.3 1.1 collective-permute-done.2.refs_3_
  13.4 1.9 %collective-permute-start.3 = (bf16[128,1024]{1,0:T(8,128)(2,1)S(1)}, bf16[128,1024]{1,0:T(8,128)(2,1)S(1)}, u32[]{:S(2)}, u32[]{:S(2)}) collective-permute-start(bf16[128,1024]{1,0:T(8,128)(2,1)S(1)} %shard_map.77.refs_4_), channel_id=1, source_target_pairs={{0,2},{1,3},{2,0},{3,1},{4,6},{5,7},{6,4},{7,5},{8,10},{9,11},{10,... | collective-permute-start | bytes 786440 | tf_op jit(solution)/shard_map/ppermute | solution.py:56
  15.3 8.2 %collective-permute-done.5.refs_7_ = bf16[128,1024]{1,0:T(8,128)(2,1)S(1)} collective-permute-done((bf16[128,1024]{1,0:T(8,128)(2,1)S(1)}, bf16[128,1024]{1,0:T(8,128)(2,1)S(1)}, u32[]{:S(2)}, u32[]{:S(2)}) %collective-permute-start.5) | collective-permute-done | bytes 262176 | tf_op jit(solution)/shard_map/ppermute | solution.py:56
  23.5 0.7 collective-permute-done.3.refs_5_
  24.5 2.9 %collective-permute-start.7 = (bf16[256,1024]{1,0:T(8,128)(2,1)S(1)}, bf16[256,1024]{1,0:T(8,128)(2,1)S(1)}, u32[]{:S(2)}, u32[]{:S(2)}) collective-permute-start(bf16[256,1024]{1,0:T(8,128)(2,1)S(1)} %get-tuple-element.39.refs_2_.refs_4_), channel_id=1, source_target_pairs={{0,24},{1,97},{2,26},{3,99},{4,28},{5,101},{6,30},{7,103},{8,16},{... | collective-permute-start | bytes 1572872 | tf_op jit(solution)/shard_map/ppermute | solution.py:56
  27.5 1.9 %collective-permute-start.12 = (bf16[256,1024]{1,0:T(8,128)(2,1)S(1)}, bf16[256,1024]{1,0:T(8,128)(2,1)S(1)}, u32[]{:S(2)}, u32[]{:S(2)}) collective-permute-start(bf16[256,1024]{1,0:T(8,128)(2,1)S(1)} %get-tuple-element.39.refs_2_.refs_4_), channel_id=1, source_target_pairs={{0,8},{1,33},{2,10},{3,35},{4,12},{5,37},{6,14},{7,39},{8,0},{9,41... | collective-permute-start | bytes 1572872 | tf_op jit(solution)/shard_map/ppermute | solution.py:56
  29.8 5.1 %collective-permute-done.7.refs_3_.refs_2_.refs_10_ = bf16[256,1024]{1,0:T(8,128)(2,1)S(1)} collective-permute-done((bf16[256,1024]{1,0:T(8,128)(2,1)S(1)}, bf16[256,1024]{1,0:T(8,128)(2,1)S(1)}, u32[]{:S(2)}, u32[]{:S(2)}) %collective-permute-start.7) | collective-permute-done | bytes 524320 | tf_op jit(solution)/shard_map/ppermute | solution.py:56
  35.1 1.4 %collective-permute-done.9.refs_2_.refs_3_.refs_7_ = bf16[256,1024]{1,0:T(8,128)(2,1)S(1)} collective-permute-done((bf16[256,1024]{1,0:T(8,128)(2,1)S(1)}, bf16[256,1024]{1,0:T(8,128)(2,1)S(1)}, u32[]{:S(2)}, u32[]{:S(2)}) %collective-permute-start.9) | collective-permute-done | bytes 524320 | tf_op jit(solution)/shard_map/ppermute | solution.py:56
  36.6 1.2 %collective-permute-start.10 = (bf16[256,1024]{1,0:T(8,128)(2,1)S(1)}, bf16[256,1024]{1,0:T(8,128)(2,1)S(1)}, u32[]{:S(2)}, u32[]{:S(2)}) collective-permute-start(bf16[256,1024]{1,0:T(8,128)(2,1)S(1)} %collective-permute-done.9.refs_2_.refs_3_.refs_7_), channel_id=1, source_target_pairs={{0,24},{1,97},{2,26},{3,99},{4,28},{5,101},{6,30},{7,103},{8,16},{... | collective-permute-start | bytes 1572872 | tf_op jit(solution)/shard_map/ppermute | solution.py:56
  37.8 3.0 %shard_map.79 = (f32[8,1024]{1,0:T(8,128)S(1)}, f32[8,512]{1,0:T(8,128)S(1)}) custom-call(bf16[512,1024]{1,0:T(8,128)(2,1)S(1)} %get-tuple-element.38.refs_0_, bf16[512,1024]{1,0:T(8,128)(2,1)S(1)} %collective-permute-done.6.refs_1_, bf16[256,1024]{1,0:T(8,128)(2,1)S(1)} %get-tuple-element.39.refs_2_.refs_4_, ...), custom_call_target="tpu_custom_call" | custom-call | flops 1073741824 | bytes 3194880 | tf_op jit(solution)/shard_map/pallas_call | solution.py:78
  40.9 1.3 %collective-permute-done.12.refs_2_.refs_6_ = bf16[256,1024]{1,0:T(8,128)(2,1)S(1)} collective-permute-done((bf16[256,1024]{1,0:T(8,128)(2,1)S(1)}, bf16[256,1024]{1,0:T(8,128)(2,1)S(1)}, u32[]{:S(2)}, u32[]{:S(2)}) %collective-permute-start.12) | collective-permute-done | bytes 524320 | tf_op jit(solution)/shard_map/ppermute | solution.py:56
  42.2 3.1 %shard_map.80 = (f32[8,1024]{1,0:T(8,128)S(1)}, f32[8,512]{1,0:T(8,128)S(1)}) custom-call(bf16[512,1024]{1,0:T(8,128)(2,1)S(1)} %get-tuple-element.38.refs_0_, bf16[512,1024]{1,0:T(8,128)(2,1)S(1)} %collective-permute-done.6.refs_1_, bf16[256,1024]{1,0:T(8,128)(2,1)S(1)} %collective-permute-done.12.refs_2_.refs_6_, ...), custom_call_target="tpu_custom_call" | custom-call | flops 1073741824 | bytes 3227648 | tf_op jit(solution)/shard_map/pallas_call | solution.py:78
  45.3 3.1 %shard_map.81 = (f32[8,1024]{1,0:T(8,128)S(1)}, f32[8,512]{1,0:T(8,128)S(1)}) custom-call(bf16[512,1024]{1,0:T(8,128)(2,1)S(1)} %get-tuple-element.38.refs_0_, bf16[512,1024]{1,0:T(8,128)(2,1)S(1)} %collective-permute-done.6.refs_1_, bf16[256,1024]{1,0:T(8,128)(2,1)S(1)} %collective-permute-done.9.refs_2_.refs_3_.refs_7_, ...), custom_call_target="tpu_custom_call" | custom-call | flops 1073741824 | bytes 3227648 | tf_op jit(solution)/shard_map/pallas_call | solution.py:78
  48.4 3.1 %shard_map.82 = (f32[8,1024]{1,0:T(8,128)S(1)}, f32[8,512]{1,0:T(8,128)S(1)}) custom-call(bf16[512,1024]{1,0:T(8,128)(2,1)S(1)} %get-tuple-element.38.refs_0_, bf16[512,1024]{1,0:T(8,128)(2,1)S(1)} %collective-permute-done.6.refs_1_, bf16[256,1024]{1,0:T(8,128)(2,1)S(1)} %collective-permute-done.8.refs_2_.refs_8_, ...), custom_call_target="tpu_custom_call" | custom-call | flops 1073741824 | bytes 3227648 | tf_op jit(solution)/shard_map/pallas_call | solution.py:78
  51.6 1.2 %collective-permute-done.13.got_ref = f32[8,2048]{1,0:T(8,128)S(1)} collective-permute-done((f32[8,2048]{1,0:T(8,128)S(1)}, f32[8,2048]{1,0:T(8,128)S(1)}, u32[]{:S(2)}, u32[]{:S(2)}) %collective-permute-start.13) | collective-permute-done | bytes 65568 | tf_op jit(solution)/shard_map/ppermute | solution.py:56
  52.9 2.8 %collective-permute-start.16 = (f32[8,2048]{1,0:T(8,128)S(1)}, f32[8,2048]{1,0:T(8,128)S(1)}, u32[]{:S(2)}, u32[]{:S(2)}) collective-permute-start(f32[8,2048]{1,0:T(8,128)S(1)} %shard_map.84.own_ref), channel_id=1, source_target_pairs={{0,96},{1,7},{2,98},{3,5},{4,100},{5,3},{6,102},{7,1},{8,104},{9,1... | collective-permute-start | bytes 196616 | tf_op jit(solution)/shard_map/ppermute | solution.py:56
  55.7 0.8 collective-permute-start.15
  56.5 0.5 collective-permute-start.14
  57.1 1.4 %collective-permute-done.16.g3 = f32[8,2048]{1,0:T(8,128)S(1)} collective-permute-done((f32[8,2048]{1,0:T(8,128)S(1)}, f32[8,2048]{1,0:T(8,128)S(1)}, u32[]{:S(2)}, u32[]{:S(2)}) %collective-permute-start.16) | collective-permute-done | bytes 65568 | tf_op jit(solution)/shard_map/ppermute | solution.py:56
  58.4 3.1 %collective-permute-done.15.g2 = f32[8,2048]{1,0:T(8,128)S(1)} collective-permute-done((f32[8,2048]{1,0:T(8,128)S(1)}, f32[8,2048]{1,0:T(8,128)S(1)}, u32[]{:S(2)}, u32[]{:S(2)}) %collective-permute-start.15) | collective-permute-done | bytes 65568 | tf_op jit(solution)/shard_map/ppermute | solution.py:56
  61.7 1.2 %collective-permute-done.17.got_ref = f32[8,2048]{1,0:T(8,128)S(1)} collective-permute-done((f32[8,2048]{1,0:T(8,128)S(1)}, f32[8,2048]{1,0:T(8,128)S(1)}, u32[]{:S(2)}, u32[]{:S(2)}) %collective-permute-start.17) | collective-permute-done | bytes 65568 | tf_op jit(solution)/shard_map/ppermute | solution.py:56
  62.9 0.8 collective-permute-start.20
  63.7 1.5 %collective-permute-start.19 = (f32[8,2048]{1,0:T(8,128)S(1)}, f32[8,2048]{1,0:T(8,128)S(1)}, u32[]{:S(2)}, u32[]{:S(2)}) collective-permute-start(f32[8,2048]{1,0:T(8,128)S(1)} %get-tuple-element.50.own_ref), channel_id=1, source_target_pairs={{0,16},{1,17},{2,18},{3,19},{4,20},{5,21},{6,22},{7,23},{8,24},{9,... | collective-permute-start | bytes 196616 | tf_op jit(solution)/shard_map/ppermute | solution.py:56
  65.2 1.9 %collective-permute-start.18 = (f32[8,2048]{1,0:T(8,128)S(1)}, f32[8,2048]{1,0:T(8,128)S(1)}, u32[]{:S(2)}, u32[]{:S(2)}) collective-permute-start(f32[8,2048]{1,0:T(8,128)S(1)} %get-tuple-element.50.own_ref), channel_id=1, source_target_pairs={{0,8},{1,9},{2,10},{3,11},{4,12},{5,13},{6,14},{7,15},{8,0},{9,1},... | collective-permute-start | bytes 196616 | tf_op jit(solution)/shard_map/ppermute | solution.py:56
  67.1 2.3 %collective-permute-done.20.g3 = f32[8,2048]{1,0:T(8,128)S(1)} collective-permute-done((f32[8,2048]{1,0:T(8,128)S(1)}, f32[8,2048]{1,0:T(8,128)S(1)}, u32[]{:S(2)}, u32[]{:S(2)}) %collective-permute-start.20) | collective-permute-done | bytes 65568 | tf_op jit(solution)/shard_map/ppermute | solution.py:56
  69.8 0.6 collective-permute-done.18.g1
  70.7 3.2 %shard_map.88 = (bf16[1024,512]{1,0:T(8,128)(2,1)S(1)}, bf16[528,512]{1,0:T(8,128)(2,1)S(1)}) custom-call(bf16[512,1024]{1,0:T(8,128)(2,1)S(1)} %get-tuple-element.38.refs_0_, bf16[512,1024]{1,0:T(8,128)(2,1)S(1)} %collective-permute-done.6.refs_1_, bf16[256,1024]{1,0:T(8,128)(2,1)S(1)} %collective-permute-done.8.refs_2_.refs_8_, ...), custom_call_target="tpu_custom_call" | custom-call | flops 1610612736 | bytes 4833280 | tf_op jit(solution)/shard_map/pallas_call | solution.py:78
  73.9 1.2 %collective-permute-start.21 = (bf16[528,512]{1,0:T(8,128)(2,1)S(1)}, bf16[528,512]{1,0:T(8,128)(2,1)S(1)}, u32[]{:S(2)}, u32[]{:S(2)}) collective-permute-start(bf16[528,512]{1,0:T(8,128)(2,1)S(1)} %get-tuple-element.51), channel_id=1, source_target_pairs={{0,16},{1,65},{2,18},{3,67},{4,20},{5,69},{6,22},{7,71},{8,24},{9,... | collective-permute-start | bytes 1622024 | tf_op jit(solution)/shard_map/ppermute | solution.py:56
  75.2 3.2 %shard_map.90 = (bf16[1024,512]{1,0:T(8,128)(2,1)S(1)}, bf16[528,512]{1,0:T(8,128)(2,1)S(1)}) custom-call(bf16[512,1024]{1,0:T(8,128)(2,1)S(1)} %get-tuple-element.38.refs_0_, bf16[512,1024]{1,0:T(8,128)(2,1)S(1)} %collective-permute-done.6.refs_1_, bf16[256,1024]{1,0:T(8,128)(2,1)S(1)} %collective-permute-done.12.refs_2_.refs_6_, ...), custom_call_target="tpu_custom_call" | custom-call | flops 1610612736 | bytes 4833280 | tf_op jit(solution)/shard_map/pallas_call | solution.py:78
  78.4 1.8 %collective-permute-start.22 = (bf16[528,512]{1,0:T(8,128)(2,1)S(1)}, bf16[528,512]{1,0:T(8,128)(2,1)S(1)}, u32[]{:S(2)}, u32[]{:S(2)}) collective-permute-start(bf16[528,512]{1,0:T(8,128)(2,1)S(1)} %get-tuple-element.57), channel_id=1, source_target_pairs={{0,8},{1,33},{2,10},{3,35},{4,12},{5,37},{6,14},{7,39},{8,0},{9,41... | collective-permute-start | bytes 1622024 | tf_op jit(solution)/shard_map/ppermute | solution.py:56
  80.1 3.2 %shard_map.91 = (bf16[1024,512]{1,0:T(8,128)(2,1)S(1)}, bf16[528,512]{1,0:T(8,128)(2,1)S(1)}) custom-call(bf16[512,1024]{1,0:T(8,128)(2,1)S(1)} %get-tuple-element.38.refs_0_, bf16[512,1024]{1,0:T(8,128)(2,1)S(1)} %collective-permute-done.6.refs_1_, bf16[256,1024]{1,0:T(8,128)(2,1)S(1)} %collective-permute-done.7.refs_3_.refs_2_.refs_10_, ...), custom_call_target="tpu_custom_call" | custom-call | flops 1610612736 | bytes 4833280 | tf_op jit(solution)/shard_map/pallas_call | solution.py:78
  83.3 1.3 %collective-permute-start.23 = (bf16[528,512]{1,0:T(8,128)(2,1)S(1)}, bf16[528,512]{1,0:T(8,128)(2,1)S(1)}, u32[]{:S(2)}, u32[]{:S(2)}) collective-permute-start(bf16[528,512]{1,0:T(8,128)(2,1)S(1)} %get-tuple-element.59), channel_id=1, source_target_pairs={{0,24},{1,97},{2,26},{3,99},{4,28},{5,101},{6,30},{7,103},{8,16},{... | collective-permute-start | bytes 1622024 | tf_op jit(solution)/shard_map/ppermute | solution.py:56
  84.9 3.2 %shard_map.89 = (bf16[1024,512]{1,0:T(8,128)(2,1)S(1)}, f32[512,512]{1,0:T(8,128)S(1)}) custom-call(bf16[512,1024]{1,0:T(8,128)(2,1)S(1)} %get-tuple-element.38.refs_0_, bf16[512,1024]{1,0:T(8,128)(2,1)S(1)} %collective-permute-done.6.refs_1_, bf16[256,1024]{1,0:T(8,128)(2,1)S(1)} %get-tuple-element.39.refs_2_.refs_4_, ...), custom_call_target="tpu_custom_call" | custom-call | flops 1610612736 | bytes 5881856 | tf_op jit(solution)/shard_map/pallas_call | solution.py:78
  88.1 1.9 %collective-permute-done.22.refs_14_.refs_15_ = bf16[528,512]{1,0:T(8,128)(2,1)S(1)} collective-permute-done((bf16[528,512]{1,0:T(8,128)(2,1)S(1)}, bf16[528,512]{1,0:T(8,128)(2,1)S(1)}, u32[]{:S(2)}, u32[]{:S(2)}) %collective-permute-start.22) | collective-permute-done | bytes 540704 | tf_op jit(solution)/shard_map/ppermute | solution.py:56
  90.0 1.6 %shard_map.92 = (bf16[528,512]{1,0:T(8,128)(2,1)S(1)}, f32[512,512]{1,0:T(8,128)S(1)}) custom-call(bf16[1024,512]{1,0:T(8,128)(2,1)S(1)} %get-tuple-element.52.refs_0_, bf16[1024,512]{1,0:T(8,128)(2,1)S(1)} %get-tuple-element.53.refs_1_, bf16[1024,512]{1,0:T(8,128)(2,1)S(1)} %get-tuple-element.54.refs_2_, bf16[1024,512]{1,0:T(8,128)(2,1)S(1)} %get-tuple-element.55.refs_3_, ...), custom_call_target="tpu_custom_call" | custom-call | flops 1073741824 | bytes 11632640 | tf_op jit(solution)/shard_map/pallas_call | solution.py:78
  91.6 2.4 %collective-permute-done.23.refs_16_ = bf16[528,512]{1,0:T(8,128)(2,1)S(1)} collective-permute-done((bf16[528,512]{1,0:T(8,128)(2,1)S(1)}, bf16[528,512]{1,0:T(8,128)(2,1)S(1)}, u32[]{:S(2)}, u32[]{:S(2)}) %collective-permute-start.23) | collective-permute-done | bytes 540704 | tf_op jit(solution)/shard_map/ppermute | solution.py:56
  94.0 1.5 %shard_map.93 = (f32[512,512]{1,0:T(8,128)S(1)}, f32[136,512]{1,0:T(8,128)S(1)}, bf16[144,512]{1,0:T(8,128)(2,1)S(1)}, bf16[144,512]{1,0:T(8,128)(2,1)S(1)}, bf16[144,512]{1,0:T(8,128)(2,1)S(1)}) custom-call(bf16[1024,512]{1,0:T(8,128)(2,1)S(1)} %get-tuple-element.52.refs_0_, bf16[1024,512]{1,0:T(8,128)(2,1)S(1)} %get-tuple-element.53.refs_1_, ...), custom_call_target="tpu_custom_call" | custom-call | flops 1073741824 | bytes 12861440 | tf_op jit(solution)/shard_map/pallas_call | solution.py:78
  95.8 2.7 %collective-permute-start.29 = (bf16[144,512]{1,0:T(8,128)(2,1)S(1)}, bf16[144,512]{1,0:T(8,128)(2,1)S(1)}, u32[]{:S(2)}, u32[]{:S(2)}) collective-permute-start(bf16[144,512]{1,0:T(8,128)(2,1)S(1)} %get-tuple-element.68), channel_id=1, source_target_pairs={{0,64},{1,17},{2,66},{3,19},{4,68},{5,21},{6,70},{7,23},{8,72},{9,... | collective-permute-start | bytes 442376 | tf_op jit(solution)/shard_map/ppermute | solution.py:56
  98.5 1.8 %collective-permute-start.30 = (bf16[144,512]{1,0:T(8,128)(2,1)S(1)}, bf16[144,512]{1,0:T(8,128)(2,1)S(1)}, u32[]{:S(2)}, u32[]{:S(2)}) collective-permute-start(bf16[144,512]{1,0:T(8,128)(2,1)S(1)} %get-tuple-element.69), channel_id=1, source_target_pairs={{0,96},{1,25},{2,98},{3,27},{4,100},{5,29},{6,102},{7,31},{8,104},... | collective-permute-start | bytes 442376 | tf_op jit(solution)/shard_map/ppermute | solution.py:56
  100.5 1.2 %collective-permute-start.25 = (bf16[144,512]{1,0:T(8,128)(2,1)S(1)}, bf16[144,512]{1,0:T(8,128)(2,1)S(1)}, u32[]{:S(2)}, u32[]{:S(2)}) collective-permute-start(bf16[144,512]{1,0:T(8,128)(2,1)S(1)} %get-tuple-element.63), channel_id=1, source_target_pairs={{0,2},{1,3},{2,0},{3,1},{4,6},{5,7},{6,4},{7,5},{8,10},{9,11},{10,... | collective-permute-start | bytes 442376 | tf_op jit(solution)/shard_map/ppermute | solution.py:56
  101.6 3.2 %collective-permute-start.26 = (bf16[144,512]{1,0:T(8,128)(2,1)S(1)}, bf16[144,512]{1,0:T(8,128)(2,1)S(1)}, u32[]{:S(2)}, u32[]{:S(2)}) collective-permute-start(bf16[144,512]{1,0:T(8,128)(2,1)S(1)} %get-tuple-element.64), channel_id=1, source_target_pairs={{0,4},{1,5},{2,6},{3,7},{4,0},{5,1},{6,2},{7,3},{8,12},{9,13},{10,... | collective-permute-start | bytes 442376 | tf_op jit(solution)/shard_map/ppermute | solution.py:56
  105.7 3.9 %collective-permute-done.26.refs_3_ = bf16[144,512]{1,0:T(8,128)(2,1)S(1)} collective-permute-done((bf16[144,512]{1,0:T(8,128)(2,1)S(1)}, bf16[144,512]{1,0:T(8,128)(2,1)S(1)}, u32[]{:S(2)}, u32[]{:S(2)}) %collective-permute-start.26) | collective-permute-done | bytes 147488 | tf_op jit(solution)/shard_map/ppermute | solution.py:56
  109.5 1.7 %collective-permute-done.27.refs_4_ = bf16[144,512]{1,0:T(8,128)(2,1)S(1)} collective-permute-done((bf16[144,512]{1,0:T(8,128)(2,1)S(1)}, bf16[144,512]{1,0:T(8,128)(2,1)S(1)}, u32[]{:S(2)}, u32[]{:S(2)}) %collective-permute-start.27) | collective-permute-done | bytes 147488 | tf_op jit(solution)/shard_map/ppermute | solution.py:56
  111.2 1.1 %shard_map.95 = (f32[128,512]{1,0:T(8,128)}, f32[128,512]{1,0:T(8,128)}, f32[1,1]{1,0:T(1,128)}) custom-call(bf16[128,512]{1,0:T(8,128)(2,1)S(1)} %copy-done.2, f32[136,512]{1,0:T(8,128)S(1)} %get-tuple-element.62.refs_1_, bf16[144,512]{1,0:T(8,128)(2,1)S(1)} %collective-permute-done.25.refs_2_, bf16[144,512]{1,0:T(8,128)(2,1)S(1)} %collective-permute-done.26.refs_3_, ...), custom_call_target="tpu_custom_call" | custom-call | bytes 2228228 | tf_op jit(solution)/shard_map/pallas_call | solution.py:78
  (44 shorter events, 4.4 us)
Async XLA Ops:
  0.6 7.0 %copy-start = (bf16[1280,512]{1,0:T(8,128)(2,1)S(1)}, bf16[1280,512]{1,0:T(8,128)(2,1)}, u32[]{:S(2)}) copy-start(bf16[1280,512]{1,0:T(8,128)(2,1)} %sketch_ref.1) | copy-start | bytes 3932164
  0.6 7.0 %copy-start.2 = (bf16[128,512]{1,0:T(8,128)(2,1)S(1)}, bf16[128,512]{1,0:T(8,128)(2,1)}, u32[]{:S(2)}) copy-start(bf16[128,512]{1,0:T(8,128)(2,1)} %refs_0_.1) | copy-start | bytes 393220
  0.7 7.0 %copy-start.4 = (bf16[128,1280]{1,0:T(8,128)(2,1)S(1)}, bf16[128,1280]{1,0:T(8,128)(2,1)}, u32[]{:S(2)}) copy-start(bf16[128,1280]{1,0:T(8,128)(2,1)} %teacher_ref.1) | copy-start | bytes 983044
  3.4 20.8 %copy-start.1 = (bf16[128,1024]{1,0:T(8,128)(2,1)S(1)}, bf16[128,1024]{1,0:T(8,128)(2,1)}, u32[]{:S(2)}) copy-start(bf16[128,1024]{1,0:T(8,128)(2,1)} %shard_map.76.refs_0_) | copy-start | bytes 786436
  3.4 9.9 %collective-permute-start.2 = (bf16[128,1024]{1,0:T(8,128)(2,1)}, bf16[128,1024]{1,0:T(8,128)(2,1)S(1)}, u32[]{:S(2)}, u32[]{:S(2)}) collective-permute-start(bf16[128,1024]{1,0:T(8,128)(2,1)} %shard_map.76.refs_0_), channel_id=1, source_target_pairs={{0,96},{1,25},{2,98},{3,27},{4,100},{5,29},{6,102},{7,31},{8,104},... | collective-permute-start | bytes 786440 | tf_op jit(solution)/shard_map/ppermute | solution.py:56
  6.4 8.9 %collective-permute-start.1 = (bf16[128,1024]{1,0:T(8,128)(2,1)}, bf16[128,1024]{1,0:T(8,128)(2,1)S(1)}, u32[]{:S(2)}, u32[]{:S(2)}) collective-permute-start(bf16[128,1024]{1,0:T(8,128)(2,1)} %shard_map.76.refs_0_), channel_id=1, source_target_pairs={{0,64},{1,17},{2,66},{3,19},{4,68},{5,21},{6,70},{7,23},{8,72},{9,... | collective-permute-start | bytes 786440 | tf_op jit(solution)/shard_map/ppermute | solution.py:56
  7.2 8.1 %collective-permute-start = (bf16[128,1024]{1,0:T(8,128)(2,1)}, bf16[128,1024]{1,0:T(8,128)(2,1)S(1)}, u32[]{:S(2)}, u32[]{:S(2)}) collective-permute-start(bf16[128,1024]{1,0:T(8,128)(2,1)} %shard_map.76.refs_0_), channel_id=1, source_target_pairs={{0,32},{1,9},{2,34},{3,11},{4,36},{5,13},{6,38},{7,15},{8,40},{9,1... | collective-permute-start | bytes 786440 | tf_op jit(solution)/shard_map/ppermute | solution.py:56
  8.1 15.4 %collective-permute-start.5 = (bf16[128,1024]{1,0:T(8,128)(2,1)S(1)}, bf16[128,1024]{1,0:T(8,128)(2,1)S(1)}, u32[]{:S(2)}, u32[]{:S(2)}) collective-permute-start(bf16[128,1024]{1,0:T(8,128)(2,1)S(1)} %shard_map.77.refs_4_), channel_id=1, source_target_pairs={{0,6},{1,7},{2,4},{3,5},{4,2},{5,3},{6,0},{7,1},{8,14},{9,15},{10,... | collective-permute-start | bytes 786440 | tf_op jit(solution)/shard_map/ppermute | solution.py:56
  12.3 11.2 %collective-permute-start.4 = (bf16[128,1024]{1,0:T(8,128)(2,1)S(1)}, bf16[128,1024]{1,0:T(8,128)(2,1)S(1)}, u32[]{:S(2)}, u32[]{:S(2)}) collective-permute-start(bf16[128,1024]{1,0:T(8,128)(2,1)S(1)} %shard_map.77.refs_4_), channel_id=1, source_target_pairs={{0,4},{1,5},{2,6},{3,7},{4,0},{5,1},{6,2},{7,3},{8,12},{9,13},{10,... | collective-permute-start | bytes 786440 | tf_op jit(solution)/shard_map/ppermute | solution.py:56
  13.4 10.8 %collective-permute-start.3 = (bf16[128,1024]{1,0:T(8,128)(2,1)S(1)}, bf16[128,1024]{1,0:T(8,128)(2,1)S(1)}, u32[]{:S(2)}, u32[]{:S(2)}) collective-permute-start(bf16[128,1024]{1,0:T(8,128)(2,1)S(1)} %shard_map.77.refs_4_), channel_id=1, source_target_pairs={{0,2},{1,3},{2,0},{3,1},{4,6},{5,7},{6,4},{7,5},{8,10},{9,11},{10,... | collective-permute-start | bytes 786440 | tf_op jit(solution)/shard_map/ppermute | solution.py:56
  24.4 13.4 %collective-permute-start.6 = (bf16[512,1024]{1,0:T(8,128)(2,1)S(1)}, bf16[512,1024]{1,0:T(8,128)(2,1)S(1)}, u32[]{:S(2)}, u32[]{:S(2)}) collective-permute-start(bf16[512,1024]{1,0:T(8,128)(2,1)S(1)} %get-tuple-element.38.refs_0_), channel_id=1, source_target_pairs={{0,1},{1,0},{2,3},{3,2},{4,5},{5,4},{6,7},{7,6},{8,9},{9,8},{10,11... | collective-permute-start | bytes 3145736 | tf_op jit(solution)/shard_map/ppermute | solution.py:56
  24.5 10.5 %collective-permute-start.7 = (bf16[256,1024]{1,0:T(8,128)(2,1)S(1)}, bf16[256,1024]{1,0:T(8,128)(2,1)S(1)}, u32[]{:S(2)}, u32[]{:S(2)}) collective-permute-start(bf16[256,1024]{1,0:T(8,128)(2,1)S(1)} %get-tuple-element.39.refs_2_.refs_4_), channel_id=1, source_target_pairs={{0,24},{1,97},{2,26},{3,99},{4,28},{5,101},{6,30},{7,103},{8,16},{... | collective-permute-start | bytes 1572872 | tf_op jit(solution)/shard_map/ppermute | solution.py:56
  27.4 9.2 %collective-permute-start.9 = (bf16[256,1024]{1,0:T(8,128)(2,1)S(1)}, bf16[256,1024]{1,0:T(8,128)(2,1)S(1)}, u32[]{:S(2)}, u32[]{:S(2)}) collective-permute-start(bf16[256,1024]{1,0:T(8,128)(2,1)S(1)} %get-tuple-element.40.refs_3_.refs_5_), channel_id=1, source_target_pairs={{0,8},{1,33},{2,10},{3,35},{4,12},{5,37},{6,14},{7,39},{8,0},{9,41... | collective-permute-start | bytes 1572872 | tf_op jit(solution)/shard_map/ppermute | solution.py:56
  27.5 14.7 %collective-permute-start.12 = (bf16[256,1024]{1,0:T(8,128)(2,1)S(1)}, bf16[256,1024]{1,0:T(8,128)(2,1)S(1)}, u32[]{:S(2)}, u32[]{:S(2)}) collective-permute-start(bf16[256,1024]{1,0:T(8,128)(2,1)S(1)} %get-tuple-element.39.refs_2_.refs_4_), channel_id=1, source_target_pairs={{0,8},{1,33},{2,10},{3,35},{4,12},{5,37},{6,14},{7,39},{8,0},{9,41... | collective-permute-start | bytes 1572872 | tf_op jit(solution)/shard_map/ppermute | solution.py:56
  29.4 15.9 %collective-permute-start.11 = (bf16[256,1024]{1,0:T(8,128)(2,1)S(1)}, bf16[256,1024]{1,0:T(8,128)(2,1)S(1)}, u32[]{:S(2)}, u32[]{:S(2)}) collective-permute-start(bf16[256,1024]{1,0:T(8,128)(2,1)S(1)} %get-tuple-element.40.refs_3_.refs_5_), channel_id=1, source_target_pairs={{0,24},{1,97},{2,26},{3,99},{4,28},{5,101},{6,30},{7,103},{8,16},{... | collective-permute-start | bytes 1572872 | tf_op jit(solution)/shard_map/ppermute | solution.py:56
  34.9 13.5 %collective-permute-start.8 = (bf16[256,1024]{1,0:T(8,128)(2,1)S(1)}, bf16[256,1024]{1,0:T(8,128)(2,1)S(1)}, u32[]{:S(2)}, u32[]{:S(2)}) collective-permute-start(bf16[256,1024]{1,0:T(8,128)(2,1)S(1)} %collective-permute-done.7.refs_3_.refs_2_.refs_10_), channel_id=1, source_target_pairs={{0,8},{1,33},{2,10},{3,35},{4,12},{5,37},{6,14},{7,39},{8,0},{9,41... | collective-permute-start | bytes 1572872 | tf_op jit(solution)/shard_map/ppermute | solution.py:56
  36.6 11.8 %collective-permute-start.10 = (bf16[256,1024]{1,0:T(8,128)(2,1)S(1)}, bf16[256,1024]{1,0:T(8,128)(2,1)S(1)}, u32[]{:S(2)}, u32[]{:S(2)}) collective-permute-start(bf16[256,1024]{1,0:T(8,128)(2,1)S(1)} %collective-permute-done.9.refs_2_.refs_3_.refs_7_), channel_id=1, source_target_pairs={{0,24},{1,97},{2,26},{3,99},{4,28},{5,101},{6,30},{7,103},{8,16},{... | collective-permute-start | bytes 1572872 | tf_op jit(solution)/shard_map/ppermute | solution.py:56
  51.5 1.3 %collective-permute-start.13 = (f32[8,2048]{1,0:T(8,128)S(1)}, f32[8,2048]{1,0:T(8,128)S(1)}, u32[]{:S(2)}, u32[]{:S(2)}) collective-permute-start(f32[8,2048]{1,0:T(8,128)S(1)} %shard_map.83.own_ref), channel_id=1, source_target_pairs={{0,1},{1,0},{2,3},{3,2},{4,5},{5,4},{6,7},{7,6},{8,9},{9,8},{10,11... | collective-permute-start | bytes 196616 | tf_op jit(solution)/shard_map/ppermute | solution.py:56
  52.9 5.6 %collective-permute-start.16 = (f32[8,2048]{1,0:T(8,128)S(1)}, f32[8,2048]{1,0:T(8,128)S(1)}, u32[]{:S(2)}, u32[]{:S(2)}) collective-permute-start(f32[8,2048]{1,0:T(8,128)S(1)} %shard_map.84.own_ref), channel_id=1, source_target_pairs={{0,96},{1,7},{2,98},{3,5},{4,100},{5,3},{6,102},{7,1},{8,104},{9,1... | collective-permute-start | bytes 196616 | tf_op jit(solution)/shard_map/ppermute | solution.py:56
  55.7 5.8 %collective-permute-start.15 = (f32[8,2048]{1,0:T(8,128)S(1)}, f32[8,2048]{1,0:T(8,128)S(1)}, u32[]{:S(2)}, u32[]{:S(2)}) collective-permute-start(f32[8,2048]{1,0:T(8,128)S(1)} %shard_map.84.own_ref), channel_id=1, source_target_pairs={{0,64},{1,5},{2,66},{3,7},{4,68},{5,1},{6,70},{7,3},{8,72},{9,13},... | collective-permute-start | bytes 196616 | tf_op jit(solution)/shard_map/ppermute | solution.py:56
  56.5 5.0 %collective-permute-start.14 = (f32[8,2048]{1,0:T(8,128)S(1)}, f32[8,2048]{1,0:T(8,128)S(1)}, u32[]{:S(2)}, u32[]{:S(2)}) collective-permute-start(f32[8,2048]{1,0:T(8,128)S(1)} %shard_map.84.own_ref), channel_id=1, source_target_pairs={{0,32},{1,3},{2,34},{3,1},{4,36},{5,7},{6,38},{7,5},{8,40},{9,11},... | collective-permute-start | bytes 196616 | tf_op jit(solution)/shard_map/ppermute | solution.py:56
  61.6 1.3 %collective-permute-start.17 = (f32[8,2048]{1,0:T(8,128)S(1)}, f32[8,2048]{1,0:T(8,128)S(1)}, u32[]{:S(2)}, u32[]{:S(2)}) collective-permute-start(f32[8,2048]{1,0:T(8,128)S(1)} %shard_map.85.own_ref), channel_id=1, source_target_pairs={{0,1},{1,0},{2,3},{3,2},{4,5},{5,4},{6,7},{7,6},{8,9},{9,8},{10,11... | collective-permute-start | bytes 196616 | tf_op jit(solution)/shard_map/ppermute | solution.py:56
  62.9 6.4 %collective-permute-start.20 = (f32[8,2048]{1,0:T(8,128)S(1)}, f32[8,2048]{1,0:T(8,128)S(1)}, u32[]{:S(2)}, u32[]{:S(2)}) collective-permute-start(f32[8,2048]{1,0:T(8,128)S(1)} %get-tuple-element.50.own_ref), channel_id=1, source_target_pairs={{0,24},{1,25},{2,26},{3,27},{4,28},{5,29},{6,30},{7,31},{8,16},{9,... | collective-permute-start | bytes 196616 | tf_op jit(solution)/shard_map/ppermute | solution.py:56
  63.7 6.1 %collective-permute-start.19 = (f32[8,2048]{1,0:T(8,128)S(1)}, f32[8,2048]{1,0:T(8,128)S(1)}, u32[]{:S(2)}, u32[]{:S(2)}) collective-permute-start(f32[8,2048]{1,0:T(8,128)S(1)} %get-tuple-element.50.own_ref), channel_id=1, source_target_pairs={{0,16},{1,17},{2,18},{3,19},{4,20},{5,21},{6,22},{7,23},{8,24},{9,... | collective-permute-start | bytes 196616 | tf_op jit(solution)/shard_map/ppermute | solution.py:56
  65.2 5.1 %collective-permute-start.18 = (f32[8,2048]{1,0:T(8,128)S(1)}, f32[8,2048]{1,0:T(8,128)S(1)}, u32[]{:S(2)}, u32[]{:S(2)}) collective-permute-start(f32[8,2048]{1,0:T(8,128)S(1)} %get-tuple-element.50.own_ref), channel_id=1, source_target_pairs={{0,8},{1,9},{2,10},{3,11},{4,12},{5,13},{6,14},{7,15},{8,0},{9,1},... | collective-permute-start | bytes 196616 | tf_op jit(solution)/shard_map/ppermute | solution.py:56
  73.9 10.9 %collective-permute-start.21 = (bf16[528,512]{1,0:T(8,128)(2,1)S(1)}, bf16[528,512]{1,0:T(8,128)(2,1)S(1)}, u32[]{:S(2)}, u32[]{:S(2)}) collective-permute-start(bf16[528,512]{1,0:T(8,128)(2,1)S(1)} %get-tuple-element.51), channel_id=1, source_target_pairs={{0,16},{1,65},{2,18},{3,67},{4,20},{5,69},{6,22},{7,71},{8,24},{9,... | collective-permute-start | bytes 1622024 | tf_op jit(solution)/shard_map/ppermute | solution.py:56
  78.4 11.6 %collective-permute-start.22 = (bf16[528,512]{1,0:T(8,128)(2,1)S(1)}, bf16[528,512]{1,0:T(8,128)(2,1)S(1)}, u32[]{:S(2)}, u32[]{:S(2)}) collective-permute-start(bf16[528,512]{1,0:T(8,128)(2,1)S(1)} %get-tuple-element.57), channel_id=1, source_target_pairs={{0,8},{1,33},{2,10},{3,35},{4,12},{5,37},{6,14},{7,39},{8,0},{9,41... | collective-permute-start | bytes 1622024 | tf_op jit(solution)/shard_map/ppermute | solution.py:56
  83.3 10.6 %collective-permute-start.23 = (bf16[528,512]{1,0:T(8,128)(2,1)S(1)}, bf16[528,512]{1,0:T(8,128)(2,1)S(1)}, u32[]{:S(2)}, u32[]{:S(2)}) collective-permute-start(bf16[528,512]{1,0:T(8,128)(2,1)S(1)} %get-tuple-element.59), channel_id=1, source_target_pairs={{0,24},{1,97},{2,26},{3,99},{4,28},{5,101},{6,30},{7,103},{8,16},{... | collective-permute-start | bytes 1622024 | tf_op jit(solution)/shard_map/ppermute | solution.py:56
  91.6 8.7 %collective-permute-start.24 = (bf16[528,512]{1,0:T(8,128)(2,1)S(1)}, bf16[528,512]{1,0:T(8,128)(2,1)S(1)}, u32[]{:S(2)}, u32[]{:S(2)}) collective-permute-start(bf16[528,512]{1,0:T(8,128)(2,1)S(1)} %get-tuple-element.61), channel_id=1, source_target_pairs={{0,1},{1,0},{2,3},{3,2},{4,5},{5,4},{6,7},{7,6},{8,9},{9,8},{10,11... | collective-permute-start | bytes 1622024 | tf_op jit(solution)/shard_map/ppermute | solution.py:56
  95.5 15.7 %copy-start.3 = (bf16[128,512]{1,0:T(8,128)(2,1)S(1)}, bf16[128,512]{1,0:T(8,128)(2,1)}, u32[]{:S(2)}) copy-start(bf16[128,512]{1,0:T(8,128)(2,1)} %refs_5_.1) | copy-start | bytes 393220
  95.5 9.3 %collective-permute-start.28 = (bf16[144,512]{1,0:T(8,128)(2,1)S(1)}, bf16[144,512]{1,0:T(8,128)(2,1)S(1)}, u32[]{:S(2)}, u32[]{:S(2)}) collective-permute-start(bf16[144,512]{1,0:T(8,128)(2,1)S(1)} %get-tuple-element.67), channel_id=1, source_target_pairs={{0,32},{1,9},{2,34},{3,11},{4,36},{5,13},{6,38},{7,15},{8,40},{9,1... | collective-permute-start | bytes 442376 | tf_op jit(solution)/shard_map/ppermute | solution.py:56
  95.8 9.4 %collective-permute-start.29 = (bf16[144,512]{1,0:T(8,128)(2,1)S(1)}, bf16[144,512]{1,0:T(8,128)(2,1)S(1)}, u32[]{:S(2)}, u32[]{:S(2)}) collective-permute-start(bf16[144,512]{1,0:T(8,128)(2,1)S(1)} %get-tuple-element.68), channel_id=1, source_target_pairs={{0,64},{1,17},{2,66},{3,19},{4,68},{5,21},{6,70},{7,23},{8,72},{9,... | collective-permute-start | bytes 442376 | tf_op jit(solution)/shard_map/ppermute | solution.py:56
  98.5 6.7 %collective-permute-start.30 = (bf16[144,512]{1,0:T(8,128)(2,1)S(1)}, bf16[144,512]{1,0:T(8,128)(2,1)S(1)}, u32[]{:S(2)}, u32[]{:S(2)}) collective-permute-start(bf16[144,512]{1,0:T(8,128)(2,1)S(1)} %get-tuple-element.69), channel_id=1, source_target_pairs={{0,96},{1,25},{2,98},{3,27},{4,100},{5,29},{6,102},{7,31},{8,104},... | collective-permute-start | bytes 442376 | tf_op jit(solution)/shard_map/ppermute | solution.py:56
  100.5 5.2 %collective-permute-start.25 = (bf16[144,512]{1,0:T(8,128)(2,1)S(1)}, bf16[144,512]{1,0:T(8,128)(2,1)S(1)}, u32[]{:S(2)}, u32[]{:S(2)}) collective-permute-start(bf16[144,512]{1,0:T(8,128)(2,1)S(1)} %get-tuple-element.63), channel_id=1, source_target_pairs={{0,2},{1,3},{2,0},{3,1},{4,6},{5,7},{6,4},{7,5},{8,10},{9,11},{10,... | collective-permute-start | bytes 442376 | tf_op jit(solution)/shard_map/ppermute | solution.py:56
  101.6 7.9 %collective-permute-start.26 = (bf16[144,512]{1,0:T(8,128)(2,1)S(1)}, bf16[144,512]{1,0:T(8,128)(2,1)S(1)}, u32[]{:S(2)}, u32[]{:S(2)}) collective-permute-start(bf16[144,512]{1,0:T(8,128)(2,1)S(1)} %get-tuple-element.64), channel_id=1, source_target_pairs={{0,4},{1,5},{2,6},{3,7},{4,0},{5,1},{6,2},{7,3},{8,12},{9,13},{10,... | collective-permute-start | bytes 442376 | tf_op jit(solution)/shard_map/ppermute | solution.py:56
  104.9 6.4 %collective-permute-start.27 = (bf16[144,512]{1,0:T(8,128)(2,1)S(1)}, bf16[144,512]{1,0:T(8,128)(2,1)S(1)}, u32[]{:S(2)}, u32[]{:S(2)}) collective-permute-start(bf16[144,512]{1,0:T(8,128)(2,1)S(1)} %get-tuple-element.65), channel_id=1, source_target_pairs={{0,6},{1,7},{2,4},{3,5},{4,2},{5,3},{6,0},{7,1},{8,14},{9,15},{10,... | collective-permute-start | bytes 442376 | tf_op jit(solution)/shard_map/ppermute | solution.py:56
where the time goes:
time: 113 us
  starting transfers between devices  39.6 us (35%)
  waiting for transfers between devices  38.6 us (34%)
  Pallas kernels  33.3 us (29%)
    ppermute x31, starting transfers between devices, send(): return lax.ppermute(x, AXES, pairs)  39.6 us
    ppermute x31, waiting for transfers between devices, send(): return lax.ppermute(x, AXES, pairs)  38.6 us
    pallas_call x20, Pallas kernels, call(): pl.pallas_call(kernel, out_shape=out_shape, in_specs=[pl.BlockSpec(memory...  33.3 us
  transfers between devices with their start and end apart: 31, of which 19 were waited for; matrix products, arithmetic and copies ran while one was open for 0% of the time, Pallas kernels for 20%

commit v1 on v0

--- a/solution.py
+++ b/solution.py
@@ -13,6 +13,7 @@
 SIDE = 4
 CORES = 2
 AXES = ("row", "col")
+ORDER = (3, 2, 1)
 
 
 def route(step):
@@ -72,15 +73,19 @@
     return lax.dot_general(a, b, dims, preferred_element_type=F32)
 
 
-def call(kernel, out_shape, args, flops=0, scratch=(), hbm=0, limit=VMEM_LIMIT, scalar=None):
+def call(kernel, out_shape, args, flops=0, scratch=(), hbm=0, limit=VMEM_LIMIT):
     size = sum(a.size * a.dtype.itemsize for a in args)
     size += sum(math.prod(o.shape) * o.dtype.itemsize for o in jax.tree.leaves(out_shape))
     return pl.pallas_call(
         kernel,
         out_shape=out_shape,
-        in_specs=[pl.BlockSpec(memory_space=pltpu.HBM)] * hbm + [pl.BlockSpec(memory_space=pltpu.VMEM)] * (len(args) - hbm),
+        in_specs=(
+            [pl.BlockSpec(memory_space=pltpu.HBM)] * max(hbm, 0)
+            + [pl.BlockSpec(memory_space=pltpu.VMEM)] * (len(args) - abs(hbm))
+            + [pl.BlockSpec(memory_space=pl.ANY)] * max(-hbm, 0)
+        ),
         out_specs=jax.tree.map(
-            lambda o: pl.BlockSpec(memory_space=pltpu.SMEM if o is scalar else pltpu.VMEM), out_shape
+            lambda o: pl.BlockSpec(memory_space=pltpu.SMEM if o.shape == (1, 1) else pltpu.VMEM), out_shape
         ),
         scratch_shapes=scratch,
         compiler_params=pltpu.CompilerParams(vmem_limit_bytes=limit),
@@ -113,36 +118,37 @@
     unit_block(*(ref[...] for ref in buffers), out_ref)
 
 
-def prepare_kernel(student_ref, teacher_ref, sketch_ref, out_ref):
+def prepare_kernel(student_ref, teacher_ref, sketch_ref, *refs):
+    out_ref = refs[-1]
     unit_block(student_ref[...], teacher_ref[...], sketch_ref[...], out_ref)
 
 
-def prepare(student, teacher, sketch, first_kernel):
+def prepare(student, teacher, sketch, first_kernel, after=()):
     rows, width = student.shape
     out = jax.ShapeDtypeStruct((rows, 2 * width), BF16)
     args = (student, teacher, sketch)
     flops = 2 * rows * sketch.size
     if not first_kernel:
-        return call(prepare_kernel, out, args, flops)
+        return call(prepare_kernel, out, (*args, *after), flops, hbm=-len(after))
     scratch = [pltpu.VMEM(x.shape, x.dtype) for x in args] + [pltpu.SemaphoreType.DMA((len(args),))]
     return call(prepare_first_kernel, out, args, flops, scratch, hbm=3, limit=FIRST_LIMIT)
 
 
-def lay_end_kernel(*refs):
-    txt_refs, img_refs, (low_ref, high_ref, img_ref) = refs[:SIDE], refs[SIDE : 2 * SIDE], refs[2 * SIDE :]
-    rows = img_refs[0].shape[0]
-    for n in range(SIDE):
-        img_ref[n * rows : (n + 1) * rows, :] = img_refs[n][...]
-        half = low_ref if n < SIDE // 2 else high_ref
-        at = n % (SIDE // 2) * rows
-        half[at : at + rows, :] = txt_refs[n][...]
-
-
-def lay_end(txt, img):
-    rows, width = txt[0].shape
-    half = jax.ShapeDtypeStruct((SIDE // 2 * rows, width), BF16)
-    out = (half, half, jax.ShapeDtypeStruct((SIDE * rows, width), BF16))
-    return call(lay_end_kernel, out, (*txt, *img))
+def lay_end_kernel(count, sizes, *refs):
+    blocks = iter(refs[:count])
+    for size, out_ref in zip(sizes, refs[count:]):
+        at = 0
+        for ref in (next(blocks) for _ in range(size)):
+            out_ref[at : at + ref.shape[0], :] = ref[...]
+            at += ref.shape[0]
+
+
+def lay_end(groups, after=()):
+    width = groups[0][0].shape[1]
+    out = [jax.ShapeDtypeStruct((sum(block.shape[0] for block in group), width), BF16) for group in groups]
+    args = [block for group in groups for block in group] + list(after)
+    sizes = [len(group) for group in groups]
+    return call(lambda *refs: lay_end_kernel(len(args), sizes, *refs), out, args, hbm=-len(after))
 
 
 def products(img, txt_refs):
@@ -177,50 +183,90 @@
         row_ref[:, pl.ds(at, 128)] = packed[k * 128 : (k + 1) * 128].T[:8]
 
 
+def put_sums(row_ref, n, *tiles):
+    for k in range(BLOCK // 128):
+        sums = [jnp.sum(tile[k * 128 : (k + 1) * 128].T, axis=0, keepdims=True) for tile in tiles]
+        at = pl.multiple_of(n * BLOCK + k * 128, 128)
+        row_ref[:, pl.ds(at, 128)] = stack_rows(*sums, (8, 128))
+
+
 def stack_rows(first, second, third, shape):
     sub = lax.broadcasted_iota(jnp.int32, shape, 0)
     return jnp.where(sub == 0, first, jnp.where(sub == 1, second, third))
 
 
-def stats_kernel(has_old, own_ref, other_ref, low_ref, high_ref, *refs):
-    txt_refs = (low_ref, high_ref)
+def merge_rows(new, old):
+    top = jnp.maximum(new, old)
+    new_w, old_w = jnp.exp2(new - top), jnp.exp2(old - top)
+    total = new_w + old_w
+    mean = (new_w[0:1] * new + old_w[0:1] * old) / total[0:1]
+    lse = top + jnp.log2(total)
+    return stack_rows(lse, lse, mean, new.shape)
+
+
+def stats_kernel(pairs, has_old, own_ref, other_ref, *refs):
+    halves, refs = refs[: 2 * pairs], refs[2 * pairs :]
     old_ref = refs[0] if has_old else None
-    row_ref, col_ref, block_ref = refs[int(has_old) :]
-    columns = col_ref.shape[1]
+    row_ref, col_ref, block_ref, low_ref, high_ref, part_ref = refs[int(has_old) :]
+    columns = col_ref.shape[1] // pairs
     blocks = 2 * own_ref.shape[0] // BLOCK
 
     def step(n, state):
         load_block(n, own_ref, other_ref, block_ref)
-        p, q = products(block_ref[...], txt_refs)
-        ep = jnp.exp2(units * p - SHIFT)
-        eq = jnp.exp2(units * q - SHIFT)
-        ed = ep * (p - q)
-        put_rows(row_ref, n, *(jnp.sum(x, axis=1, keepdims=True) for x in (ep, eq, ed)))
-        return tuple(s + jnp.sum(x, axis=0, keepdims=True) for s, x in zip(state, (ep, eq, ed)))
+        row_sums, out = None, []
+        for m in range(pairs):
+            p, q = products(block_ref[...], halves[2 * m : 2 * m + 2])
+            ep = jnp.exp2(units * p - SHIFT)
+            eq = jnp.exp2(units * q - SHIFT)
+            tiles = (ep, eq, ep * (p - q))
+            out += [s + jnp.sum(x, axis=0, keepdims=True) for s, x in zip(state[3 * m : 3 * m + 3], tiles)]
+            part = [sum(x[:, c : c + 128] for c in range(0, columns, 128)) for x in tiles]
+            row_sums = part if row_sums is None else [x + y for x, y in zip(row_sums, part)]
+        put_sums(row_ref, n, *row_sums)
+        return tuple(out)
 
     zero = jnp.zeros((1, columns), F32)
-    sp, sq, u = lax.fori_loop(0, blocks, step, (zero, zero, zero))
+    state = lax.fori_loop(0, blocks, step, (zero,) * (3 * pairs), unroll=pairs == 1)
     rows = row_ref[...]
-    lowest = jnp.minimum(jnp.min(rows[0:2, :]), jnp.min(jnp.minimum(sp, sq)))
-    col_ref[...] = stack_rows(SHIFT + jnp.log2(sp), SHIFT + jnp.log2(sq), units * u / sp, col_ref.shape)
+    lowest = jnp.min(rows[0:2, :])
+    for m in range(pairs):
+        sp, sq, u = state[3 * m : 3 * m + 3]
+        lowest = jnp.minimum(lowest, jnp.min(jnp.minimum(sp, sq)))
+        col_ref[:, m * columns : (m + 1) * columns] = stack_rows(
+            SHIFT + jnp.log2(sp), SHIFT + jnp.log2(sq), units * u / sp, (8, columns)
+        )
     row_ref[...] = stack_rows(SHIFT + jnp.log2(rows), SHIFT + jnp.log2(rows), units * rows / rows[0:1], rows.shape)
 
     @pl.when(lowest < 2.0 ** (LOWEST - SHIFT))
     def _():
-        careful_stats(own_ref, other_ref, txt_refs, row_ref, col_ref, block_ref)
+        def pair(m, _):
+            for n in range(pairs):
+
+                @pl.when(m == n)
+                def _():
+                    low_ref[...] = halves[2 * n][...]
+                    high_ref[...] = halves[2 * n + 1][...]
+
+            col = careful_stats(own_ref, other_ref, (low_ref, high_ref), part_ref, columns, block_ref)
+            col_ref[:, pl.ds(pl.multiple_of(m * columns, columns), columns)] = col
+
+            @pl.when(m == 0)
+            def _():
+                row_ref[...] = part_ref[...]
+
+            @pl.when(m > 0)
+            def _():
+                row_ref[...] = merge_rows(part_ref[...], row_ref[...])
+
+            return 0
+
+        lax.fori_loop(0, pairs, pair, 0)
 
     if has_old:
-        new, old = row_ref[...], old_ref[...]
-        top = jnp.maximum(new, old)
-        new_w, old_w = jnp.exp2(new - top), jnp.exp2(old - top)
-        total = new_w + old_w
-        mean = (new_w[0:1] * new + old_w[0:1] * old) / total[0:1]
-        lse = top + jnp.log2(total)
-        row_ref[...] = stack_rows(lse, lse, mean, new.shape)
-
-
-def careful_stats(own_ref, other_ref, txt_refs, row_ref, col_ref, block_ref):
-    columns = col_ref.shape[1]
+        row_ref[...] = merge_rows(row_ref[...], old_ref[...])
+
+
+def careful_stats(own_ref, other_ref, txt_refs, row_ref, columns, block_ref):
 
     def step(n, state):
         load_block(n, own_ref, other_ref, block_ref)
@@ -246,19 +292,26 @@
     zero = jnp.zeros((1, columns), F32)
     blocks = 2 * own_ref.shape[0] // BLOCK
     mp, sp, u, mq, sq = lax.fori_loop(0, blocks, step, (low, zero, zero, low, zero))
-    col_ref[...] = stack_rows(mp + jnp.log2(sp), mq + jnp.log2(sq), u / sp, col_ref.shape)
-
-
-def tile_stats(own, other, txt, old):
-    columns = 2 * txt[0].shape[0]
+    return stack_rows(mp + jnp.log2(sp), mq + jnp.log2(sq), u / sp, (8, columns))
+
+
+def tile_stats(own, other, halves, old):
+    pairs = len(halves) // 2
+    half = halves[0].shape
+    columns = len(halves) * half[0]
     rows = 2 * own.shape[0]
-    args = [own, other, *txt] + ([] if old is None else [old])
+    args = [own, other, *halves] + ([] if old is None else [old])
     return call(
-        lambda *refs: stats_kernel(old is not None, *refs),
+        lambda *refs: stats_kernel(pairs, old is not None, *refs),
         (jax.ShapeDtypeStruct((8, rows), F32), jax.ShapeDtypeStruct((8, columns), F32)),
         args,
         2 * rows * columns * own.shape[1],
-        scratch=[pltpu.VMEM((BLOCK, own.shape[1]), BF16)],
+        scratch=[
+            pltpu.VMEM((BLOCK, half[1]), BF16),
+            pltpu.VMEM(half, BF16),
+            pltpu.VMEM(half, BF16),
+            pltpu.VMEM((8, rows), F32),
+        ],
     )
 
 
@@ -288,12 +341,12 @@
     return jnp.concatenate([first[:3], second[:3], first[:2]], axis=0)
 
 
-def local_kernel(row_ref, c0, c1, c2, c3, out_ref):
+def local_kernel(row_ref, near_ref, far_ref, out_ref):
     def columns(second, first):
+        if second == 2:
+            return far_ref[:, lanes(first)]
         half, at = divmod(first, SIDE // 2)
-        if second in (0, 2):
-            return (c0 if second == 0 else c3)[:, lanes(first)]
-        return (c1, c2)[half][:, lanes(at + (0 if second == 1 else 2))]
+        return near_ref[:, lanes({0: (0, 2), 1: (4, 8), 3: (6, 10)}[second][half] + at)]
 
     for core in range(CORES):
 
@@ -321,7 +374,7 @@
             out_ref[:, lanes(z, 0)] = rows_3(rows[:, lanes(0, z)], rows[:, lanes(1, z)])
 
 
-def line_kernel(own_ref, g1, g2, g3, out_ref):
+def line_kernel(own_ref, g3, g2, g1, out_ref):
     width = own_ref.shape[1] // SIDE
     got = (own_ref, g1, g2, g3)
     for n in range(SIDE):
@@ -343,7 +396,7 @@
                     row_ref[:, lanes(k, z)] = rows_3(part, part)
 
 
-def plane_kernel(own_ref, g1, g2, g3, out_ref):
+def plane_kernel(own_ref, g3, g2, g1, row_ref, out_ref, row_tail_ref, col_tail_ref, lowest_ref):
     got = (own_ref, g1, g2, g3)
     for x in range(SIDE):
         for y in range(SIDE):
@@ -357,14 +410,25 @@
             def _():
                 out_ref[:, lanes(x, y)] = part
 
+    put_tail(row_tail_ref, 0, kl_sum(row_ref[...]))
+    put_tail(col_tail_ref, 0, kl_sum(out_ref[...]))
+    lowest = jnp.minimum(
+        jnp.min(row_ref[0:2, :], axis=1, keepdims=True), jnp.min(out_ref[0:2, :], axis=1, keepdims=True)
+    )
+    lowest_ref[...] = jnp.broadcast_to(jnp.min(lowest, axis=0, keepdims=True), lowest_ref.shape)
+
 
 def exchange(row, cols):
-    out = jax.ShapeDtypeStruct((8, len(cols) * cols[0].shape[1]), F32)
+    columns = sum(col.shape[1] for col in cols)
+    out = jax.ShapeDtypeStruct((8, columns), F32)
+    tail = jax.ShapeDtypeStruct((TAIL, columns // SIDE), BF16)
     local = call(local_kernel, out, (row, *cols))
     chip = call(chip_kernel, out, (local, send(local, other_core())))
-    line = call(line_kernel, out, (chip, *(send(chip, x_or_z(e)) for e in range(1, SIDE))))
+    line = call(line_kernel, out, (chip, *(send(chip, x_or_z(e)) for e in ORDER)))
     col, row = call(split_kernel, (out, jax.ShapeDtypeStruct(row.shape, F32)), (line, send(line, other_core())))
-    return call(plane_kernel, out, (col, *(send(col, along_y(e)) for e in range(1, SIDE)))), row
+    parts = [send(col, along_y(e)) for e in ORDER]
+    col, *rest = call(plane_kernel, (out, tail, tail, jax.ShapeDtypeStruct((8, 128), F32)), (col, *parts, row))
+    return row, col, *rest
 
 
 def kl_sum(stats):
@@ -388,15 +452,15 @@
     return jnp.sum(ref[at : at + TAIL, :].astype(F32), axis=0, keepdims=True)
 
 
-def grad_kernel(piece, own_ref, other_ref, low_ref, high_ref, row_ref, col_ref, *refs):
+def grad_kernel(piece, own_ref, other_ref, low_ref, high_ref, row_ref, col_ref, lowest_ref, *refs):
+    *tail, g_ref, out_ref, block_ref = refs
     txt_refs = (low_ref, high_ref)
-    *got, g_ref, out_ref, block_ref = refs
     columns = g_ref.shape[1]
     width = own_ref.shape[1] // 2
     half = own_ref.shape[0]
     blocks = 2 * half // BLOCK
     stats = col_ref[:, piece * columns : (piece + 1) * columns]
-    lowest = jnp.minimum(jnp.min(row_ref[0:2, :]), jnp.min(stats[0:2, :]))
+    lowest = lowest_ref[0, 0]
 
     def turned(n, x):
         out = []
@@ -418,7 +482,7 @@
             g_ref[pl.ds(pl.multiple_of(n * BLOCK, BLOCK), BLOCK), :] = g.astype(BF16)
             return 0
 
-        lax.fori_loop(0, blocks, step, 0)
+        lax.fori_loop(0, blocks, step, 0, unroll=True)
 
     @pl.when(lowest < LOWEST)
     def _():
@@ -436,22 +500,21 @@
         lax.fori_loop(0, blocks, step, 0)
 
     total = dot(g_ref[:half, :], own_ref[:, :width], TN) + dot(g_ref[half:, :], other_ref[:, :width], TN)
-    if got:
-        out_ref[...] = total + got[0][:columns, :].astype(F32)
-    else:
-        out_ref[:columns, :] = total.astype(BF16)
-        put_tail(out_ref, columns, kl_sum(row_ref[...]))
-
-
-def tile_grad(own, other, txt, row, col, piece, got=None):
+    out_ref[:columns, :] = total.astype(out_ref.dtype)
+    if tail:
+        out_ref[columns:, :] = tail[0][...]
+
+
+def tile_grad(own, other, txt, stats, piece):
+    row, col, row_tail, _, lowest = stats
     rows = own.shape[0] + other.shape[0]
     columns, width = 2 * txt[0].shape[0], own.shape[1]
     shape = jax.ShapeDtypeStruct
-    out = shape((columns + TAIL, width // 2), BF16) if got is None else shape((columns, width // 2), F32)
+    out = shape((columns + TAIL, width // 2), BF16) if piece else shape((columns, width // 2), F32)
     return call(
         lambda *refs: grad_kernel(piece, *refs),
         (shape((rows, columns), BF16), out),
-        (own, other, *txt, row, col) + (() if got is None else (got,)),
+        (own, other, *txt, row, col, lowest) + ((row_tail,) if piece else ()),
         3 * rows * columns * width,
         scratch=[pltpu.VMEM((BLOCK, width), BF16)],
     )
@@ -471,63 +534,59 @@
         store(pl.ds(at, BLOCK), total)
         return 0
 
-    lax.fori_loop(0, half // BLOCK, step, 0)
+    lax.fori_loop(0, half // BLOCK, step, 0, unroll=True)
 
 
 def other_images_kernel(*refs):
-    grad_refs, txt_refs = refs[:SIDE], refs[SIDE : 3 * SIDE]
-    stats_ref, own_ref, got_ref, out_ref, sum_ref = refs[3 * SIDE :]
+    tail_ref, out_ref = refs[3 * SIDE :]
     half = out_ref.shape[0] - TAIL
-    sum_ref[...] = own_ref[...] + got_ref[: own_ref.shape[0], :].astype(F32)
 
     def store(span, value):
         out_ref[span, :] = value.astype(BF16)
 
-    image_rows(half, half, grad_refs, txt_refs, store)
-    put_tail(out_ref, half, kl_sum(stats_ref[...]))
+    image_rows(half, half, refs[:SIDE], refs[SIDE : 3 * SIDE], store)
+    out_ref[half:, :] = tail_ref[...]
 
 
 def own_images_kernel(*refs):
-    grad_refs, txt_refs = refs[:SIDE], refs[SIDE : 3 * SIDE]
     out_ref = refs[-5]
-    image_rows(0, out_ref.shape[0], grad_refs, txt_refs, lambda span, value: out_ref.__setitem__((span, slice(None)), value))
-    combine_kernel(2, *refs[3 * SIDE : -5], *refs[-4:])
-
-
-def image_grads(grads, txts, every, row, own, got):
+
+    def store(span, value):
+        out_ref[span, :] = value
+
+    image_rows(0, out_ref.shape[0], refs[:SIDE], refs[SIDE : 3 * SIDE], store)
+    combine_kernel(*refs[3 * SIDE : -5], *refs[-4:])
+
+
+def image_grads(grads, txts, stats, own, got):
     rows, columns = grads[0].shape
     txts = [half for piece in txts for half in piece]
     width = txts[0].shape[1] // 2
     half = rows // 2
     shape = jax.ShapeDtypeStruct
     flops = half * columns * SIDE * width * 2
-    message, own = call(
-        other_images_kernel,
-        (shape((half + TAIL, width), BF16), shape(own.shape, F32)),
-        (*grads, *txts, every, own, got[1]),
-        flops,
-    )
+    message = call(other_images_kernel, shape((half + TAIL, width), BF16), (*grads, *txts, stats[3]), flops)
     step = own.shape[0] // SIDE
     out = shape((step + TAIL, width), BF16)
     own_img, *texts = call(
         own_images_kernel,
         (shape((half, width), F32), shape((step + 8, width), F32), out, out, out),
-        (*grads, *txts, own, row, *got),
+        (*grads, *txts, own, stats[2], *got),
         flops,
     )
     return message, own_img, texts
 
 
-def combine_kernel(added, own_ref, stats_ref, *refs):
+def combine_kernel(own_ref, tail_ref, *refs):
     count = len(refs) - SIDE
-    got, (keep_ref, *out) = refs[:count], refs[count:]
+    got, outs = refs[:count], refs[count:]
     size = own_ref.shape[0]
     step = size // SIDE
-    value = kl_sum(stats_ref[...]) + sum(get_tail(ref, size) for ref in got)
-    for n, ref in enumerate([keep_ref, *out]):
+    value = get_tail(tail_ref, 0) + sum(get_tail(ref, size) for ref in got)
+    for n, ref in enumerate(outs):
         span = slice(n * step, (n + 1) * step)
         total = own_ref[span, :]
-        for part in got[added:]:
+        for part in got:
             total = total + part[span, :].astype(F32)
         ref[:step, :] = total.astype(ref.dtype)
         if n:
@@ -536,13 +595,12 @@
             ref[step:, :] = jnp.broadcast_to(value, (8, value.shape[1]))
 
 
-def combine(own, stats, got):
+def combine(own, tail, got):
     size, width = own.shape
     step = size // SIDE
     message = jax.ShapeDtypeStruct((step + TAIL, width), BF16)
     keep = jax.ShapeDtypeStruct((step + 8, width), F32)
-    out = (keep, message, message, message)
-    return call(lambda *refs: combine_kernel(0, *refs), out, (own, stats, *got))
+    return call(combine_kernel, (keep, message, message, message), (own, tail, *got))
 
 
 def tangent(x_ref, keep_ref, got, grad_ref):
@@ -566,39 +624,37 @@
 def finish(image, text, factor):
     loss = jax.ShapeDtypeStruct((1, 1), F32)
     out = tuple(jax.ShapeDtypeStruct(x.shape, F32) for x in (image[0], text[0])) + (loss,)
-    return call(lambda *refs: finish_kernel(factor, *refs), out, (*image, *text), scalar=loss)
+    return call(lambda *refs: finish_kernel(factor, *refs), out, (*image, *text))
 
 
 def shards(image_student, text_student, image_teacher, text_teacher, sketch):
     rows, width = image_student.shape
     txt = prepare(text_student, text_teacher, sketch, True)
-    img = prepare(image_student, image_teacher, sketch, False)
-
-    low, high, own = lay_end(
-        [txt] + [send(txt, first(e)) for e in range(1, SIDE)],
-        [img] + [send(img, along_z(e)) for e in range(1, SIDE)],
-    )
+
+    blocks = [txt] + [send(txt, first(e)) for e in range(1, SIDE)]
+    img = prepare(image_student, image_teacher, sketch, False, (blocks[1],))
+    img_1, img_3 = send(img, along_z(1)), send(img, along_z(3))
+    low, high = lay_end([blocks[:2], blocks[2:]], (img_1, img_3))
     low_1, low_3 = send(low, second(1)), send(low, second(3))
     high_1, high_3 = send(high, second(1)), send(high, second(3))
     low_2, high_2 = send(low_3, second(1)), send(high_1, second(3))
     txt_all = [(low, high), (low_1, high_1), (low_2, high_2), (low_3, high_3)]
+    (own,) = lay_end([[img, img_1, send(img, along_z(2)), img_3]], (low_1, low_3, high_1, high_3))
     other = send(own, other_core())
 
-    row, cols = None, []
-    for pair in ((low, high), (low_1, low_3), (high_1, high_3), (low_2, high_2)):
-        row, col = tile_stats(own, other, pair, row)
-        cols.append(col)
-    col, row = exchange(row, cols)
+    row, near_col = tile_stats(own, other, (low, high, low_1, low_3, high_1, high_3), None)
+    row, far_col = tile_stats(own, other, (low_2, high_2), row)
+    stats = exchange(row, (near_col, far_col))
 
     grads, got = [None] * SIDE, []
     for b in (2, 1, 3):
-        grads[b], message = tile_grad(own, other, txt_all[b], row, col, b)
+        grads[b], message = tile_grad(own, other, txt_all[b], stats, b)
         got.append(send(message, second(b)))
-    grads[0], own_txt = tile_grad(own, other, txt_all[0], row, col, 0, got[0])
-    message, own_img, (keep_txt, *messages_txt) = image_grads(grads, txt_all, col, row, own_txt, got)
-    keep, *messages = combine(own_img, col, [send(message, other_core())])
-    image = [image_student, keep] + [send(m, along_z(e)) for e, m in enumerate(messages, 1)]
-    text = [text_student, keep_txt] + [send(m, first(e)) for e, m in enumerate(messages_txt, 1)]
+    grads[0], own_txt = tile_grad(own, other, txt_all[0], stats, 0)
+    message, own_img, (keep_txt, *messages_txt) = image_grads(grads, txt_all, stats, own_txt, got)
+    keep, *messages = combine(own_img, stats[3], [send(message, other_core())])
+    image = [image_student, keep] + [send(messages[e - 1], along_z(e)) for e in (3, 2, 1)]
+    text = [text_student, keep_txt] + [send(messages_txt[e - 1], first(e)) for e in (3, 2, 1)]
     pairs = rows * lax.axis_size("row") * lax.axis_size("col")
     grad_image, grad_text, mean_loss = finish(image, text, 0.5 / (LOG2E * pairs))
     return (grad_image, grad_text, mean_loss.reshape(()))

time: 113 us -> 108 us (0.956)
  Pallas kernels: 33.3 us -> 26.6 us
  waiting for transfers between devices: 38.6 us -> 40 us
    pallas_call x20 -> x19, Pallas kernels: 33.3 us -> 26.6 us  [call(): pl.pallas_call(kernel, out_shape=out_shape, in_specs=[pl.BlockSpec(memory...]
    ppermute x31, waiting for transfers between devices: 38.6 us -> 40 us  [send(): return lax.ppermute(x, AXES, pairs)]
  transfers between devices with their start and end apart: 31 -> 31, of which waited for: 19 -> 24; matrix products, arithmetic and copies ran while one was open for 0% -> 0% of each run, Pallas kernels for 20% -> 16%
where the time goes in v1:
time: 108 us
  starting transfers between devices  40.6 us (38%)
  waiting for transfers between devices  40 us (37%)
  Pallas kernels  26.6 us (25%)
    ppermute x31, starting transfers between devices, send(): return lax.ppermute(x, AXES, pairs)  40.6 us
    ppermute x31, waiting for transfers between devices, send(): return lax.ppermute(x, AXES, pairs)  40 us
    pallas_call x19, Pallas kernels, call(): pl.pallas_call(kernel, out_shape=out_shape, in_specs=[pl.BlockSpec(memory...  26.6 us
  transfers between devices with their start and end apart: 31, of which 24 were waited for; matrix products, arithmetic and copies ran while one was open for 0% of the time, Pallas kernels for 16%

profile of v1, /device:TPU:0, one launch (start us, length us, event | category | flops | bytes accessed | tf_op | source)
XLA Modules:
  0.0 108.4 jit_solution(10416817170820287508)
XLA Ops:
  0.7 2.8 %shard_map.76.refs_0_ = bf16[128,1024]{1,0:T(8,128)(2,1)} custom-call(bf16[128,512]{1,0:T(8,128)(2,1)} %refs_5_.1, bf16[128,1280]{1,0:T(8,128)(2,1)} %teacher_hbm.1, bf16[1280,512]{1,0:T(8,128)(2,1)} %sketch_ref.1), custom_call_target="tpu_custom_call" | custom-call | flops 167772160 | bytes 2031616 | tf_op jit(solution)/shard_map/pallas_call | solution.py:79
  3.4 1.7 %collective-permute-start = (bf16[128,1024]{1,0:T(8,128)(2,1)}, bf16[128,1024]{1,0:T(8,128)(2,1)S(1)}, u32[]{:S(2)}, u32[]{:S(2)}) collective-permute-start(bf16[128,1024]{1,0:T(8,128)(2,1)} %shard_map.76.refs_0_), channel_id=1, source_target_pairs={{0,32},{1,9},{2,34},{3,11},{4,36},{5,13},{6,38},{7,15},{8,40},{9,1... | collective-permute-start | bytes 786440 | tf_op jit(solution)/shard_map/ppermute | solution.py:57
  5.1 2.7 %collective-permute-start.4 = (bf16[128,1024]{1,0:T(8,128)(2,1)}, bf16[128,1024]{1,0:T(8,128)(2,1)S(1)}, u32[]{:S(2)}, u32[]{:S(2)}) collective-permute-start(bf16[128,1024]{1,0:T(8,128)(2,1)} %shard_map.76.refs_0_), channel_id=1, source_target_pairs={{0,64},{1,17},{2,66},{3,19},{4,68},{5,21},{6,70},{7,23},{8,72},{9,... | collective-permute-start | bytes 786440 | tf_op jit(solution)/shard_map/ppermute | solution.py:57
  8.2 1.9 %collective-permute-done.refs_0_.refs_1_ = bf16[128,1024]{1,0:T(8,128)(2,1)S(1)} collective-permute-done((bf16[128,1024]{1,0:T(8,128)(2,1)}, bf16[128,1024]{1,0:T(8,128)(2,1)S(1)}, u32[]{:S(2)}, u32[]{:S(2)}) %collective-permute-start) | collective-permute-done | bytes 262176 | tf_op jit(solution)/shard_map/ppermute | solution.py:57
  10.6 2.1 %collective-permute-start.1 = (bf16[128,1024]{1,0:T(8,128)(2,1)S(1)}, bf16[128,1024]{1,0:T(8,128)(2,1)S(1)}, u32[]{:S(2)}, u32[]{:S(2)}) collective-permute-start(bf16[128,1024]{1,0:T(8,128)(2,1)S(1)} %shard_map.77.refs_0_), channel_id=1, source_target_pairs={{0,2},{1,3},{2,0},{3,1},{4,6},{5,7},{6,4},{7,5},{8,10},{9,11},{10,... | collective-permute-start | bytes 786440 | tf_op jit(solution)/shard_map/ppermute | solution.py:57
  12.6 2.5 %collective-permute-start.3 = (bf16[128,1024]{1,0:T(8,128)(2,1)S(1)}, bf16[128,1024]{1,0:T(8,128)(2,1)S(1)}, u32[]{:S(2)}, u32[]{:S(2)}) collective-permute-start(bf16[128,1024]{1,0:T(8,128)(2,1)S(1)} %shard_map.77.refs_0_), channel_id=1, source_target_pairs={{0,6},{1,7},{2,4},{3,5},{4,2},{5,3},{6,0},{7,1},{8,14},{9,15},{10,... | collective-permute-start | bytes 786440 | tf_op jit(solution)/shard_map/ppermute | solution.py:57
  15.3 2.7 %collective-permute-done.5.refs_3_ = bf16[128,1024]{1,0:T(8,128)(2,1)S(1)} collective-permute-done((bf16[128,1024]{1,0:T(8,128)(2,1)}, bf16[128,1024]{1,0:T(8,128)(2,1)S(1)}, u32[]{:S(2)}, u32[]{:S(2)}) %collective-permute-start.5) | collective-permute-done | bytes 262176 | tf_op jit(solution)/shard_map/ppermute | solution.py:57
  18.1 2.7 %collective-permute-done.3.refs_5_.refs_3_ = bf16[128,1024]{1,0:T(8,128)(2,1)S(1)} collective-permute-done((bf16[128,1024]{1,0:T(8,128)(2,1)S(1)}, bf16[128,1024]{1,0:T(8,128)(2,1)S(1)}, u32[]{:S(2)}, u32[]{:S(2)}) %collective-permute-start.3) | collective-permute-done | bytes 262176 | tf_op jit(solution)/shard_map/ppermute | solution.py:57
  20.9 1.6 %collective-permute-start.6 = (bf16[256,1024]{1,0:T(8,128)(2,1)S(1)}, bf16[256,1024]{1,0:T(8,128)(2,1)S(1)}, u32[]{:S(2)}, u32[]{:S(2)}) collective-permute-start(bf16[256,1024]{1,0:T(8,128)(2,1)S(1)} %get-tuple-element.35.refs_2_.refs_4_), channel_id=1, source_target_pairs={{0,8},{1,33},{2,10},{3,35},{4,12},{5,37},{6,14},{7,39},{8,0},{9,41... | collective-permute-start | bytes 1572872 | tf_op jit(solution)/shard_map/ppermute | solution.py:57
  22.5 2.2 %collective-permute-start.7 = (bf16[256,1024]{1,0:T(8,128)(2,1)S(1)}, bf16[256,1024]{1,0:T(8,128)(2,1)S(1)}, u32[]{:S(2)}, u32[]{:S(2)}) collective-permute-start(bf16[256,1024]{1,0:T(8,128)(2,1)S(1)} %get-tuple-element.35.refs_2_.refs_4_), channel_id=1, source_target_pairs={{0,24},{1,97},{2,26},{3,99},{4,28},{5,101},{6,30},{7,103},{8,16},{... | collective-permute-start | bytes 1572872 | tf_op jit(solution)/shard_map/ppermute | solution.py:57
  26.0 2.4 %collective-permute-start.2 = (bf16[128,1024]{1,0:T(8,128)(2,1)S(1)}, bf16[128,1024]{1,0:T(8,128)(2,1)S(1)}, u32[]{:S(2)}, u32[]{:S(2)}) collective-permute-start(bf16[128,1024]{1,0:T(8,128)(2,1)S(1)} %shard_map.77.refs_0_), channel_id=1, source_target_pairs={{0,4},{1,5},{2,6},{3,7},{4,0},{5,1},{6,2},{7,3},{8,12},{9,13},{10,... | collective-permute-start | bytes 786440 | tf_op jit(solution)/shard_map/ppermute | solution.py:57
  28.3 5.5 %collective-permute-done.2.refs_2_ = bf16[128,1024]{1,0:T(8,128)(2,1)S(1)} collective-permute-done((bf16[128,1024]{1,0:T(8,128)(2,1)S(1)}, bf16[128,1024]{1,0:T(8,128)(2,1)S(1)}, u32[]{:S(2)}, u32[]{:S(2)}) %collective-permute-start.2) | collective-permute-done | bytes 262176 | tf_op jit(solution)/shard_map/ppermute | solution.py:57
  33.9 1.9 %collective-permute-done.8.refs_6_.refs_3_.refs_7_ = bf16[256,1024]{1,0:T(8,128)(2,1)S(1)} collective-permute-done((bf16[256,1024]{1,0:T(8,128)(2,1)S(1)}, bf16[256,1024]{1,0:T(8,128)(2,1)S(1)}, u32[]{:S(2)}, u32[]{:S(2)}) %collective-permute-start.8) | collective-permute-done | bytes 524320 | tf_op jit(solution)/shard_map/ppermute | solution.py:57
  35.7 2.8 %collective-permute-done.9.refs_7_.refs_3_.refs_11_ = bf16[256,1024]{1,0:T(8,128)(2,1)S(1)} collective-permute-done((bf16[256,1024]{1,0:T(8,128)(2,1)S(1)}, bf16[256,1024]{1,0:T(8,128)(2,1)S(1)}, u32[]{:S(2)}, u32[]{:S(2)}) %collective-permute-start.9) | collective-permute-done | bytes 524320 | tf_op jit(solution)/shard_map/ppermute | solution.py:57
  38.8 2.3 %collective-permute-start.12 = (bf16[256,1024]{1,0:T(8,128)(2,1)S(1)}, bf16[256,1024]{1,0:T(8,128)(2,1)S(1)}, u32[]{:S(2)}, u32[]{:S(2)}) collective-permute-start(bf16[256,1024]{1,0:T(8,128)(2,1)S(1)} %collective-permute-done.8.refs_6_.refs_3_.refs_7_), channel_id=1, source_target_pairs={{0,24},{1,97},{2,26},{3,99},{4,28},{5,101},{6,30},{7,103},{8,16},{... | collective-permute-start | bytes 1572872 | tf_op jit(solution)/shard_map/ppermute | solution.py:57
  41.3 6.1 %shard_map.80 = (f32[8,1024]{1,0:T(8,128)S(1)}, f32[8,1536]{1,0:T(8,128)S(1)}) custom-call(bf16[512,1024]{1,0:T(8,128)(2,1)S(1)} %shard_map.79.refs_0_, bf16[512,1024]{1,0:T(8,128)(2,1)S(1)} %collective-permute-done.10.refs_1_, bf16[256,1024]{1,0:T(8,128)(2,1)S(1)} %get-tuple-element.35.refs_2_.refs_4_, ...), custom_call_target="tpu_custom_call" | custom-call | flops 3221225472 | bytes 5324800 | tf_op jit(solution)/shard_map/pallas_call | solution.py:79
  47.9 1.3 %collective-permute-done.12.refs_3_.refs_9_ = bf16[256,1024]{1,0:T(8,128)(2,1)S(1)} collective-permute-done((bf16[256,1024]{1,0:T(8,128)(2,1)S(1)}, bf16[256,1024]{1,0:T(8,128)(2,1)S(1)}, u32[]{:S(2)}, u32[]{:S(2)}) %collective-permute-start.12) | collective-permute-done | bytes 524320 | tf_op jit(solution)/shard_map/ppermute | solution.py:57
  49.2 2.0 %shard_map.81 = (f32[8,1024]{1,0:T(8,128)S(1)}, f32[8,512]{1,0:T(8,128)S(1)}) custom-call(bf16[512,1024]{1,0:T(8,128)(2,1)S(1)} %shard_map.79.refs_0_, bf16[512,1024]{1,0:T(8,128)(2,1)S(1)} %collective-permute-done.10.refs_1_, bf16[256,1024]{1,0:T(8,128)(2,1)S(1)} %collective-permute-done.11.refs_2_.refs_8_, ...), custom_call_target="tpu_custom_call" | custom-call | flops 1073741824 | bytes 3227648 | tf_op jit(solution)/shard_map/pallas_call | solution.py:79
  51.8 0.9 collective-permute-done.13.got_ref
  52.7 2.8 %collective-permute-start.14 = (f32[8,2048]{1,0:T(8,128)S(1)}, f32[8,2048]{1,0:T(8,128)S(1)}, u32[]{:S(2)}, u32[]{:S(2)}) collective-permute-start(f32[8,2048]{1,0:T(8,128)S(1)} %shard_map.83.own_ref), channel_id=1, source_target_pairs={{0,96},{1,7},{2,98},{3,5},{4,100},{5,3},{6,102},{7,1},{8,104},{9,1... | collective-permute-start | bytes 196616 | tf_op jit(solution)/shard_map/ppermute | solution.py:57
  55.5 0.8 collective-permute-start.15
  56.9 1.4 %collective-permute-done.14.g3 = f32[8,2048]{1,0:T(8,128)S(1)} collective-permute-done((f32[8,2048]{1,0:T(8,128)S(1)}, f32[8,2048]{1,0:T(8,128)S(1)}, u32[]{:S(2)}, u32[]{:S(2)}) %collective-permute-start.14) | collective-permute-done | bytes 65568 | tf_op jit(solution)/shard_map/ppermute | solution.py:57
  58.3 3.0 %collective-permute-done.15.g2 = f32[8,2048]{1,0:T(8,128)S(1)} collective-permute-done((f32[8,2048]{1,0:T(8,128)S(1)}, f32[8,2048]{1,0:T(8,128)S(1)}, u32[]{:S(2)}, u32[]{:S(2)}) %collective-permute-start.15) | collective-permute-done | bytes 65568 | tf_op jit(solution)/shard_map/ppermute | solution.py:57
  61.5 1.2 %collective-permute-done.17.got_ref = f32[8,2048]{1,0:T(8,128)S(1)} collective-permute-done((f32[8,2048]{1,0:T(8,128)S(1)}, f32[8,2048]{1,0:T(8,128)S(1)}, u32[]{:S(2)}, u32[]{:S(2)}) %collective-permute-start.17) | collective-permute-done | bytes 65568 | tf_op jit(solution)/shard_map/ppermute | solution.py:57
  62.7 2.4 %collective-permute-start.18 = (f32[8,2048]{1,0:T(8,128)S(1)}, f32[8,2048]{1,0:T(8,128)S(1)}, u32[]{:S(2)}, u32[]{:S(2)}) collective-permute-start(f32[8,2048]{1,0:T(8,128)S(1)} %get-tuple-element.42.own_ref), channel_id=1, source_target_pairs={{0,24},{1,25},{2,26},{3,27},{4,28},{5,29},{6,30},{7,31},{8,16},{9,... | collective-permute-start | bytes 196616 | tf_op jit(solution)/shard_map/ppermute | solution.py:57
  65.8 1.3 %collective-permute-start.20 = (f32[8,2048]{1,0:T(8,128)S(1)}, f32[8,2048]{1,0:T(8,128)S(1)}, u32[]{:S(2)}, u32[]{:S(2)}) collective-permute-start(f32[8,2048]{1,0:T(8,128)S(1)} %get-tuple-element.42.own_ref), channel_id=1, source_target_pairs={{0,8},{1,9},{2,10},{3,11},{4,12},{5,13},{6,14},{7,15},{8,0},{9,1},... | collective-permute-start | bytes 196616 | tf_op jit(solution)/shard_map/ppermute | solution.py:57
  67.1 1.4 %collective-permute-done.18.g3 = f32[8,2048]{1,0:T(8,128)S(1)} collective-permute-done((f32[8,2048]{1,0:T(8,128)S(1)}, f32[8,2048]{1,0:T(8,128)S(1)}, u32[]{:S(2)}, u32[]{:S(2)}) %collective-permute-start.18) | collective-permute-done | bytes 65568 | tf_op jit(solution)/shard_map/ppermute | solution.py:57
  68.5 2.8 %collective-permute-done.19.g2 = f32[8,2048]{1,0:T(8,128)S(1)} collective-permute-done((f32[8,2048]{1,0:T(8,128)S(1)}, f32[8,2048]{1,0:T(8,128)S(1)}, u32[]{:S(2)}, u32[]{:S(2)}) %collective-permute-start.19) | collective-permute-done | bytes 65568 | tf_op jit(solution)/shard_map/ppermute | solution.py:57
  71.7 2.6 %shard_map.89 = (bf16[1024,512]{1,0:T(8,128)(2,1)S(1)}, bf16[528,512]{1,0:T(8,128)(2,1)S(1)}) custom-call(bf16[512,1024]{1,0:T(8,128)(2,1)S(1)} %shard_map.79.refs_0_, bf16[512,1024]{1,0:T(8,128)(2,1)S(1)} %collective-permute-done.10.refs_1_, bf16[256,1024]{1,0:T(8,128)(2,1)S(1)} %collective-permute-done.11.refs_2_.refs_8_, ...), custom_call_target="tpu_custom_call" | custom-call | flops 1610612736 | bytes 4853760 | tf_op jit(solution)/shard_map/pallas_call | solution.py:79
  74.3 1.8 %collective-permute-start.21 = (bf16[528,512]{1,0:T(8,128)(2,1)S(1)}, bf16[528,512]{1,0:T(8,128)(2,1)S(1)}, u32[]{:S(2)}, u32[]{:S(2)}) collective-permute-start(bf16[528,512]{1,0:T(8,128)(2,1)S(1)} %get-tuple-element.51), channel_id=1, source_target_pairs={{0,16},{1,65},{2,18},{3,67},{4,20},{5,69},{6,22},{7,71},{8,24},{9,... | collective-permute-start | bytes 1622024 | tf_op jit(solution)/shard_map/ppermute | solution.py:57
  76.2 2.6 %shard_map.88 = (bf16[1024,512]{1,0:T(8,128)(2,1)S(1)}, bf16[528,512]{1,0:T(8,128)(2,1)S(1)}) custom-call(bf16[512,1024]{1,0:T(8,128)(2,1)S(1)} %shard_map.79.refs_0_, bf16[512,1024]{1,0:T(8,128)(2,1)S(1)} %collective-permute-done.10.refs_1_, bf16[256,1024]{1,0:T(8,128)(2,1)S(1)} %collective-permute-done.6.refs_4_.refs_2_.refs_6_, ...), custom_call_target="tpu_custom_call" | custom-call | flops 1610612736 | bytes 4853760 | tf_op jit(solution)/shard_map/pallas_call | solution.py:79
  79.2 2.6 %shard_map.90 = (bf16[1024,512]{1,0:T(8,128)(2,1)S(1)}, bf16[528,512]{1,0:T(8,128)(2,1)S(1)}) custom-call(bf16[512,1024]{1,0:T(8,128)(2,1)S(1)} %shard_map.79.refs_0_, bf16[512,1024]{1,0:T(8,128)(2,1)S(1)} %collective-permute-done.10.refs_1_, bf16[256,1024]{1,0:T(8,128)(2,1)S(1)} %collective-permute-done.7.refs_5_.refs_2_.refs_10_, ...), custom_call_target="tpu_custom_call" | custom-call | flops 1610612736 | bytes 4853760 | tf_op jit(solution)/shard_map/pallas_call | solution.py:79
  81.8 2.1 %collective-permute-start.23 = (bf16[528,512]{1,0:T(8,128)(2,1)S(1)}, bf16[528,512]{1,0:T(8,128)(2,1)S(1)}, u32[]{:S(2)}, u32[]{:S(2)}) collective-permute-start(bf16[528,512]{1,0:T(8,128)(2,1)S(1)} %get-tuple-element.53), channel_id=1, source_target_pairs={{0,24},{1,97},{2,26},{3,99},{4,28},{5,101},{6,30},{7,103},{8,16},{... | collective-permute-start | bytes 1622024 | tf_op jit(solution)/shard_map/ppermute | solution.py:57
  83.9 2.8 %shard_map.87 = (bf16[1024,512]{1,0:T(8,128)(2,1)S(1)}, f32[512,512]{1,0:T(8,128)S(1)}) custom-call(bf16[512,1024]{1,0:T(8,128)(2,1)S(1)} %shard_map.79.refs_0_, bf16[512,1024]{1,0:T(8,128)(2,1)S(1)} %collective-permute-done.10.refs_1_, bf16[256,1024]{1,0:T(8,128)(2,1)S(1)} %get-tuple-element.35.refs_2_.refs_4_, ...), custom_call_target="tpu_custom_call" | custom-call | flops 1610612736 | bytes 5345280 | tf_op jit(solution)/shard_map/pallas_call | solution.py:79
  86.7 1.2 %shard_map.92 = bf16[528,512]{1,0:T(8,128)(2,1)S(1)} custom-call(bf16[1024,512]{1,0:T(8,128)(2,1)S(1)} %get-tuple-element.45.refs_0_, bf16[1024,512]{1,0:T(8,128)(2,1)S(1)} %get-tuple-element.47.refs_1_, bf16[1024,512]{1,0:T(8,128)(2,1)S(1)} %get-tuple-element.48.refs_2_, bf16[1024,512]{1,0:T(8,128)(2,1)S(1)} %get-tuple-element.49.refs_3_, ...), custom_call_target="tpu_custom_call" | custom-call | flops 1073741824 | bytes 8945664 | tf_op jit(solution)/shard_map/pallas_call | solution.py:79
  88.0 1.6 %collective-permute-done.22.refs_15_ = bf16[528,512]{1,0:T(8,128)(2,1)S(1)} collective-permute-done((bf16[528,512]{1,0:T(8,128)(2,1)S(1)}, bf16[528,512]{1,0:T(8,128)(2,1)S(1)}, u32[]{:S(2)}, u32[]{:S(2)}) %collective-permute-start.22) | collective-permute-done | bytes 540704 | tf_op jit(solution)/shard_map/ppermute | solution.py:57
  89.7 2.8 %collective-permute-done.23.refs_16_ = bf16[528,512]{1,0:T(8,128)(2,1)S(1)} collective-permute-done((bf16[528,512]{1,0:T(8,128)(2,1)S(1)}, bf16[528,512]{1,0:T(8,128)(2,1)S(1)}, u32[]{:S(2)}, u32[]{:S(2)}) %collective-permute-start.23) | collective-permute-done | bytes 540704 | tf_op jit(solution)/shard_map/ppermute | solution.py:57
  92.5 1.5 %shard_map.91 = (f32[512,512]{1,0:T(8,128)S(1)}, f32[136,512]{1,0:T(8,128)S(1)}, bf16[144,512]{1,0:T(8,128)(2,1)S(1)}, bf16[144,512]{1,0:T(8,128)(2,1)S(1)}, bf16[144,512]{1,0:T(8,128)(2,1)S(1)}) custom-call(bf16[1024,512]{1,0:T(8,128)(2,1)S(1)} %get-tuple-element.45.refs_0_, bf16[1024,512]{1,0:T(8,128)(2,1)S(1)} %get-tuple-element.47.refs_1_, ...), custom_call_target="tpu_custom_call" | custom-call | flops 1073741824 | bytes 12845056 | tf_op jit(solution)/shard_map/pallas_call | solution.py:79
  94.1 2.6 %collective-permute-start.25 = (bf16[144,512]{1,0:T(8,128)(2,1)S(1)}, bf16[144,512]{1,0:T(8,128)(2,1)S(1)}, u32[]{:S(2)}, u32[]{:S(2)}) collective-permute-start(bf16[144,512]{1,0:T(8,128)(2,1)S(1)} %get-tuple-element.57), channel_id=1, source_target_pairs={{0,6},{1,7},{2,4},{3,5},{4,2},{5,3},{6,0},{7,1},{8,14},{9,15},{10,... | collective-permute-start | bytes 442376 | tf_op jit(solution)/shard_map/ppermute | solution.py:57
  96.8 1.4 %collective-permute-start.27 = (bf16[144,512]{1,0:T(8,128)(2,1)S(1)}, bf16[144,512]{1,0:T(8,128)(2,1)S(1)}, u32[]{:S(2)}, u32[]{:S(2)}) collective-permute-start(bf16[144,512]{1,0:T(8,128)(2,1)S(1)} %get-tuple-element.59), channel_id=1, source_target_pairs={{0,2},{1,3},{2,0},{3,1},{4,6},{5,7},{6,4},{7,5},{8,10},{9,11},{10,... | collective-permute-start | bytes 442376 | tf_op jit(solution)/shard_map/ppermute | solution.py:57
  98.3 1.4 %collective-permute-start.28 = (bf16[144,512]{1,0:T(8,128)(2,1)S(1)}, bf16[144,512]{1,0:T(8,128)(2,1)S(1)}, u32[]{:S(2)}, u32[]{:S(2)}) collective-permute-start(bf16[144,512]{1,0:T(8,128)(2,1)S(1)} %get-tuple-element.61), channel_id=1, source_target_pairs={{0,96},{1,25},{2,98},{3,27},{4,100},{5,29},{6,102},{7,31},{8,104},... | collective-permute-start | bytes 442376 | tf_op jit(solution)/shard_map/ppermute | solution.py:57
  99.7 0.9 collective-permute-start.29
  101.0 1.4 %collective-permute-start.30 = (bf16[144,512]{1,0:T(8,128)(2,1)S(1)}, bf16[144,512]{1,0:T(8,128)(2,1)S(1)}, u32[]{:S(2)}, u32[]{:S(2)}) collective-permute-start(bf16[144,512]{1,0:T(8,128)(2,1)S(1)} %get-tuple-element.63), channel_id=1, source_target_pairs={{0,32},{1,9},{2,34},{3,11},{4,36},{5,13},{6,38},{7,15},{8,40},{9,1... | collective-permute-start | bytes 442376 | tf_op jit(solution)/shard_map/ppermute | solution.py:57
  102.4 1.0 collective-permute-done.26.refs_3_
  103.4 1.3 %collective-permute-done.28.refs_7_ = bf16[144,512]{1,0:T(8,128)(2,1)S(1)} collective-permute-done((bf16[144,512]{1,0:T(8,128)(2,1)S(1)}, bf16[144,512]{1,0:T(8,128)(2,1)S(1)}, u32[]{:S(2)}, u32[]{:S(2)}) %collective-permute-start.28) | collective-permute-done | bytes 147488 | tf_op jit(solution)/shard_map/ppermute | solution.py:57
  104.6 1.7 %collective-permute-done.29.refs_8_ = bf16[144,512]{1,0:T(8,128)(2,1)S(1)} collective-permute-done((bf16[144,512]{1,0:T(8,128)(2,1)S(1)}, bf16[144,512]{1,0:T(8,128)(2,1)S(1)}, u32[]{:S(2)}, u32[]{:S(2)}) %collective-permute-start.29) | collective-permute-done | bytes 147488 | tf_op jit(solution)/shard_map/ppermute | solution.py:57
  106.3 0.7 collective-permute-done.30.refs_9_
  107.1 1.1 %shard_map.94 = (f32[128,512]{1,0:T(8,128)}, f32[128,512]{1,0:T(8,128)}, f32[1,1]{1,0:T(1,128)}) custom-call(bf16[128,512]{1,0:T(8,128)(2,1)S(1)} %copy-done.2, f32[136,512]{1,0:T(8,128)S(1)} %get-tuple-element.56.refs_1_, bf16[144,512]{1,0:T(8,128)(2,1)S(1)} %collective-permute-done.25.refs_2_, bf16[144,512]{1,0:T(8,128)(2,1)S(1)} %collective-permute-done.26.refs_3_, ...), custom_call_target="tpu_custom_call" | custom-call | bytes 2228228 | tf_op jit(solution)/shard_map/pallas_call | solution.py:79
  (43 shorter events, 7.1 us)
Async XLA Ops:
  0.6 9.5 %copy-start = (bf16[1280,512]{1,0:T(8,128)(2,1)S(1)}, bf16[1280,512]{1,0:T(8,128)(2,1)}, u32[]{:S(2)}) copy-start(bf16[1280,512]{1,0:T(8,128)(2,1)} %sketch_ref.1) | copy-start | bytes 3932164
  0.6 9.5 %copy-start.2 = (bf16[128,512]{1,0:T(8,128)(2,1)S(1)}, bf16[128,512]{1,0:T(8,128)(2,1)}, u32[]{:S(2)}) copy-start(bf16[128,512]{1,0:T(8,128)(2,1)} %refs_0_.1) | copy-start | bytes 393220
  0.7 9.5 %copy-start.4 = (bf16[128,1280]{1,0:T(8,128)(2,1)S(1)}, bf16[128,1280]{1,0:T(8,128)(2,1)}, u32[]{:S(2)}) copy-start(bf16[128,1280]{1,0:T(8,128)(2,1)} %teacher_ref.1) | copy-start | bytes 983044
  3.4 17.3 %copy-start.1 = (bf16[128,1024]{1,0:T(8,128)(2,1)S(1)}, bf16[128,1024]{1,0:T(8,128)(2,1)}, u32[]{:S(2)}) copy-start(bf16[128,1024]{1,0:T(8,128)(2,1)} %shard_map.76.refs_0_) | copy-start | bytes 786436
  3.4 6.7 %collective-permute-start = (bf16[128,1024]{1,0:T(8,128)(2,1)}, bf16[128,1024]{1,0:T(8,128)(2,1)S(1)}, u32[]{:S(2)}, u32[]{:S(2)}) collective-permute-start(bf16[128,1024]{1,0:T(8,128)(2,1)} %shard_map.76.refs_0_), channel_id=1, source_target_pairs={{0,32},{1,9},{2,34},{3,11},{4,36},{5,13},{6,38},{7,15},{8,40},{9,1... | collective-permute-start | bytes 786440 | tf_op jit(solution)/shard_map/ppermute | solution.py:57
  5.1 10.2 %collective-permute-start.4 = (bf16[128,1024]{1,0:T(8,128)(2,1)}, bf16[128,1024]{1,0:T(8,128)(2,1)S(1)}, u32[]{:S(2)}, u32[]{:S(2)}) collective-permute-start(bf16[128,1024]{1,0:T(8,128)(2,1)} %shard_map.76.refs_0_), channel_id=1, source_target_pairs={{0,64},{1,17},{2,66},{3,19},{4,68},{5,21},{6,70},{7,23},{8,72},{9,... | collective-permute-start | bytes 786440 | tf_op jit(solution)/shard_map/ppermute | solution.py:57
  7.8 10.2 %collective-permute-start.5 = (bf16[128,1024]{1,0:T(8,128)(2,1)}, bf16[128,1024]{1,0:T(8,128)(2,1)S(1)}, u32[]{:S(2)}, u32[]{:S(2)}) collective-permute-start(bf16[128,1024]{1,0:T(8,128)(2,1)} %shard_map.76.refs_0_), channel_id=1, source_target_pairs={{0,96},{1,25},{2,98},{3,27},{4,100},{5,29},{6,102},{7,31},{8,104},... | collective-permute-start | bytes 786440 | tf_op jit(solution)/shard_map/ppermute | solution.py:57
  10.6 7.5 %collective-permute-start.1 = (bf16[128,1024]{1,0:T(8,128)(2,1)S(1)}, bf16[128,1024]{1,0:T(8,128)(2,1)S(1)}, u32[]{:S(2)}, u32[]{:S(2)}) collective-permute-start(bf16[128,1024]{1,0:T(8,128)(2,1)S(1)} %shard_map.77.refs_0_), channel_id=1, source_target_pairs={{0,2},{1,3},{2,0},{3,1},{4,6},{5,7},{6,4},{7,5},{8,10},{9,11},{10,... | collective-permute-start | bytes 786440 | tf_op jit(solution)/shard_map/ppermute | solution.py:57
  12.6 8.1 %collective-permute-start.3 = (bf16[128,1024]{1,0:T(8,128)(2,1)S(1)}, bf16[128,1024]{1,0:T(8,128)(2,1)S(1)}, u32[]{:S(2)}, u32[]{:S(2)}) collective-permute-start(bf16[128,1024]{1,0:T(8,128)(2,1)S(1)} %shard_map.77.refs_0_), channel_id=1, source_target_pairs={{0,6},{1,7},{2,4},{3,5},{4,2},{5,3},{6,0},{7,1},{8,14},{9,15},{10,... | collective-permute-start | bytes 786440 | tf_op jit(solution)/shard_map/ppermute | solution.py:57
  20.9 13.0 %collective-permute-start.6 = (bf16[256,1024]{1,0:T(8,128)(2,1)S(1)}, bf16[256,1024]{1,0:T(8,128)(2,1)S(1)}, u32[]{:S(2)}, u32[]{:S(2)}) collective-permute-start(bf16[256,1024]{1,0:T(8,128)(2,1)S(1)} %get-tuple-element.35.refs_2_.refs_4_), channel_id=1, source_target_pairs={{0,8},{1,33},{2,10},{3,35},{4,12},{5,37},{6,14},{7,39},{8,0},{9,41... | collective-permute-start | bytes 1572872 | tf_op jit(solution)/shard_map/ppermute | solution.py:57
  22.5 11.3 %collective-permute-start.7 = (bf16[256,1024]{1,0:T(8,128)(2,1)S(1)}, bf16[256,1024]{1,0:T(8,128)(2,1)S(1)}, u32[]{:S(2)}, u32[]{:S(2)}) collective-permute-start(bf16[256,1024]{1,0:T(8,128)(2,1)S(1)} %get-tuple-element.35.refs_2_.refs_4_), channel_id=1, source_target_pairs={{0,24},{1,97},{2,26},{3,99},{4,28},{5,101},{6,30},{7,103},{8,16},{... | collective-permute-start | bytes 1572872 | tf_op jit(solution)/shard_map/ppermute | solution.py:57
  24.7 11.1 %collective-permute-start.8 = (bf16[256,1024]{1,0:T(8,128)(2,1)S(1)}, bf16[256,1024]{1,0:T(8,128)(2,1)S(1)}, u32[]{:S(2)}, u32[]{:S(2)}) collective-permute-start(bf16[256,1024]{1,0:T(8,128)(2,1)S(1)} %get-tuple-element.36.refs_3_.refs_5_), channel_id=1, source_target_pairs={{0,8},{1,33},{2,10},{3,35},{4,12},{5,37},{6,14},{7,39},{8,0},{9,41... | collective-permute-start | bytes 1572872 | tf_op jit(solution)/shard_map/ppermute | solution.py:57
  25.4 13.2 %collective-permute-start.9 = (bf16[256,1024]{1,0:T(8,128)(2,1)S(1)}, bf16[256,1024]{1,0:T(8,128)(2,1)S(1)}, u32[]{:S(2)}, u32[]{:S(2)}) collective-permute-start(bf16[256,1024]{1,0:T(8,128)(2,1)S(1)} %get-tuple-element.36.refs_3_.refs_5_), channel_id=1, source_target_pairs={{0,24},{1,97},{2,26},{3,99},{4,28},{5,101},{6,30},{7,103},{8,16},{... | collective-permute-start | bytes 1572872 | tf_op jit(solution)/shard_map/ppermute | solution.py:57
  26.0 7.9 %collective-permute-start.2 = (bf16[128,1024]{1,0:T(8,128)(2,1)S(1)}, bf16[128,1024]{1,0:T(8,128)(2,1)S(1)}, u32[]{:S(2)}, u32[]{:S(2)}) collective-permute-start(bf16[128,1024]{1,0:T(8,128)(2,1)S(1)} %shard_map.77.refs_0_), channel_id=1, source_target_pairs={{0,4},{1,5},{2,6},{3,7},{4,0},{5,1},{6,2},{7,3},{8,12},{9,13},{10,... | collective-permute-start | bytes 786440 | tf_op jit(solution)/shard_map/ppermute | solution.py:57
  38.6 2.7 %collective-permute-start.10 = (bf16[512,1024]{1,0:T(8,128)(2,1)S(1)}, bf16[512,1024]{1,0:T(8,128)(2,1)S(1)}, u32[]{:S(2)}, u32[]{:S(2)}) collective-permute-start(bf16[512,1024]{1,0:T(8,128)(2,1)S(1)} %shard_map.79.refs_0_), channel_id=1, source_target_pairs={{0,1},{1,0},{2,3},{3,2},{4,5},{5,4},{6,7},{7,6},{8,9},{9,8},{10,11... | collective-permute-start | bytes 3145736 | tf_op jit(solution)/shard_map/ppermute | solution.py:57
  38.7 9.3 %collective-permute-start.11 = (bf16[256,1024]{1,0:T(8,128)(2,1)S(1)}, bf16[256,1024]{1,0:T(8,128)(2,1)S(1)}, u32[]{:S(2)}, u32[]{:S(2)}) collective-permute-start(bf16[256,1024]{1,0:T(8,128)(2,1)S(1)} %collective-permute-done.7.refs_5_.refs_2_.refs_10_), channel_id=1, source_target_pairs={{0,8},{1,33},{2,10},{3,35},{4,12},{5,37},{6,14},{7,39},{8,0},{9,41... | collective-permute-start | bytes 1572872 | tf_op jit(solution)/shard_map/ppermute | solution.py:57
  38.8 10.5 %collective-permute-start.12 = (bf16[256,1024]{1,0:T(8,128)(2,1)S(1)}, bf16[256,1024]{1,0:T(8,128)(2,1)S(1)}, u32[]{:S(2)}, u32[]{:S(2)}) collective-permute-start(bf16[256,1024]{1,0:T(8,128)(2,1)S(1)} %collective-permute-done.8.refs_6_.refs_3_.refs_7_), channel_id=1, source_target_pairs={{0,24},{1,97},{2,26},{3,99},{4,28},{5,101},{6,30},{7,103},{8,16},{... | collective-permute-start | bytes 1572872 | tf_op jit(solution)/shard_map/ppermute | solution.py:57
  51.3 1.4 %collective-permute-start.13 = (f32[8,2048]{1,0:T(8,128)S(1)}, f32[8,2048]{1,0:T(8,128)S(1)}, u32[]{:S(2)}, u32[]{:S(2)}) collective-permute-start(f32[8,2048]{1,0:T(8,128)S(1)} %shard_map.82.own_ref), channel_id=1, source_target_pairs={{0,1},{1,0},{2,3},{3,2},{4,5},{5,4},{6,7},{7,6},{8,9},{9,8},{10,11... | collective-permute-start | bytes 196616 | tf_op jit(solution)/shard_map/ppermute | solution.py:57
  52.7 5.6 %collective-permute-start.14 = (f32[8,2048]{1,0:T(8,128)S(1)}, f32[8,2048]{1,0:T(8,128)S(1)}, u32[]{:S(2)}, u32[]{:S(2)}) collective-permute-start(f32[8,2048]{1,0:T(8,128)S(1)} %shard_map.83.own_ref), channel_id=1, source_target_pairs={{0,96},{1,7},{2,98},{3,5},{4,100},{5,3},{6,102},{7,1},{8,104},{9,1... | collective-permute-start | bytes 196616 | tf_op jit(solution)/shard_map/ppermute | solution.py:57
  55.5 5.8 %collective-permute-start.15 = (f32[8,2048]{1,0:T(8,128)S(1)}, f32[8,2048]{1,0:T(8,128)S(1)}, u32[]{:S(2)}, u32[]{:S(2)}) collective-permute-start(f32[8,2048]{1,0:T(8,128)S(1)} %shard_map.83.own_ref), channel_id=1, source_target_pairs={{0,64},{1,5},{2,66},{3,7},{4,68},{5,1},{6,70},{7,3},{8,72},{9,13},... | collective-permute-start | bytes 196616 | tf_op jit(solution)/shard_map/ppermute | solution.py:57
  56.3 5.0 %collective-permute-start.16 = (f32[8,2048]{1,0:T(8,128)S(1)}, f32[8,2048]{1,0:T(8,128)S(1)}, u32[]{:S(2)}, u32[]{:S(2)}) collective-permute-start(f32[8,2048]{1,0:T(8,128)S(1)} %shard_map.83.own_ref), channel_id=1, source_target_pairs={{0,32},{1,3},{2,34},{3,1},{4,36},{5,7},{6,38},{7,5},{8,40},{9,11},... | collective-permute-start | bytes 196616 | tf_op jit(solution)/shard_map/ppermute | solution.py:57
  61.4 1.3 %collective-permute-start.17 = (f32[8,2048]{1,0:T(8,128)S(1)}, f32[8,2048]{1,0:T(8,128)S(1)}, u32[]{:S(2)}, u32[]{:S(2)}) collective-permute-start(f32[8,2048]{1,0:T(8,128)S(1)} %shard_map.84.own_ref), channel_id=1, source_target_pairs={{0,1},{1,0},{2,3},{3,2},{4,5},{5,4},{6,7},{7,6},{8,9},{9,8},{10,11... | collective-permute-start | bytes 196616 | tf_op jit(solution)/shard_map/ppermute | solution.py:57
  62.7 5.7 %collective-permute-start.18 = (f32[8,2048]{1,0:T(8,128)S(1)}, f32[8,2048]{1,0:T(8,128)S(1)}, u32[]{:S(2)}, u32[]{:S(2)}) collective-permute-start(f32[8,2048]{1,0:T(8,128)S(1)} %get-tuple-element.42.own_ref), channel_id=1, source_target_pairs={{0,24},{1,25},{2,26},{3,27},{4,28},{5,29},{6,30},{7,31},{8,16},{9,... | collective-permute-start | bytes 196616 | tf_op jit(solution)/shard_map/ppermute | solution.py:57
  65.2 6.1 %collective-permute-start.19 = (f32[8,2048]{1,0:T(8,128)S(1)}, f32[8,2048]{1,0:T(8,128)S(1)}, u32[]{:S(2)}, u32[]{:S(2)}) collective-permute-start(f32[8,2048]{1,0:T(8,128)S(1)} %get-tuple-element.42.own_ref), channel_id=1, source_target_pairs={{0,16},{1,17},{2,18},{3,19},{4,20},{5,21},{6,22},{7,23},{8,24},{9,... | collective-permute-start | bytes 196616 | tf_op jit(solution)/shard_map/ppermute | solution.py:57
  65.8 5.5 %collective-permute-start.20 = (f32[8,2048]{1,0:T(8,128)S(1)}, f32[8,2048]{1,0:T(8,128)S(1)}, u32[]{:S(2)}, u32[]{:S(2)}) collective-permute-start(f32[8,2048]{1,0:T(8,128)S(1)} %get-tuple-element.42.own_ref), channel_id=1, source_target_pairs={{0,8},{1,9},{2,10},{3,11},{4,12},{5,13},{6,14},{7,15},{8,0},{9,1},... | collective-permute-start | bytes 196616 | tf_op jit(solution)/shard_map/ppermute | solution.py:57
  74.3 13.7 %collective-permute-start.21 = (bf16[528,512]{1,0:T(8,128)(2,1)S(1)}, bf16[528,512]{1,0:T(8,128)(2,1)S(1)}, u32[]{:S(2)}, u32[]{:S(2)}) collective-permute-start(bf16[528,512]{1,0:T(8,128)(2,1)S(1)} %get-tuple-element.51), channel_id=1, source_target_pairs={{0,16},{1,65},{2,18},{3,67},{4,20},{5,69},{6,22},{7,71},{8,24},{9,... | collective-permute-start | bytes 1622024 | tf_op jit(solution)/shard_map/ppermute | solution.py:57
  78.8 10.9 %collective-permute-start.22 = (bf16[528,512]{1,0:T(8,128)(2,1)S(1)}, bf16[528,512]{1,0:T(8,128)(2,1)S(1)}, u32[]{:S(2)}, u32[]{:S(2)}) collective-permute-start(bf16[528,512]{1,0:T(8,128)(2,1)S(1)} %get-tuple-element.52), channel_id=1, source_target_pairs={{0,8},{1,33},{2,10},{3,35},{4,12},{5,37},{6,14},{7,39},{8,0},{9,41... | collective-permute-start | bytes 1622024 | tf_op jit(solution)/shard_map/ppermute | solution.py:57
  81.8 10.6 %collective-permute-start.23 = (bf16[528,512]{1,0:T(8,128)(2,1)S(1)}, bf16[528,512]{1,0:T(8,128)(2,1)S(1)}, u32[]{:S(2)}, u32[]{:S(2)}) collective-permute-start(bf16[528,512]{1,0:T(8,128)(2,1)S(1)} %get-tuple-element.53), channel_id=1, source_target_pairs={{0,24},{1,97},{2,26},{3,99},{4,28},{5,101},{6,30},{7,103},{8,16},{... | collective-permute-start | bytes 1622024 | tf_op jit(solution)/shard_map/ppermute | solution.py:57
  87.9 6.0 %collective-permute-start.24 = (bf16[528,512]{1,0:T(8,128)(2,1)S(1)}, bf16[528,512]{1,0:T(8,128)(2,1)S(1)}, u32[]{:S(2)}, u32[]{:S(2)}) collective-permute-start(bf16[528,512]{1,0:T(8,128)(2,1)S(1)} %shard_map.92), channel_id=1, source_target_pairs={{0,1},{1,0},{2,3},{3,2},{4,5},{5,4},{6,7},{7,6},{8,9},{9,8},{10,11... | collective-permute-start | bytes 1622024 | tf_op jit(solution)/shard_map/ppermute | solution.py:57
  94.0 13.1 %copy-start.3 = (bf16[128,512]{1,0:T(8,128)(2,1)S(1)}, bf16[128,512]{1,0:T(8,128)(2,1)}, u32[]{:S(2)}) copy-start(bf16[128,512]{1,0:T(8,128)(2,1)} %refs_5_.1) | copy-start | bytes 393220
  94.1 6.9 %collective-permute-start.25 = (bf16[144,512]{1,0:T(8,128)(2,1)S(1)}, bf16[144,512]{1,0:T(8,128)(2,1)S(1)}, u32[]{:S(2)}, u32[]{:S(2)}) collective-permute-start(bf16[144,512]{1,0:T(8,128)(2,1)S(1)} %get-tuple-element.57), channel_id=1, source_target_pairs={{0,6},{1,7},{2,4},{3,5},{4,2},{5,3},{6,0},{7,1},{8,14},{9,15},{10,... | collective-permute-start | bytes 442376 | tf_op jit(solution)/shard_map/ppermute | solution.py:57
  96.7 6.6 %collective-permute-start.26 = (bf16[144,512]{1,0:T(8,128)(2,1)S(1)}, bf16[144,512]{1,0:T(8,128)(2,1)S(1)}, u32[]{:S(2)}, u32[]{:S(2)}) collective-permute-start(bf16[144,512]{1,0:T(8,128)(2,1)S(1)} %get-tuple-element.58), channel_id=1, source_target_pairs={{0,4},{1,5},{2,6},{3,7},{4,0},{5,1},{6,2},{7,3},{8,12},{9,13},{10,... | collective-permute-start | bytes 442376 | tf_op jit(solution)/shard_map/ppermute | solution.py:57
  96.8 6.5 %collective-permute-start.27 = (bf16[144,512]{1,0:T(8,128)(2,1)S(1)}, bf16[144,512]{1,0:T(8,128)(2,1)S(1)}, u32[]{:S(2)}, u32[]{:S(2)}) collective-permute-start(bf16[144,512]{1,0:T(8,128)(2,1)S(1)} %get-tuple-element.59), channel_id=1, source_target_pairs={{0,2},{1,3},{2,0},{3,1},{4,6},{5,7},{6,4},{7,5},{8,10},{9,11},{10,... | collective-permute-start | bytes 442376 | tf_op jit(solution)/shard_map/ppermute | solution.py:57
  98.3 6.4 %collective-permute-start.28 = (bf16[144,512]{1,0:T(8,128)(2,1)S(1)}, bf16[144,512]{1,0:T(8,128)(2,1)S(1)}, u32[]{:S(2)}, u32[]{:S(2)}) collective-permute-start(bf16[144,512]{1,0:T(8,128)(2,1)S(1)} %get-tuple-element.61), channel_id=1, source_target_pairs={{0,96},{1,25},{2,98},{3,27},{4,100},{5,29},{6,102},{7,31},{8,104},... | collective-permute-start | bytes 442376 | tf_op jit(solution)/shard_map/ppermute | solution.py:57
  99.7 6.6 %collective-permute-start.29 = (bf16[144,512]{1,0:T(8,128)(2,1)S(1)}, bf16[144,512]{1,0:T(8,128)(2,1)S(1)}, u32[]{:S(2)}, u32[]{:S(2)}) collective-permute-start(bf16[144,512]{1,0:T(8,128)(2,1)S(1)} %get-tuple-element.62), channel_id=1, source_target_pairs={{0,64},{1,17},{2,66},{3,19},{4,68},{5,21},{6,70},{7,23},{8,72},{9,... | collective-permute-start | bytes 442376 | tf_op jit(solution)/shard_map/ppermute | solution.py:57
  101.0 6.1 %collective-permute-start.30 = (bf16[144,512]{1,0:T(8,128)(2,1)S(1)}, bf16[144,512]{1,0:T(8,128)(2,1)S(1)}, u32[]{:S(2)}, u32[]{:S(2)}) collective-permute-start(bf16[144,512]{1,0:T(8,128)(2,1)S(1)} %get-tuple-element.63), channel_id=1, source_target_pairs={{0,32},{1,9},{2,34},{3,11},{4,36},{5,13},{6,38},{7,15},{8,40},{9,1... | collective-permute-start | bytes 442376 | tf_op jit(solution)/shard_map/ppermute | solution.py:57

commit v2 on v1

--- a/solution.py
+++ b/solution.py
@@ -13,7 +13,7 @@
 SIDE = 4
 CORES = 2
 AXES = ("row", "col")
-ORDER = (3, 2, 1)
+ORDER = (1, 2, 3)
 
 
 def route(step):
@@ -76,6 +76,7 @@
 def call(kernel, out_shape, args, flops=0, scratch=(), hbm=0, limit=VMEM_LIMIT):
     size = sum(a.size * a.dtype.itemsize for a in args)
     size += sum(math.prod(o.shape) * o.dtype.itemsize for o in jax.tree.leaves(out_shape))
+    size = size if flops else 0
     return pl.pallas_call(
         kernel,
         out_shape=out_shape,
@@ -207,7 +208,7 @@
 def stats_kernel(pairs, has_old, own_ref, other_ref, *refs):
     halves, refs = refs[: 2 * pairs], refs[2 * pairs :]
     old_ref = refs[0] if has_old else None
-    row_ref, col_ref, block_ref, low_ref, high_ref, part_ref = refs[int(has_old) :]
+    row_ref, col_ref, *tile_refs, block_ref, low_ref, high_ref, part_ref = refs[int(has_old) :]
     columns = col_ref.shape[1] // pairs
     blocks = 2 * own_ref.shape[0] // BLOCK
 
@@ -219,6 +220,10 @@
             ep = jnp.exp2(units * p - SHIFT)
             eq = jnp.exp2(units * q - SHIFT)
             tiles = (ep, eq, ep * (p - q))
+            span = pl.ds(pl.multiple_of(n * BLOCK, BLOCK), BLOCK)
+            for k in range(4):
+                at = k // 2 * (columns // 2)
+                tile_refs[4 * m + k][span, :] = tiles[k % 2][:, at : at + columns // 2]
             out += [s + jnp.sum(x, axis=0, keepdims=True) for s, x in zip(state[3 * m : 3 * m + 3], tiles)]
             part = [sum(x[:, c : c + 128] for c in range(0, columns, 128)) for x in tiles]
             row_sums = part if row_sums is None else [x + y for x, y in zip(row_sums, part)]
@@ -301,9 +306,10 @@
     columns = len(halves) * half[0]
     rows = 2 * own.shape[0]
     args = [own, other, *halves] + ([] if old is None else [old])
-    return call(
+    tile = jax.ShapeDtypeStruct((rows, half[0]), F32)
+    row, col, *tiles = call(
         lambda *refs: stats_kernel(pairs, old is not None, *refs),
-        (jax.ShapeDtypeStruct((8, rows), F32), jax.ShapeDtypeStruct((8, columns), F32)),
+        (jax.ShapeDtypeStruct((8, rows), F32), jax.ShapeDtypeStruct((8, columns), F32), *[tile] * (2 * len(halves))),
         args,
         2 * rows * columns * own.shape[1],
         scratch=[
@@ -313,6 +319,7 @@
             pltpu.VMEM((8, rows), F32),
         ],
     )
+    return row, col, [tiles[n : n + 2] for n in range(0, len(tiles), 2)]
 
 
 def merge(parts):
@@ -374,7 +381,7 @@
             out_ref[:, lanes(z, 0)] = rows_3(rows[:, lanes(0, z)], rows[:, lanes(1, z)])
 
 
-def line_kernel(own_ref, g3, g2, g1, out_ref):
+def line_kernel(own_ref, g1, g2, g3, out_ref):
     width = own_ref.shape[1] // SIDE
     got = (own_ref, g1, g2, g3)
     for n in range(SIDE):
@@ -396,7 +403,7 @@
                     row_ref[:, lanes(k, z)] = rows_3(part, part)
 
 
-def plane_kernel(own_ref, g3, g2, g1, row_ref, out_ref, row_tail_ref, col_tail_ref, lowest_ref):
+def plane_kernel(own_ref, g1, g2, g3, row_ref, out_ref, row_tail_ref, col_tail_ref, lowest_ref):
     got = (own_ref, g1, g2, g3)
     for x in range(SIDE):
         for y in range(SIDE):
@@ -453,7 +460,7 @@
 
 
 def grad_kernel(piece, own_ref, other_ref, low_ref, high_ref, row_ref, col_ref, lowest_ref, *refs):
-    *tail, g_ref, out_ref, block_ref = refs
+    ep_low, eq_low, ep_high, eq_high, *tail, g_ref, out_ref, block_ref = refs
     txt_refs = (low_ref, high_ref)
     columns = g_ref.shape[1]
     width = own_ref.shape[1] // 2
@@ -475,11 +482,12 @@
         col = jnp.exp2(SHIFT - 1.0 - stats)
 
         def step(n, _):
-            load_block(n, own_ref, other_ref, block_ref)
+            span = pl.ds(pl.multiple_of(n * BLOCK, BLOCK), BLOCK)
             rp, rq = turned(n, lambda x: jnp.exp2(SHIFT - 1.0 - x))
-            p, q = logits(block_ref[...], txt_refs)
-            g = jnp.exp2(q - SHIFT) * (rq + col[1:2, :]) - jnp.exp2(p - SHIFT) * (rp + col[0:1, :])
-            g_ref[pl.ds(pl.multiple_of(n * BLOCK, BLOCK), BLOCK), :] = g.astype(BF16)
+            ep = jnp.concatenate([ep_low[span, :], ep_high[span, :]], axis=1)
+            eq = jnp.concatenate([eq_low[span, :], eq_high[span, :]], axis=1)
+            g = eq * (rq + col[1:2, :]) - ep * (rp + col[0:1, :])
+            g_ref[span, :] = g.astype(BF16)
             return 0
 
         lax.fori_loop(0, blocks, step, 0, unroll=True)
@@ -505,7 +513,7 @@
         out_ref[columns:, :] = tail[0][...]
 
 
-def tile_grad(own, other, txt, stats, piece):
+def tile_grad(own, other, txt, tiles, stats, piece):
     row, col, row_tail, _, lowest = stats
     rows = own.shape[0] + other.shape[0]
     columns, width = 2 * txt[0].shape[0], own.shape[1]
@@ -514,8 +522,8 @@
     return call(
         lambda *refs: grad_kernel(piece, *refs),
         (shape((rows, columns), BF16), out),
-        (own, other, *txt, row, col, lowest) + ((row_tail,) if piece else ()),
-        3 * rows * columns * width,
+        (own, other, *txt, row, col, lowest, *tiles) + ((row_tail,) if piece else ()),
+        0,
         scratch=[pltpu.VMEM((BLOCK, width), BF16)],
     )
 
@@ -549,37 +557,27 @@
 
 
 def own_images_kernel(*refs):
-    out_ref = refs[-5]
+    out_ref = refs[-1]
 
     def store(span, value):
         out_ref[span, :] = value
 
     image_rows(0, out_ref.shape[0], refs[:SIDE], refs[SIDE : 3 * SIDE], store)
-    combine_kernel(*refs[3 * SIDE : -5], *refs[-4:])
-
-
-def image_grads(grads, txts, stats, own, got):
+
+
+def image_grads(grads, txts, tail):
     rows, columns = grads[0].shape
     txts = [half for piece in txts for half in piece]
     width = txts[0].shape[1] // 2
     half = rows // 2
     shape = jax.ShapeDtypeStruct
-    flops = half * columns * SIDE * width * 2
-    message = call(other_images_kernel, shape((half + TAIL, width), BF16), (*grads, *txts, stats[3]), flops)
-    step = own.shape[0] // SIDE
-    out = shape((step + TAIL, width), BF16)
-    own_img, *texts = call(
-        own_images_kernel,
-        (shape((half, width), F32), shape((step + 8, width), F32), out, out, out),
-        (*grads, *txts, own, stats[2], *got),
-        flops,
-    )
-    return message, own_img, texts
-
-
-def combine_kernel(own_ref, tail_ref, *refs):
-    count = len(refs) - SIDE
-    got, outs = refs[:count], refs[count:]
+    flops = 0
+    message = call(other_images_kernel, shape((half + TAIL, width), BF16), (*grads, *txts, tail), flops)
+    return message, call(own_images_kernel, shape((half, width), F32), (*grads, *txts), flops)
+
+
+def combine_kernel(count, own_ref, tail_ref, *refs):
+    got, outs = refs[:count], refs[-SIDE:]
     size = own_ref.shape[0]
     step = size // SIDE
     value = get_tail(tail_ref, 0) + sum(get_tail(ref, size) for ref in got)
@@ -595,12 +593,17 @@
             ref[step:, :] = jnp.broadcast_to(value, (8, value.shape[1]))
 
 
-def combine(own, tail, got):
+def combine(own, tail, got, after=()):
     size, width = own.shape
     step = size // SIDE
     message = jax.ShapeDtypeStruct((step + TAIL, width), BF16)
     keep = jax.ShapeDtypeStruct((step + 8, width), F32)
-    return call(combine_kernel, (keep, message, message, message), (own, tail, *got))
+    return call(
+        lambda *refs: combine_kernel(len(got), *refs),
+        (keep, message, message, message),
+        (own, tail, *got, *after),
+        hbm=-len(after),
+    )
 
 
 def tangent(x_ref, keep_ref, got, grad_ref):
@@ -642,18 +645,20 @@
     (own,) = lay_end([[img, img_1, send(img, along_z(2)), img_3]], (low_1, low_3, high_1, high_3))
     other = send(own, other_core())
 
-    row, near_col = tile_stats(own, other, (low, high, low_1, low_3, high_1, high_3), None)
-    row, far_col = tile_stats(own, other, (low_2, high_2), row)
+    row, near_col, near = tile_stats(own, other, (low, high, low_1, low_3, high_1, high_3), None)
+    row, far_col, far = tile_stats(own, other, (low_2, high_2), row)
+    tiles = [near[0] + near[1], near[2] + near[4], far[0] + far[1], near[3] + near[5]]
     stats = exchange(row, (near_col, far_col))
 
     grads, got = [None] * SIDE, []
     for b in (2, 1, 3):
-        grads[b], message = tile_grad(own, other, txt_all[b], stats, b)
+        grads[b], message = tile_grad(own, other, txt_all[b], tiles[b], stats, b)
         got.append(send(message, second(b)))
-    grads[0], own_txt = tile_grad(own, other, txt_all[0], stats, 0)
-    message, own_img, (keep_txt, *messages_txt) = image_grads(grads, txt_all, stats, own_txt, got)
+    grads[0], own_txt = tile_grad(own, other, txt_all[0], tiles[0], stats, 0)
+    message, own_img = image_grads(grads, txt_all, stats[3])
     keep, *messages = combine(own_img, stats[3], [send(message, other_core())])
     image = [image_student, keep] + [send(messages[e - 1], along_z(e)) for e in (3, 2, 1)]
+    keep_txt, *messages_txt = combine(own_txt, stats[2], got, image[2:3])
     text = [text_student, keep_txt] + [send(messages_txt[e - 1], first(e)) for e in (3, 2, 1)]
     pairs = rows * lax.axis_size("row") * lax.axis_size("col")
     grad_image, grad_text, mean_loss = finish(image, text, 0.5 / (LOG2E * pairs))

time: 108 us -> 107 us (level)
  waiting for transfers between devices: 40 us -> 47.9 us
  starting transfers between devices: 40.6 us -> 35.4 us
  Pallas kernels: 26.6 us -> 22.3 us
    ppermute x31, waiting for transfers between devices: 40 us -> 47.9 us  [send(): return lax.ppermute(x, AXES, pairs)]
    ppermute x31, starting transfers between devices: 40.6 us -> 35.4 us  [send(): return lax.ppermute(x, AXES, pairs)]
    pallas_call x19 -> x20, Pallas kernels: 26.6 us -> 22.3 us  [call(): pl.pallas_call(kernel, out_shape=out_shape, in_specs=[pl.BlockSpec(memory...]
  transfers between devices with their start and end apart: 31 -> 31, of which waited for: 24 -> 22; matrix products, arithmetic and copies ran while one was open for 0% -> 0% of each run, Pallas kernels for 16% -> 8%
where the time goes in v2:
time: 107 us
  waiting for transfers between devices  47.9 us (45%)
  starting transfers between devices  35.4 us (33%)
  Pallas kernels  22.3 us (21%)
    ppermute x31, waiting for transfers between devices, send(): return lax.ppermute(x, AXES, pairs)  47.9 us
    ppermute x31, starting transfers between devices, send(): return lax.ppermute(x, AXES, pairs)  35.4 us
    pallas_call x20, Pallas kernels, call(): pl.pallas_call(kernel, out_shape=out_shape, in_specs=[pl.BlockSpec(memory...  22.3 us
  transfers between devices with their start and end apart: 31, of which 22 were waited for; matrix products, arithmetic and copies ran while one was open for 0% of the time, Pallas kernels for 8%

profile of v2, /device:TPU:0, one launch (start us, length us, event | category | flops | bytes accessed | tf_op | source)
XLA Modules:
  0.0 106.6 jit_solution(11033560310094352295)
XLA Ops:
  0.7 2.8 %shard_map.76.refs_0_ = bf16[128,1024]{1,0:T(8,128)(2,1)} custom-call(bf16[128,512]{1,0:T(8,128)(2,1)} %refs_5_.1, bf16[128,1280]{1,0:T(8,128)(2,1)} %teacher_hbm.1, bf16[1280,512]{1,0:T(8,128)(2,1)} %sketch_ref.1), custom_call_target="tpu_custom_call" | custom-call | flops 167772160 | bytes 2031616 | tf_op jit(solution)/shard_map/pallas_call | solution.py:80
  3.4 1.7 %collective-permute-start = (bf16[128,1024]{1,0:T(8,128)(2,1)}, bf16[128,1024]{1,0:T(8,128)(2,1)S(1)}, u32[]{:S(2)}, u32[]{:S(2)}) collective-permute-start(bf16[128,1024]{1,0:T(8,128)(2,1)} %shard_map.76.refs_0_), channel_id=1, source_target_pairs={{0,32},{1,9},{2,34},{3,11},{4,36},{5,13},{6,38},{7,15},{8,40},{9,1... | collective-permute-start | bytes 786440 | tf_op jit(solution)/shard_map/ppermute | solution.py:57
  5.1 2.1 %collective-permute-start.5 = (bf16[128,1024]{1,0:T(8,128)(2,1)}, bf16[128,1024]{1,0:T(8,128)(2,1)S(1)}, u32[]{:S(2)}, u32[]{:S(2)}) collective-permute-start(bf16[128,1024]{1,0:T(8,128)(2,1)} %shard_map.76.refs_0_), channel_id=1, source_target_pairs={{0,96},{1,25},{2,98},{3,27},{4,100},{5,29},{6,102},{7,31},{8,104},... | collective-permute-start | bytes 786440 | tf_op jit(solution)/shard_map/ppermute | solution.py:57
  7.8 2.3 %collective-permute-done.refs_0_.refs_1_ = bf16[128,1024]{1,0:T(8,128)(2,1)S(1)} collective-permute-done((bf16[128,1024]{1,0:T(8,128)(2,1)}, bf16[128,1024]{1,0:T(8,128)(2,1)S(1)}, u32[]{:S(2)}, u32[]{:S(2)}) %collective-permute-start) | collective-permute-done | bytes 262176 | tf_op jit(solution)/shard_map/ppermute | solution.py:57
  10.6 4.2 %collective-permute-start.3 = (bf16[128,1024]{1,0:T(8,128)(2,1)S(1)}, bf16[128,1024]{1,0:T(8,128)(2,1)S(1)}, u32[]{:S(2)}, u32[]{:S(2)}) collective-permute-start(bf16[128,1024]{1,0:T(8,128)(2,1)S(1)} %shard_map.77.refs_0_), channel_id=1, source_target_pairs={{0,6},{1,7},{2,4},{3,5},{4,2},{5,3},{6,0},{7,1},{8,14},{9,15},{10,... | collective-permute-start | bytes 786440 | tf_op jit(solution)/shard_map/ppermute | solution.py:57
  14.8 0.9 collective-permute-done.5.refs_3_
  15.7 4.5 %collective-permute-done.3.refs_5_.refs_3_ = bf16[128,1024]{1,0:T(8,128)(2,1)S(1)} collective-permute-done((bf16[128,1024]{1,0:T(8,128)(2,1)S(1)}, bf16[128,1024]{1,0:T(8,128)(2,1)S(1)}, u32[]{:S(2)}, u32[]{:S(2)}) %collective-permute-start.3) | collective-permute-done | bytes 262176 | tf_op jit(solution)/shard_map/ppermute | solution.py:57
  20.2 1.5 %collective-permute-done.1.refs_4_.refs_1_ = bf16[128,1024]{1,0:T(8,128)(2,1)S(1)} collective-permute-done((bf16[128,1024]{1,0:T(8,128)(2,1)S(1)}, bf16[128,1024]{1,0:T(8,128)(2,1)S(1)}, u32[]{:S(2)}, u32[]{:S(2)}) %collective-permute-start.1) | collective-permute-done | bytes 262176 | tf_op jit(solution)/shard_map/ppermute | solution.py:57
  21.8 3.1 %collective-permute-start.7 = (bf16[256,1024]{1,0:T(8,128)(2,1)S(1)}, bf16[256,1024]{1,0:T(8,128)(2,1)S(1)}, u32[]{:S(2)}, u32[]{:S(2)}) collective-permute-start(bf16[256,1024]{1,0:T(8,128)(2,1)S(1)} %get-tuple-element.50.refs_2_.refs_4_), channel_id=1, source_target_pairs={{0,24},{1,97},{2,26},{3,99},{4,28},{5,101},{6,30},{7,103},{8,16},{... | collective-permute-start | bytes 1572872 | tf_op jit(solution)/shard_map/ppermute | solution.py:57
  25.0 1.1 collective-permute-start.9
  26.0 0.8 collective-permute-start.8
  27.1 7.7 %collective-permute-done.2.refs_2_ = bf16[128,1024]{1,0:T(8,128)(2,1)S(1)} collective-permute-done((bf16[128,1024]{1,0:T(8,128)(2,1)S(1)}, bf16[128,1024]{1,0:T(8,128)(2,1)S(1)}, u32[]{:S(2)}, u32[]{:S(2)}) %collective-permute-start.2) | collective-permute-done | bytes 262176 | tf_op jit(solution)/shard_map/ppermute | solution.py:57
  34.8 3.1 %collective-permute-done.9.refs_7_.refs_3_.refs_11_ = bf16[256,1024]{1,0:T(8,128)(2,1)S(1)} collective-permute-done((bf16[256,1024]{1,0:T(8,128)(2,1)S(1)}, bf16[256,1024]{1,0:T(8,128)(2,1)S(1)}, u32[]{:S(2)}, u32[]{:S(2)}) %collective-permute-start.9) | collective-permute-done | bytes 524320 | tf_op jit(solution)/shard_map/ppermute | solution.py:57
  37.8 1.8 %collective-permute-done.8.refs_6_.refs_3_.refs_7_ = bf16[256,1024]{1,0:T(8,128)(2,1)S(1)} collective-permute-done((bf16[256,1024]{1,0:T(8,128)(2,1)S(1)}, bf16[256,1024]{1,0:T(8,128)(2,1)S(1)}, u32[]{:S(2)}, u32[]{:S(2)}) %collective-permute-start.8) | collective-permute-done | bytes 524320 | tf_op jit(solution)/shard_map/ppermute | solution.py:57
  40.0 1.2 %collective-permute-start.12 = (bf16[256,1024]{1,0:T(8,128)(2,1)S(1)}, bf16[256,1024]{1,0:T(8,128)(2,1)S(1)}, u32[]{:S(2)}, u32[]{:S(2)}) collective-permute-start(bf16[256,1024]{1,0:T(8,128)(2,1)S(1)} %collective-permute-done.8.refs_6_.refs_3_.refs_7_), channel_id=1, source_target_pairs={{0,24},{1,97},{2,26},{3,99},{4,28},{5,101},{6,30},{7,103},{8,16},{... | collective-permute-start | bytes 1572872 | tf_op jit(solution)/shard_map/ppermute | solution.py:57
  41.2 1.3 %collective-permute-done.10.refs_1_ = bf16[512,1024]{1,0:T(8,128)(2,1)S(1)} collective-permute-done((bf16[512,1024]{1,0:T(8,128)(2,1)S(1)}, bf16[512,1024]{1,0:T(8,128)(2,1)S(1)}, u32[]{:S(2)}, u32[]{:S(2)}) %collective-permute-start.10) | collective-permute-done | bytes 1048608 | tf_op jit(solution)/shard_map/ppermute | solution.py:57
  42.5 6.5 %shard_map.80 = (f32[8,1024]{1,0:T(8,128)S(1)}, f32[8,1536]{1,0:T(8,128)S(1)}, f32[1024,256]{1,0:T(8,128)S(1)}, f32[1024,256]{1,0:T(8,128)S(1)}, f32[1024,256]{1...) custom-call(bf16[512,1024]{1,0:T(8,128)(2,1)S(1)} %shard_map.79.refs, ...), custom_call_target="tpu_custom_call" | custom-call | flops 3221225472 | bytes 17907712 | tf_op jit(solution)/shard_map/pallas_call | solution.py:80
  49.1 1.3 %collective-permute-done.12.refs_3_.refs_9_ = bf16[256,1024]{1,0:T(8,128)(2,1)S(1)} collective-permute-done((bf16[256,1024]{1,0:T(8,128)(2,1)S(1)}, bf16[256,1024]{1,0:T(8,128)(2,1)S(1)}, u32[]{:S(2)}, u32[]{:S(2)}) %collective-permute-start.12) | collective-permute-done | bytes 524320 | tf_op jit(solution)/shard_map/ppermute | solution.py:57
  50.4 2.0 %shard_map.81 = (f32[8,1024]{1,0:T(8,128)S(1)}, f32[8,512]{1,0:T(8,128)S(1)}, f32[1024,256]{1,0:T(8,128)S(1)}, f32[1024,256]{1,0:T(8,128)S(1)}, f32[1024,256]{1,0:T(8,128)S(1)}, /*index=5*/f32[1024,256]{1,0:T(8,128)S(1)}) custom-call(bf16[512,1024]{1,0:T(8,128)(2,1)S(1)} %shard_map.79.refs_0_, bf16[512,1024]{1,0:T(8,128)(2,1)S(1)} %collective-permute-done.10.refs_1_, ...), custom_call_target="tpu_custom_call" | custom-call | flops 1073741824 | bytes 7421952 | tf_op jit(solution)/shard_map/pallas_call | solution.py:80
  52.9 0.9 collective-permute-done.13.got_ref
  53.9 2.8 %collective-permute-start.16 = (f32[8,2048]{1,0:T(8,128)S(1)}, f32[8,2048]{1,0:T(8,128)S(1)}, u32[]{:S(2)}, u32[]{:S(2)}) collective-permute-start(f32[8,2048]{1,0:T(8,128)S(1)} %shard_map.83.own_ref), channel_id=1, source_target_pairs={{0,96},{1,7},{2,98},{3,5},{4,100},{5,3},{6,102},{7,1},{8,104},{9,1... | collective-permute-start | bytes 196616 | tf_op jit(solution)/shard_map/ppermute | solution.py:57
  56.7 0.8 collective-permute-start.15
  58.0 1.4 %collective-permute-done.16.g3 = f32[8,2048]{1,0:T(8,128)S(1)} collective-permute-done((f32[8,2048]{1,0:T(8,128)S(1)}, f32[8,2048]{1,0:T(8,128)S(1)}, u32[]{:S(2)}, u32[]{:S(2)}) %collective-permute-start.16) | collective-permute-done | bytes 65568 | tf_op jit(solution)/shard_map/ppermute | solution.py:57
  59.4 3.1 %collective-permute-done.15.g2 = f32[8,2048]{1,0:T(8,128)S(1)} collective-permute-done((f32[8,2048]{1,0:T(8,128)S(1)}, f32[8,2048]{1,0:T(8,128)S(1)}, u32[]{:S(2)}, u32[]{:S(2)}) %collective-permute-start.15) | collective-permute-done | bytes 65568 | tf_op jit(solution)/shard_map/ppermute | solution.py:57
  62.7 1.2 %collective-permute-done.17.got_ref = f32[8,2048]{1,0:T(8,128)S(1)} collective-permute-done((f32[8,2048]{1,0:T(8,128)S(1)}, f32[8,2048]{1,0:T(8,128)S(1)}, u32[]{:S(2)}, u32[]{:S(2)}) %collective-permute-start.17) | collective-permute-done | bytes 65568 | tf_op jit(solution)/shard_map/ppermute | solution.py:57
  64.1 1.3 %collective-permute-start.20 = (f32[8,2048]{1,0:T(8,128)S(1)}, f32[8,2048]{1,0:T(8,128)S(1)}, u32[]{:S(2)}, u32[]{:S(2)}) collective-permute-start(f32[8,2048]{1,0:T(8,128)S(1)} %get-tuple-element.57.own_ref), channel_id=1, source_target_pairs={{0,24},{1,25},{2,26},{3,27},{4,28},{5,29},{6,30},{7,31},{8,16},{9,... | collective-permute-start | bytes 196616 | tf_op jit(solution)/shard_map/ppermute | solution.py:57
  65.4 1.6 %collective-permute-start.19 = (f32[8,2048]{1,0:T(8,128)S(1)}, f32[8,2048]{1,0:T(8,128)S(1)}, u32[]{:S(2)}, u32[]{:S(2)}) collective-permute-start(f32[8,2048]{1,0:T(8,128)S(1)} %get-tuple-element.57.own_ref), channel_id=1, source_target_pairs={{0,16},{1,17},{2,18},{3,19},{4,20},{5,21},{6,22},{7,23},{8,24},{9,... | collective-permute-start | bytes 196616 | tf_op jit(solution)/shard_map/ppermute | solution.py:57
  66.9 1.4 %collective-permute-start.18 = (f32[8,2048]{1,0:T(8,128)S(1)}, f32[8,2048]{1,0:T(8,128)S(1)}, u32[]{:S(2)}, u32[]{:S(2)}) collective-permute-start(f32[8,2048]{1,0:T(8,128)S(1)} %get-tuple-element.57.own_ref), channel_id=1, source_target_pairs={{0,8},{1,9},{2,10},{3,11},{4,12},{5,13},{6,14},{7,15},{8,0},{9,1},... | collective-permute-start | bytes 196616 | tf_op jit(solution)/shard_map/ppermute | solution.py:57
  68.3 2.1 %collective-permute-done.20.g3 = f32[8,2048]{1,0:T(8,128)S(1)} collective-permute-done((f32[8,2048]{1,0:T(8,128)S(1)}, f32[8,2048]{1,0:T(8,128)S(1)}, u32[]{:S(2)}, u32[]{:S(2)}) %collective-permute-start.20) | collective-permute-done | bytes 65568 | tf_op jit(solution)/shard_map/ppermute | solution.py:57
  70.4 0.9 collective-permute-done.19.g2
  71.8 1.4 %shard_map.90 = (bf16[1024,512]{1,0:T(8,128)(2,1)S(1)}, bf16[528,512]{1,0:T(8,128)(2,1)S(1)}) custom-call(bf16[512,1024]{1,0:T(8,128)(2,1)S(1)} %shard_map.79.refs_0_, bf16[512,1024]{1,0:T(8,128)(2,1)S(1)} %collective-permute-done.10.refs_1_, bf16[256,1024]{1,0:T(8,128)(2,1)S(1)} %collective-permute-done.7.refs_5_.refs_2_.refs_10_, ...), custom_call_target="tpu_custom_call" | custom-call | tf_op jit(solution)/shard_map/pallas_call | solution.py:80
  73.3 1.4 %shard_map.89 = (bf16[1024,512]{1,0:T(8,128)(2,1)S(1)}, bf16[528,512]{1,0:T(8,128)(2,1)S(1)}) custom-call(bf16[512,1024]{1,0:T(8,128)(2,1)S(1)} %shard_map.79.refs_0_, bf16[512,1024]{1,0:T(8,128)(2,1)S(1)} %collective-permute-done.10.refs_1_, bf16[256,1024]{1,0:T(8,128)(2,1)S(1)} %collective-permute-done.11.refs_2_.refs_8_, ...), custom_call_target="tpu_custom_call" | custom-call | tf_op jit(solution)/shard_map/pallas_call | solution.py:80
  74.7 1.4 %shard_map.88 = (bf16[1024,512]{1,0:T(8,128)(2,1)S(1)}, bf16[528,512]{1,0:T(8,128)(2,1)S(1)}) custom-call(bf16[512,1024]{1,0:T(8,128)(2,1)S(1)} %shard_map.79.refs_0_, bf16[512,1024]{1,0:T(8,128)(2,1)S(1)} %collective-permute-done.10.refs_1_, bf16[256,1024]{1,0:T(8,128)(2,1)S(1)} %collective-permute-done.6.refs_4_.refs_2_.refs_6_, ...), custom_call_target="tpu_custom_call" | custom-call | tf_op jit(solution)/shard_map/pallas_call | solution.py:80
  76.1 1.4 %shard_map.87 = (bf16[1024,512]{1,0:T(8,128)(2,1)S(1)}, f32[512,512]{1,0:T(8,128)S(1)}) custom-call(bf16[512,1024]{1,0:T(8,128)(2,1)S(1)} %shard_map.79.refs_0_, bf16[512,1024]{1,0:T(8,128)(2,1)S(1)} %collective-permute-done.10.refs_1_, bf16[256,1024]{1,0:T(8,128)(2,1)S(1)} %get-tuple-element.50.refs_2_.refs_4_, ...), custom_call_target="tpu_custom_call" | custom-call | tf_op jit(solution)/shard_map/pallas_call | solution.py:80
  77.5 1.2 %shard_map.92 = bf16[528,512]{1,0:T(8,128)(2,1)S(1)} custom-call(bf16[1024,512]{1,0:T(8,128)(2,1)S(1)} %get-tuple-element.64.refs_0_, bf16[1024,512]{1,0:T(8,128)(2,1)S(1)} %get-tuple-element.70.refs_1_, bf16[1024,512]{1,0:T(8,128)(2,1)S(1)} %get-tuple-element.75.refs_2_, bf16[1024,512]{1,0:T(8,128)(2,1)S(1)} %get-tuple-element.80.refs_3_, ...), custom_call_target="tpu_custom_call" | custom-call | tf_op jit(solution)/shard_map/pallas_call | solution.py:80
  78.8 2.1 %collective-permute-start.27 = (bf16[528,512]{1,0:T(8,128)(2,1)S(1)}, bf16[528,512]{1,0:T(8,128)(2,1)S(1)}, u32[]{:S(2)}, u32[]{:S(2)}) collective-permute-start(bf16[528,512]{1,0:T(8,128)(2,1)S(1)} %get-tuple-element.89), channel_id=1, source_target_pairs={{0,24},{1,97},{2,26},{3,99},{4,28},{5,101},{6,30},{7,103},{8,16},{... | collective-permute-start | bytes 1622024 | tf_op jit(solution)/shard_map/ppermute | solution.py:57
  80.9 1.3 %collective-permute-start.25 = (bf16[528,512]{1,0:T(8,128)(2,1)S(1)}, bf16[528,512]{1,0:T(8,128)(2,1)S(1)}, u32[]{:S(2)}, u32[]{:S(2)}) collective-permute-start(bf16[528,512]{1,0:T(8,128)(2,1)S(1)} %get-tuple-element.87), channel_id=1, source_target_pairs={{0,16},{1,65},{2,18},{3,67},{4,20},{5,69},{6,22},{7,71},{8,24},{9,... | collective-permute-start | bytes 1622024 | tf_op jit(solution)/shard_map/ppermute | solution.py:57
  82.2 0.8 collective-permute-start.26
  83.0 1.2 %shard_map.91.refs_0_ = f32[512,512]{1,0:T(8,128)S(1)} custom-call(bf16[1024,512]{1,0:T(8,128)(2,1)S(1)} %get-tuple-element.64.refs_0_, bf16[1024,512]{1,0:T(8,128)(2,1)S(1)} %get-tuple-element.70.refs_1_, bf16[1024,512]{1,0:T(8,128)(2,1)S(1)} %get-tuple-element.75.refs_2_, bf16[1024,512]{1,0:T(8,128)(2,1)S(1)} %get-tuple-element.80.refs_3_, ...), custom_call_target="tpu_custom_call" | custom-call | tf_op jit(solution)/shard_map/pallas_call | solution.py:80
  84.4 1.6 %collective-permute-start.22 = (bf16[144,512]{1,0:T(8,128)(2,1)S(1)}, bf16[144,512]{1,0:T(8,128)(2,1)S(1)}, u32[]{:S(2)}, u32[]{:S(2)}) collective-permute-start(bf16[144,512]{1,0:T(8,128)(2,1)S(1)} %get-tuple-element.83), channel_id=1, source_target_pairs={{0,6},{1,7},{2,4},{3,5},{4,2},{5,3},{6,0},{7,1},{8,14},{9,15},{10,... | collective-permute-start | bytes 442376 | tf_op jit(solution)/shard_map/ppermute | solution.py:57
  86.0 0.9 collective-permute-start.23
  86.8 8.5 %collective-permute-done.27.refs_4_ = bf16[528,512]{1,0:T(8,128)(2,1)S(1)} collective-permute-done((bf16[528,512]{1,0:T(8,128)(2,1)S(1)}, bf16[528,512]{1,0:T(8,128)(2,1)S(1)}, u32[]{:S(2)}, u32[]{:S(2)}) %collective-permute-start.27) | collective-permute-done | bytes 540704 | tf_op jit(solution)/shard_map/ppermute | solution.py:57
  96.5 1.5 %collective-permute-start.28 = (bf16[144,512]{1,0:T(8,128)(2,1)S(1)}, bf16[144,512]{1,0:T(8,128)(2,1)S(1)}, u32[]{:S(2)}, u32[]{:S(2)}) collective-permute-start(bf16[144,512]{1,0:T(8,128)(2,1)S(1)} %get-tuple-element.91), channel_id=1, source_target_pairs={{0,96},{1,25},{2,98},{3,27},{4,100},{5,29},{6,102},{7,31},{8,104},... | collective-permute-start | bytes 442376 | tf_op jit(solution)/shard_map/ppermute | solution.py:57
  97.9 0.9 collective-permute-start.29
  98.8 1.8 %collective-permute-start.30 = (bf16[144,512]{1,0:T(8,128)(2,1)S(1)}, bf16[144,512]{1,0:T(8,128)(2,1)S(1)}, u32[]{:S(2)}, u32[]{:S(2)}) collective-permute-start(bf16[144,512]{1,0:T(8,128)(2,1)S(1)} %get-tuple-element.93), channel_id=1, source_target_pairs={{0,32},{1,9},{2,34},{3,11},{4,36},{5,13},{6,38},{7,15},{8,40},{9,1... | collective-permute-start | bytes 442376 | tf_op jit(solution)/shard_map/ppermute | solution.py:57
  100.6 2.3 %collective-permute-done.28.refs_7_ = bf16[144,512]{1,0:T(8,128)(2,1)S(1)} collective-permute-done((bf16[144,512]{1,0:T(8,128)(2,1)S(1)}, bf16[144,512]{1,0:T(8,128)(2,1)S(1)}, u32[]{:S(2)}, u32[]{:S(2)}) %collective-permute-start.28) | collective-permute-done | bytes 147488 | tf_op jit(solution)/shard_map/ppermute | solution.py:57
  102.9 1.7 %collective-permute-done.29.refs_8_ = bf16[144,512]{1,0:T(8,128)(2,1)S(1)} collective-permute-done((bf16[144,512]{1,0:T(8,128)(2,1)S(1)}, bf16[144,512]{1,0:T(8,128)(2,1)S(1)}, u32[]{:S(2)}, u32[]{:S(2)}) %collective-permute-start.29) | collective-permute-done | bytes 147488 | tf_op jit(solution)/shard_map/ppermute | solution.py:57
  105.3 1.1 %shard_map.95 = (f32[128,512]{1,0:T(8,128)}, f32[128,512]{1,0:T(8,128)}, f32[1,1]{1,0:T(1,128)}) custom-call(bf16[128,512]{1,0:T(8,128)(2,1)S(1)} %copy-done.2, f32[136,512]{1,0:T(8,128)S(1)} %get-tuple-element.82.refs_1_, bf16[144,512]{1,0:T(8,128)(2,1)S(1)} %collective-permute-done.22.refs_5_.refs_2_, ...), custom_call_target="tpu_custom_call" | custom-call | tf_op jit(solution)/shard_map/pallas_call | solution.py:80
  (44 shorter events, 6.0 us)
Async XLA Ops:
  0.6 9.5 %copy-start = (bf16[1280,512]{1,0:T(8,128)(2,1)S(1)}, bf16[1280,512]{1,0:T(8,128)(2,1)}, u32[]{:S(2)}) copy-start(bf16[1280,512]{1,0:T(8,128)(2,1)} %sketch_ref.1) | copy-start | bytes 3932164
  0.6 9.5 %copy-start.2 = (bf16[128,512]{1,0:T(8,128)(2,1)S(1)}, bf16[128,512]{1,0:T(8,128)(2,1)}, u32[]{:S(2)}) copy-start(bf16[128,512]{1,0:T(8,128)(2,1)} %refs_0_.1) | copy-start | bytes 393220
  0.7 9.5 %copy-start.4 = (bf16[128,1280]{1,0:T(8,128)(2,1)S(1)}, bf16[128,1280]{1,0:T(8,128)(2,1)}, u32[]{:S(2)}) copy-start(bf16[128,1280]{1,0:T(8,128)(2,1)} %teacher_ref.1) | copy-start | bytes 983044
  3.4 18.2 %copy-start.1 = (bf16[128,1024]{1,0:T(8,128)(2,1)S(1)}, bf16[128,1024]{1,0:T(8,128)(2,1)}, u32[]{:S(2)}) copy-start(bf16[128,1024]{1,0:T(8,128)(2,1)} %shard_map.76.refs_0_) | copy-start | bytes 786436
  3.4 6.7 %collective-permute-start = (bf16[128,1024]{1,0:T(8,128)(2,1)}, bf16[128,1024]{1,0:T(8,128)(2,1)S(1)}, u32[]{:S(2)}, u32[]{:S(2)}) collective-permute-start(bf16[128,1024]{1,0:T(8,128)(2,1)} %shard_map.76.refs_0_), channel_id=1, source_target_pairs={{0,32},{1,9},{2,34},{3,11},{4,36},{5,13},{6,38},{7,15},{8,40},{9,1... | collective-permute-start | bytes 786440 | tf_op jit(solution)/shard_map/ppermute | solution.py:57
  5.1 10.6 %collective-permute-start.5 = (bf16[128,1024]{1,0:T(8,128)(2,1)}, bf16[128,1024]{1,0:T(8,128)(2,1)S(1)}, u32[]{:S(2)}, u32[]{:S(2)}) collective-permute-start(bf16[128,1024]{1,0:T(8,128)(2,1)} %shard_map.76.refs_0_), channel_id=1, source_target_pairs={{0,96},{1,25},{2,98},{3,27},{4,100},{5,29},{6,102},{7,31},{8,104},... | collective-permute-start | bytes 786440 | tf_op jit(solution)/shard_map/ppermute | solution.py:57
  7.2 8.5 %collective-permute-start.4 = (bf16[128,1024]{1,0:T(8,128)(2,1)}, bf16[128,1024]{1,0:T(8,128)(2,1)S(1)}, u32[]{:S(2)}, u32[]{:S(2)}) collective-permute-start(bf16[128,1024]{1,0:T(8,128)(2,1)} %shard_map.76.refs_0_), channel_id=1, source_target_pairs={{0,64},{1,17},{2,66},{3,19},{4,68},{5,21},{6,70},{7,23},{8,72},{9,... | collective-permute-start | bytes 786440 | tf_op jit(solution)/shard_map/ppermute | solution.py:57
  10.6 9.6 %collective-permute-start.3 = (bf16[128,1024]{1,0:T(8,128)(2,1)S(1)}, bf16[128,1024]{1,0:T(8,128)(2,1)S(1)}, u32[]{:S(2)}, u32[]{:S(2)}) collective-permute-start(bf16[128,1024]{1,0:T(8,128)(2,1)S(1)} %shard_map.77.refs_0_), channel_id=1, source_target_pairs={{0,6},{1,7},{2,4},{3,5},{4,2},{5,3},{6,0},{7,1},{8,14},{9,15},{10,... | collective-permute-start | bytes 786440 | tf_op jit(solution)/shard_map/ppermute | solution.py:57
  14.8 6.9 %collective-permute-start.1 = (bf16[128,1024]{1,0:T(8,128)(2,1)S(1)}, bf16[128,1024]{1,0:T(8,128)(2,1)S(1)}, u32[]{:S(2)}, u32[]{:S(2)}) collective-permute-start(bf16[128,1024]{1,0:T(8,128)(2,1)S(1)} %shard_map.77.refs_0_), channel_id=1, source_target_pairs={{0,2},{1,3},{2,0},{3,1},{4,6},{5,7},{6,4},{7,5},{8,10},{9,11},{10,... | collective-permute-start | bytes 786440 | tf_op jit(solution)/shard_map/ppermute | solution.py:57
  21.8 13.0 %collective-permute-start.7 = (bf16[256,1024]{1,0:T(8,128)(2,1)S(1)}, bf16[256,1024]{1,0:T(8,128)(2,1)S(1)}, u32[]{:S(2)}, u32[]{:S(2)}) collective-permute-start(bf16[256,1024]{1,0:T(8,128)(2,1)S(1)} %get-tuple-element.50.refs_2_.refs_4_), channel_id=1, source_target_pairs={{0,24},{1,97},{2,26},{3,99},{4,28},{5,101},{6,30},{7,103},{8,16},{... | collective-permute-start | bytes 1572872 | tf_op jit(solution)/shard_map/ppermute | solution.py:57
  24.8 9.9 %collective-permute-start.6 = (bf16[256,1024]{1,0:T(8,128)(2,1)S(1)}, bf16[256,1024]{1,0:T(8,128)(2,1)S(1)}, u32[]{:S(2)}, u32[]{:S(2)}) collective-permute-start(bf16[256,1024]{1,0:T(8,128)(2,1)S(1)} %get-tuple-element.50.refs_2_.refs_4_), channel_id=1, source_target_pairs={{0,8},{1,33},{2,10},{3,35},{4,12},{5,37},{6,14},{7,39},{8,0},{9,41... | collective-permute-start | bytes 1572872 | tf_op jit(solution)/shard_map/ppermute | solution.py:57
  25.0 12.9 %collective-permute-start.9 = (bf16[256,1024]{1,0:T(8,128)(2,1)S(1)}, bf16[256,1024]{1,0:T(8,128)(2,1)S(1)}, u32[]{:S(2)}, u32[]{:S(2)}) collective-permute-start(bf16[256,1024]{1,0:T(8,128)(2,1)S(1)} %get-tuple-element.51.refs_3_.refs_5_), channel_id=1, source_target_pairs={{0,24},{1,97},{2,26},{3,99},{4,28},{5,101},{6,30},{7,103},{8,16},{... | collective-permute-start | bytes 1572872 | tf_op jit(solution)/shard_map/ppermute | solution.py:57
  26.0 13.6 %collective-permute-start.8 = (bf16[256,1024]{1,0:T(8,128)(2,1)S(1)}, bf16[256,1024]{1,0:T(8,128)(2,1)S(1)}, u32[]{:S(2)}, u32[]{:S(2)}) collective-permute-start(bf16[256,1024]{1,0:T(8,128)(2,1)S(1)} %get-tuple-element.51.refs_3_.refs_5_), channel_id=1, source_target_pairs={{0,8},{1,33},{2,10},{3,35},{4,12},{5,37},{6,14},{7,39},{8,0},{9,41... | collective-permute-start | bytes 1572872 | tf_op jit(solution)/shard_map/ppermute | solution.py:57
  26.9 7.9 %collective-permute-start.2 = (bf16[128,1024]{1,0:T(8,128)(2,1)S(1)}, bf16[128,1024]{1,0:T(8,128)(2,1)S(1)}, u32[]{:S(2)}, u32[]{:S(2)}) collective-permute-start(bf16[128,1024]{1,0:T(8,128)(2,1)S(1)} %shard_map.77.refs_0_), channel_id=1, source_target_pairs={{0,4},{1,5},{2,6},{3,7},{4,0},{5,1},{6,2},{7,3},{8,12},{9,13},{10,... | collective-permute-start | bytes 786440 | tf_op jit(solution)/shard_map/ppermute | solution.py:57
  39.7 2.7 %collective-permute-start.10 = (bf16[512,1024]{1,0:T(8,128)(2,1)S(1)}, bf16[512,1024]{1,0:T(8,128)(2,1)S(1)}, u32[]{:S(2)}, u32[]{:S(2)}) collective-permute-start(bf16[512,1024]{1,0:T(8,128)(2,1)S(1)} %shard_map.79.refs_0_), channel_id=1, source_target_pairs={{0,1},{1,0},{2,3},{3,2},{4,5},{5,4},{6,7},{7,6},{8,9},{9,8},{10,11... | collective-permute-start | bytes 3145736 | tf_op jit(solution)/shard_map/ppermute | solution.py:57
  39.8 9.3 %collective-permute-start.11 = (bf16[256,1024]{1,0:T(8,128)(2,1)S(1)}, bf16[256,1024]{1,0:T(8,128)(2,1)S(1)}, u32[]{:S(2)}, u32[]{:S(2)}) collective-permute-start(bf16[256,1024]{1,0:T(8,128)(2,1)S(1)} %collective-permute-done.7.refs_5_.refs_2_.refs_10_), channel_id=1, source_target_pairs={{0,8},{1,33},{2,10},{3,35},{4,12},{5,37},{6,14},{7,39},{8,0},{9,41... | collective-permute-start | bytes 1572872 | tf_op jit(solution)/shard_map/ppermute | solution.py:57
  40.0 10.4 %collective-permute-start.12 = (bf16[256,1024]{1,0:T(8,128)(2,1)S(1)}, bf16[256,1024]{1,0:T(8,128)(2,1)S(1)}, u32[]{:S(2)}, u32[]{:S(2)}) collective-permute-start(bf16[256,1024]{1,0:T(8,128)(2,1)S(1)} %collective-permute-done.8.refs_6_.refs_3_.refs_7_), channel_id=1, source_target_pairs={{0,24},{1,97},{2,26},{3,99},{4,28},{5,101},{6,30},{7,103},{8,16},{... | collective-permute-start | bytes 1572872 | tf_op jit(solution)/shard_map/ppermute | solution.py:57
  52.5 1.3 %collective-permute-start.13 = (f32[8,2048]{1,0:T(8,128)S(1)}, f32[8,2048]{1,0:T(8,128)S(1)}, u32[]{:S(2)}, u32[]{:S(2)}) collective-permute-start(f32[8,2048]{1,0:T(8,128)S(1)} %shard_map.82.own_ref), channel_id=1, source_target_pairs={{0,1},{1,0},{2,3},{3,2},{4,5},{5,4},{6,7},{7,6},{8,9},{9,8},{10,11... | collective-permute-start | bytes 196616 | tf_op jit(solution)/shard_map/ppermute | solution.py:57
  53.9 5.6 %collective-permute-start.16 = (f32[8,2048]{1,0:T(8,128)S(1)}, f32[8,2048]{1,0:T(8,128)S(1)}, u32[]{:S(2)}, u32[]{:S(2)}) collective-permute-start(f32[8,2048]{1,0:T(8,128)S(1)} %shard_map.83.own_ref), channel_id=1, source_target_pairs={{0,96},{1,7},{2,98},{3,5},{4,100},{5,3},{6,102},{7,1},{8,104},{9,1... | collective-permute-start | bytes 196616 | tf_op jit(solution)/shard_map/ppermute | solution.py:57
  56.7 5.8 %collective-permute-start.15 = (f32[8,2048]{1,0:T(8,128)S(1)}, f32[8,2048]{1,0:T(8,128)S(1)}, u32[]{:S(2)}, u32[]{:S(2)}) collective-permute-start(f32[8,2048]{1,0:T(8,128)S(1)} %shard_map.83.own_ref), channel_id=1, source_target_pairs={{0,64},{1,5},{2,66},{3,7},{4,68},{5,1},{6,70},{7,3},{8,72},{9,13},... | collective-permute-start | bytes 196616 | tf_op jit(solution)/shard_map/ppermute | solution.py:57
  57.5 5.0 %collective-permute-start.14 = (f32[8,2048]{1,0:T(8,128)S(1)}, f32[8,2048]{1,0:T(8,128)S(1)}, u32[]{:S(2)}, u32[]{:S(2)}) collective-permute-start(f32[8,2048]{1,0:T(8,128)S(1)} %shard_map.83.own_ref), channel_id=1, source_target_pairs={{0,32},{1,3},{2,34},{3,1},{4,36},{5,7},{6,38},{7,5},{8,40},{9,11},... | collective-permute-start | bytes 196616 | tf_op jit(solution)/shard_map/ppermute | solution.py:57
  62.6 1.3 %collective-permute-start.17 = (f32[8,2048]{1,0:T(8,128)S(1)}, f32[8,2048]{1,0:T(8,128)S(1)}, u32[]{:S(2)}, u32[]{:S(2)}) collective-permute-start(f32[8,2048]{1,0:T(8,128)S(1)} %shard_map.84.own_ref), channel_id=1, source_target_pairs={{0,1},{1,0},{2,3},{3,2},{4,5},{5,4},{6,7},{7,6},{8,9},{9,8},{10,11... | collective-permute-start | bytes 196616 | tf_op jit(solution)/shard_map/ppermute | solution.py:57
  64.1 6.3 %collective-permute-start.20 = (f32[8,2048]{1,0:T(8,128)S(1)}, f32[8,2048]{1,0:T(8,128)S(1)}, u32[]{:S(2)}, u32[]{:S(2)}) collective-permute-start(f32[8,2048]{1,0:T(8,128)S(1)} %get-tuple-element.57.own_ref), channel_id=1, source_target_pairs={{0,24},{1,25},{2,26},{3,27},{4,28},{5,29},{6,30},{7,31},{8,16},{9,... | collective-permute-start | bytes 196616 | tf_op jit(solution)/shard_map/ppermute | solution.py:57
  65.4 5.9 %collective-permute-start.19 = (f32[8,2048]{1,0:T(8,128)S(1)}, f32[8,2048]{1,0:T(8,128)S(1)}, u32[]{:S(2)}, u32[]{:S(2)}) collective-permute-start(f32[8,2048]{1,0:T(8,128)S(1)} %get-tuple-element.57.own_ref), channel_id=1, source_target_pairs={{0,16},{1,17},{2,18},{3,19},{4,20},{5,21},{6,22},{7,23},{8,24},{9,... | collective-permute-start | bytes 196616 | tf_op jit(solution)/shard_map/ppermute | solution.py:57
  66.9 4.4 %collective-permute-start.18 = (f32[8,2048]{1,0:T(8,128)S(1)}, f32[8,2048]{1,0:T(8,128)S(1)}, u32[]{:S(2)}, u32[]{:S(2)}) collective-permute-start(f32[8,2048]{1,0:T(8,128)S(1)} %get-tuple-element.57.own_ref), channel_id=1, source_target_pairs={{0,8},{1,9},{2,10},{3,11},{4,12},{5,13},{6,14},{7,15},{8,0},{9,1},... | collective-permute-start | bytes 196616 | tf_op jit(solution)/shard_map/ppermute | solution.py:57
  78.8 5.5 %collective-permute-start.21 = (bf16[528,512]{1,0:T(8,128)(2,1)S(1)}, bf16[528,512]{1,0:T(8,128)(2,1)S(1)}, u32[]{:S(2)}, u32[]{:S(2)}) collective-permute-start(bf16[528,512]{1,0:T(8,128)(2,1)S(1)} %shard_map.92), channel_id=1, source_target_pairs={{0,1},{1,0},{2,3},{3,2},{4,5},{5,4},{6,7},{7,6},{8,9},{9,8},{10,11... | collective-permute-start | bytes 1622024 | tf_op jit(solution)/shard_map/ppermute | solution.py:57
  78.8 16.4 %collective-permute-start.27 = (bf16[528,512]{1,0:T(8,128)(2,1)S(1)}, bf16[528,512]{1,0:T(8,128)(2,1)S(1)}, u32[]{:S(2)}, u32[]{:S(2)}) collective-permute-start(bf16[528,512]{1,0:T(8,128)(2,1)S(1)} %get-tuple-element.89), channel_id=1, source_target_pairs={{0,24},{1,97},{2,26},{3,99},{4,28},{5,101},{6,30},{7,103},{8,16},{... | collective-permute-start | bytes 1622024 | tf_op jit(solution)/shard_map/ppermute | solution.py:57
  80.9 14.7 %collective-permute-start.25 = (bf16[528,512]{1,0:T(8,128)(2,1)S(1)}, bf16[528,512]{1,0:T(8,128)(2,1)S(1)}, u32[]{:S(2)}, u32[]{:S(2)}) collective-permute-start(bf16[528,512]{1,0:T(8,128)(2,1)S(1)} %get-tuple-element.87), channel_id=1, source_target_pairs={{0,16},{1,65},{2,18},{3,67},{4,20},{5,69},{6,22},{7,71},{8,24},{9,... | collective-permute-start | bytes 1622024 | tf_op jit(solution)/shard_map/ppermute | solution.py:57
  82.2 14.0 %collective-permute-start.26 = (bf16[528,512]{1,0:T(8,128)(2,1)S(1)}, bf16[528,512]{1,0:T(8,128)(2,1)S(1)}, u32[]{:S(2)}, u32[]{:S(2)}) collective-permute-start(bf16[528,512]{1,0:T(8,128)(2,1)S(1)} %get-tuple-element.88), channel_id=1, source_target_pairs={{0,8},{1,33},{2,10},{3,35},{4,12},{5,37},{6,14},{7,39},{8,0},{9,41... | collective-permute-start | bytes 1622024 | tf_op jit(solution)/shard_map/ppermute | solution.py:57
  84.4 11.8 %collective-permute-start.22 = (bf16[144,512]{1,0:T(8,128)(2,1)S(1)}, bf16[144,512]{1,0:T(8,128)(2,1)S(1)}, u32[]{:S(2)}, u32[]{:S(2)}) collective-permute-start(bf16[144,512]{1,0:T(8,128)(2,1)S(1)} %get-tuple-element.83), channel_id=1, source_target_pairs={{0,6},{1,7},{2,4},{3,5},{4,2},{5,3},{6,0},{7,1},{8,14},{9,15},{10,... | collective-permute-start | bytes 442376 | tf_op jit(solution)/shard_map/ppermute | solution.py:57
  86.0 14.7 %collective-permute-start.23 = (bf16[144,512]{1,0:T(8,128)(2,1)S(1)}, bf16[144,512]{1,0:T(8,128)(2,1)S(1)}, u32[]{:S(2)}, u32[]{:S(2)}) collective-permute-start(bf16[144,512]{1,0:T(8,128)(2,1)S(1)} %get-tuple-element.84), channel_id=1, source_target_pairs={{0,4},{1,5},{2,6},{3,7},{4,0},{5,1},{6,2},{7,3},{8,12},{9,13},{10,... | collective-permute-start | bytes 442376 | tf_op jit(solution)/shard_map/ppermute | solution.py:57
  95.3 5.3 %collective-permute-start.24 = (bf16[144,512]{1,0:T(8,128)(2,1)S(1)}, bf16[144,512]{1,0:T(8,128)(2,1)S(1)}, u32[]{:S(2)}, u32[]{:S(2)}) collective-permute-start(bf16[144,512]{1,0:T(8,128)(2,1)S(1)} %get-tuple-element.85), channel_id=1, source_target_pairs={{0,2},{1,3},{2,0},{3,1},{4,6},{5,7},{6,4},{7,5},{8,10},{9,11},{10,... | collective-permute-start | bytes 442376 | tf_op jit(solution)/shard_map/ppermute | solution.py:57
  96.2 9.1 %copy-start.3 = (bf16[128,512]{1,0:T(8,128)(2,1)S(1)}, bf16[128,512]{1,0:T(8,128)(2,1)}, u32[]{:S(2)}) copy-start(bf16[128,512]{1,0:T(8,128)(2,1)} %refs_5_.1) | copy-start | bytes 393220
  96.5 6.4 %collective-permute-start.28 = (bf16[144,512]{1,0:T(8,128)(2,1)S(1)}, bf16[144,512]{1,0:T(8,128)(2,1)S(1)}, u32[]{:S(2)}, u32[]{:S(2)}) collective-permute-start(bf16[144,512]{1,0:T(8,128)(2,1)S(1)} %get-tuple-element.91), channel_id=1, source_target_pairs={{0,96},{1,25},{2,98},{3,27},{4,100},{5,29},{6,102},{7,31},{8,104},... | collective-permute-start | bytes 442376 | tf_op jit(solution)/shard_map/ppermute | solution.py:57
  97.9 6.6 %collective-permute-start.29 = (bf16[144,512]{1,0:T(8,128)(2,1)S(1)}, bf16[144,512]{1,0:T(8,128)(2,1)S(1)}, u32[]{:S(2)}, u32[]{:S(2)}) collective-permute-start(bf16[144,512]{1,0:T(8,128)(2,1)S(1)} %get-tuple-element.92), channel_id=1, source_target_pairs={{0,64},{1,17},{2,66},{3,19},{4,68},{5,21},{6,70},{7,23},{8,72},{9,... | collective-permute-start | bytes 442376 | tf_op jit(solution)/shard_map/ppermute | solution.py:57
  98.8 6.5 %collective-permute-start.30 = (bf16[144,512]{1,0:T(8,128)(2,1)S(1)}, bf16[144,512]{1,0:T(8,128)(2,1)S(1)}, u32[]{:S(2)}, u32[]{:S(2)}) collective-permute-start(bf16[144,512]{1,0:T(8,128)(2,1)S(1)} %get-tuple-element.93), channel_id=1, source_target_pairs={{0,32},{1,9},{2,34},{3,11},{4,36},{5,13},{6,38},{7,15},{8,40},{9,1... | collective-permute-start | bytes 442376 | tf_op jit(solution)/shard_map/ppermute | solution.py:57

commit v3 on v2

--- a/solution.py
+++ b/solution.py
@@ -565,7 +565,7 @@
     image_rows(0, out_ref.shape[0], refs[:SIDE], refs[SIDE : 3 * SIDE], store)
 
 
-def image_grads(grads, txts, tail):
+def image_grads(grads, txts, tail, after):
     rows, columns = grads[0].shape
     txts = [half for piece in txts for half in piece]
     width = txts[0].shape[1] // 2
@@ -573,7 +573,8 @@
     shape = jax.ShapeDtypeStruct
     flops = 0
     message = call(other_images_kernel, shape((half + TAIL, width), BF16), (*grads, *txts, tail), flops)
-    return message, call(own_images_kernel, shape((half, width), F32), (*grads, *txts), flops)
+    own = call(own_images_kernel, shape((half, width), F32), (*grads, *txts, *after), flops, hbm=-len(after))
+    return message, own
 
 
 def combine_kernel(count, own_ref, tail_ref, *refs):
@@ -651,11 +652,11 @@
     stats = exchange(row, (near_col, far_col))
 
     grads, got = [None] * SIDE, []
-    for b in (2, 1, 3):
+    for b in (3, 1, 2):
         grads[b], message = tile_grad(own, other, txt_all[b], tiles[b], stats, b)
         got.append(send(message, second(b)))
     grads[0], own_txt = tile_grad(own, other, txt_all[0], tiles[0], stats, 0)
-    message, own_img = image_grads(grads, txt_all, stats[3])
+    message, own_img = image_grads(grads, txt_all, stats[3], got[:2])
     keep, *messages = combine(own_img, stats[3], [send(message, other_core())])
     image = [image_student, keep] + [send(messages[e - 1], along_z(e)) for e in (3, 2, 1)]
     keep_txt, *messages_txt = combine(own_txt, stats[2], got, image[2:3])

time: 107 us -> 105 us (0.981)
  waiting for transfers between devices: 47.9 us -> 43.4 us
  starting transfers between devices: 35.4 us -> 37.6 us
    ppermute x31, waiting for transfers between devices: 47.9 us -> 43.4 us  [send(): return lax.ppermute(x, AXES, pairs)]
    ppermute x31, starting transfers between devices: 35.4 us -> 37.6 us  [send(): return lax.ppermute(x, AXES, pairs)]
  transfers between devices with their start and end apart: 31 -> 31, of which waited for: 22 -> 24; matrix products, arithmetic and copies ran while one was open for 0% -> 0% of each run, Pallas kernels for 8% -> 13%
where the time goes in v3:
time: 105 us; the launch traced here: 104 us
  waiting for transfers between devices  43.4 us (41%)
  starting transfers between devices  37.6 us (36%)
  Pallas kernels  22.3 us (21%)
    ppermute x31, waiting for transfers between devices, send(): return lax.ppermute(x, AXES, pairs)  43.4 us
    ppermute x31, starting transfers between devices, send(): return lax.ppermute(x, AXES, pairs)  37.6 us
    pallas_call x20, Pallas kernels, call(): pl.pallas_call(kernel, out_shape=out_shape, in_specs=[pl.BlockSpec(memory...  22.3 us
  transfers between devices with their start and end apart: 31, of which 24 were waited for; matrix products, arithmetic and copies ran while one was open for 0% of the time, Pallas kernels for 13%

profile of v3, /device:TPU:0, one launch (start us, length us, event | category | flops | bytes accessed | tf_op | source)
XLA Modules:
  0.0 104.4 jit_solution(233679739059514864)
XLA Ops:
  0.7 2.8 %shard_map.76.refs_0_ = bf16[128,1024]{1,0:T(8,128)(2,1)} custom-call(bf16[128,512]{1,0:T(8,128)(2,1)} %refs_5_.1, bf16[128,1280]{1,0:T(8,128)(2,1)} %teacher_hbm.1, bf16[1280,512]{1,0:T(8,128)(2,1)} %sketch_ref.1), custom_call_target="tpu_custom_call" | custom-call | flops 167772160 | bytes 2031616 | tf_op jit(solution)/shard_map/pallas_call | solution.py:80
  3.4 1.7 %collective-permute-start = (bf16[128,1024]{1,0:T(8,128)(2,1)}, bf16[128,1024]{1,0:T(8,128)(2,1)S(1)}, u32[]{:S(2)}, u32[]{:S(2)}) collective-permute-start(bf16[128,1024]{1,0:T(8,128)(2,1)} %shard_map.76.refs_0_), channel_id=1, source_target_pairs={{0,32},{1,9},{2,34},{3,11},{4,36},{5,13},{6,38},{7,15},{8,40},{9,1... | collective-permute-start | bytes 786440 | tf_op jit(solution)/shard_map/ppermute | solution.py:57
  5.1 2.1 %collective-permute-start.5 = (bf16[128,1024]{1,0:T(8,128)(2,1)}, bf16[128,1024]{1,0:T(8,128)(2,1)S(1)}, u32[]{:S(2)}, u32[]{:S(2)}) collective-permute-start(bf16[128,1024]{1,0:T(8,128)(2,1)} %shard_map.76.refs_0_), channel_id=1, source_target_pairs={{0,96},{1,25},{2,98},{3,27},{4,100},{5,29},{6,102},{7,31},{8,104},... | collective-permute-start | bytes 786440 | tf_op jit(solution)/shard_map/ppermute | solution.py:57
  7.8 2.3 %collective-permute-done.refs_0_.refs_1_ = bf16[128,1024]{1,0:T(8,128)(2,1)S(1)} collective-permute-done((bf16[128,1024]{1,0:T(8,128)(2,1)}, bf16[128,1024]{1,0:T(8,128)(2,1)S(1)}, u32[]{:S(2)}, u32[]{:S(2)}) %collective-permute-start) | collective-permute-done | bytes 262176 | tf_op jit(solution)/shard_map/ppermute | solution.py:57
  10.6 4.2 %collective-permute-start.3 = (bf16[128,1024]{1,0:T(8,128)(2,1)S(1)}, bf16[128,1024]{1,0:T(8,128)(2,1)S(1)}, u32[]{:S(2)}, u32[]{:S(2)}) collective-permute-start(bf16[128,1024]{1,0:T(8,128)(2,1)S(1)} %shard_map.77.refs_0_), channel_id=1, source_target_pairs={{0,6},{1,7},{2,4},{3,5},{4,2},{5,3},{6,0},{7,1},{8,14},{9,15},{10,... | collective-permute-start | bytes 786440 | tf_op jit(solution)/shard_map/ppermute | solution.py:57
  14.8 0.9 collective-permute-done.5.refs_3_
  15.7 4.5 %collective-permute-done.3.refs_5_.refs_3_ = bf16[128,1024]{1,0:T(8,128)(2,1)S(1)} collective-permute-done((bf16[128,1024]{1,0:T(8,128)(2,1)S(1)}, bf16[128,1024]{1,0:T(8,128)(2,1)S(1)}, u32[]{:S(2)}, u32[]{:S(2)}) %collective-permute-start.3) | collective-permute-done | bytes 262176 | tf_op jit(solution)/shard_map/ppermute | solution.py:57
  20.2 1.5 %collective-permute-done.1.refs_4_.refs_1_ = bf16[128,1024]{1,0:T(8,128)(2,1)S(1)} collective-permute-done((bf16[128,1024]{1,0:T(8,128)(2,1)S(1)}, bf16[128,1024]{1,0:T(8,128)(2,1)S(1)}, u32[]{:S(2)}, u32[]{:S(2)}) %collective-permute-start.1) | collective-permute-done | bytes 262176 | tf_op jit(solution)/shard_map/ppermute | solution.py:57
  21.8 3.1 %collective-permute-start.7 = (bf16[256,1024]{1,0:T(8,128)(2,1)S(1)}, bf16[256,1024]{1,0:T(8,128)(2,1)S(1)}, u32[]{:S(2)}, u32[]{:S(2)}) collective-permute-start(bf16[256,1024]{1,0:T(8,128)(2,1)S(1)} %get-tuple-element.50.refs_2_.refs_4_), channel_id=1, source_target_pairs={{0,24},{1,97},{2,26},{3,99},{4,28},{5,101},{6,30},{7,103},{8,16},{... | collective-permute-start | bytes 1572872 | tf_op jit(solution)/shard_map/ppermute | solution.py:57
  25.0 1.1 %collective-permute-start.9 = (bf16[256,1024]{1,0:T(8,128)(2,1)S(1)}, bf16[256,1024]{1,0:T(8,128)(2,1)S(1)}, u32[]{:S(2)}, u32[]{:S(2)}) collective-permute-start(bf16[256,1024]{1,0:T(8,128)(2,1)S(1)} %get-tuple-element.51.refs_3_.refs_5_), channel_id=1, source_target_pairs={{0,24},{1,97},{2,26},{3,99},{4,28},{5,101},{6,30},{7,103},{8,16},{... | collective-permute-start | bytes 1572872 | tf_op jit(solution)/shard_map/ppermute | solution.py:57
  27.1 7.7 %collective-permute-done.2.refs_2_ = bf16[128,1024]{1,0:T(8,128)(2,1)S(1)} collective-permute-done((bf16[128,1024]{1,0:T(8,128)(2,1)S(1)}, bf16[128,1024]{1,0:T(8,128)(2,1)S(1)}, u32[]{:S(2)}, u32[]{:S(2)}) %collective-permute-start.2) | collective-permute-done | bytes 262176 | tf_op jit(solution)/shard_map/ppermute | solution.py:57
  34.8 3.1 %collective-permute-done.9.refs_7_.refs_3_.refs_11_ = bf16[256,1024]{1,0:T(8,128)(2,1)S(1)} collective-permute-done((bf16[256,1024]{1,0:T(8,128)(2,1)S(1)}, bf16[256,1024]{1,0:T(8,128)(2,1)S(1)}, u32[]{:S(2)}, u32[]{:S(2)}) %collective-permute-start.9) | collective-permute-done | bytes 524320 | tf_op jit(solution)/shard_map/ppermute | solution.py:57
  37.8 1.8 %collective-permute-done.8.refs_6_.refs_3_.refs_7_ = bf16[256,1024]{1,0:T(8,128)(2,1)S(1)} collective-permute-done((bf16[256,1024]{1,0:T(8,128)(2,1)S(1)}, bf16[256,1024]{1,0:T(8,128)(2,1)S(1)}, u32[]{:S(2)}, u32[]{:S(2)}) %collective-permute-start.8) | collective-permute-done | bytes 524320 | tf_op jit(solution)/shard_map/ppermute | solution.py:57
  40.0 1.2 %collective-permute-start.12 = (bf16[256,1024]{1,0:T(8,128)(2,1)S(1)}, bf16[256,1024]{1,0:T(8,128)(2,1)S(1)}, u32[]{:S(2)}, u32[]{:S(2)}) collective-permute-start(bf16[256,1024]{1,0:T(8,128)(2,1)S(1)} %collective-permute-done.8.refs_6_.refs_3_.refs_7_), channel_id=1, source_target_pairs={{0,24},{1,97},{2,26},{3,99},{4,28},{5,101},{6,30},{7,103},{8,16},{... | collective-permute-start | bytes 1572872 | tf_op jit(solution)/shard_map/ppermute | solution.py:57
  41.2 1.3 %collective-permute-done.10.refs_1_ = bf16[512,1024]{1,0:T(8,128)(2,1)S(1)} collective-permute-done((bf16[512,1024]{1,0:T(8,128)(2,1)S(1)}, bf16[512,1024]{1,0:T(8,128)(2,1)S(1)}, u32[]{:S(2)}, u32[]{:S(2)}) %collective-permute-start.10) | collective-permute-done | bytes 1048608 | tf_op jit(solution)/shard_map/ppermute | solution.py:57
  42.5 6.5 %shard_map.80 = (f32[8,1024]{1,0:T(8,128)S(1)}, f32[8,1536]{1,0:T(8,128)S(1)}, f32[1024,256]{1,0:T(8,128)S(1)}, f32[1024,256]{1,0:T(8,128)S(1)}, f32[1024,256]{1...) custom-call(bf16[512,1024]{1,0:T(8,128)(2,1)S(1)} %shard_map.79.refs, ...), custom_call_target="tpu_custom_call" | custom-call | flops 3221225472 | bytes 17907712 | tf_op jit(solution)/shard_map/pallas_call | solution.py:80
  49.1 1.3 %collective-permute-done.12.refs_3_.refs_9_ = bf16[256,1024]{1,0:T(8,128)(2,1)S(1)} collective-permute-done((bf16[256,1024]{1,0:T(8,128)(2,1)S(1)}, bf16[256,1024]{1,0:T(8,128)(2,1)S(1)}, u32[]{:S(2)}, u32[]{:S(2)}) %collective-permute-start.12) | collective-permute-done | bytes 524320 | tf_op jit(solution)/shard_map/ppermute | solution.py:57
  50.4 2.0 %shard_map.81 = (f32[8,1024]{1,0:T(8,128)S(1)}, f32[8,512]{1,0:T(8,128)S(1)}, f32[1024,256]{1,0:T(8,128)S(1)}, f32[1024,256]{1,0:T(8,128)S(1)}, f32[1024,256]{1,0:T(8,128)S(1)}, /*index=5*/f32[1024,256]{1,0:T(8,128)S(1)}) custom-call(bf16[512,1024]{1,0:T(8,128)(2,1)S(1)} %shard_map.79.refs_0_, bf16[512,1024]{1,0:T(8,128)(2,1)S(1)} %collective-permute-done.10.refs_1_, ...), custom_call_target="tpu_custom_call" | custom-call | flops 1073741824 | bytes 7421952 | tf_op jit(solution)/shard_map/pallas_call | solution.py:80
  52.9 0.9 collective-permute-done.13.got_ref
  53.9 2.8 %collective-permute-start.16 = (f32[8,2048]{1,0:T(8,128)S(1)}, f32[8,2048]{1,0:T(8,128)S(1)}, u32[]{:S(2)}, u32[]{:S(2)}) collective-permute-start(f32[8,2048]{1,0:T(8,128)S(1)} %shard_map.83.own_ref), channel_id=1, source_target_pairs={{0,96},{1,7},{2,98},{3,5},{4,100},{5,3},{6,102},{7,1},{8,104},{9,1... | collective-permute-start | bytes 196616 | tf_op jit(solution)/shard_map/ppermute | solution.py:57
  58.0 1.4 %collective-permute-done.16.g3 = f32[8,2048]{1,0:T(8,128)S(1)} collective-permute-done((f32[8,2048]{1,0:T(8,128)S(1)}, f32[8,2048]{1,0:T(8,128)S(1)}, u32[]{:S(2)}, u32[]{:S(2)}) %collective-permute-start.16) | collective-permute-done | bytes 65568 | tf_op jit(solution)/shard_map/ppermute | solution.py:57
  59.4 3.1 %collective-permute-done.15.g2 = f32[8,2048]{1,0:T(8,128)S(1)} collective-permute-done((f32[8,2048]{1,0:T(8,128)S(1)}, f32[8,2048]{1,0:T(8,128)S(1)}, u32[]{:S(2)}, u32[]{:S(2)}) %collective-permute-start.15) | collective-permute-done | bytes 65568 | tf_op jit(solution)/shard_map/ppermute | solution.py:57
  62.7 1.2 %collective-permute-done.17.got_ref = f32[8,2048]{1,0:T(8,128)S(1)} collective-permute-done((f32[8,2048]{1,0:T(8,128)S(1)}, f32[8,2048]{1,0:T(8,128)S(1)}, u32[]{:S(2)}, u32[]{:S(2)}) %collective-permute-start.17) | collective-permute-done | bytes 65568 | tf_op jit(solution)/shard_map/ppermute | solution.py:57
  64.1 1.3 %collective-permute-start.20 = (f32[8,2048]{1,0:T(8,128)S(1)}, f32[8,2048]{1,0:T(8,128)S(1)}, u32[]{:S(2)}, u32[]{:S(2)}) collective-permute-start(f32[8,2048]{1,0:T(8,128)S(1)} %get-tuple-element.57.own_ref), channel_id=1, source_target_pairs={{0,24},{1,25},{2,26},{3,27},{4,28},{5,29},{6,30},{7,31},{8,16},{9,... | collective-permute-start | bytes 196616 | tf_op jit(solution)/shard_map/ppermute | solution.py:57
  65.4 1.6 %collective-permute-start.19 = (f32[8,2048]{1,0:T(8,128)S(1)}, f32[8,2048]{1,0:T(8,128)S(1)}, u32[]{:S(2)}, u32[]{:S(2)}) collective-permute-start(f32[8,2048]{1,0:T(8,128)S(1)} %get-tuple-element.57.own_ref), channel_id=1, source_target_pairs={{0,16},{1,17},{2,18},{3,19},{4,20},{5,21},{6,22},{7,23},{8,24},{9,... | collective-permute-start | bytes 196616 | tf_op jit(solution)/shard_map/ppermute | solution.py:57
  66.9 1.4 %collective-permute-start.18 = (f32[8,2048]{1,0:T(8,128)S(1)}, f32[8,2048]{1,0:T(8,128)S(1)}, u32[]{:S(2)}, u32[]{:S(2)}) collective-permute-start(f32[8,2048]{1,0:T(8,128)S(1)} %get-tuple-element.57.own_ref), channel_id=1, source_target_pairs={{0,8},{1,9},{2,10},{3,11},{4,12},{5,13},{6,14},{7,15},{8,0},{9,1},... | collective-permute-start | bytes 196616 | tf_op jit(solution)/shard_map/ppermute | solution.py:57
  68.3 2.1 %collective-permute-done.20.g3 = f32[8,2048]{1,0:T(8,128)S(1)} collective-permute-done((f32[8,2048]{1,0:T(8,128)S(1)}, f32[8,2048]{1,0:T(8,128)S(1)}, u32[]{:S(2)}, u32[]{:S(2)}) %collective-permute-start.20) | collective-permute-done | bytes 65568 | tf_op jit(solution)/shard_map/ppermute | solution.py:57
  70.4 0.9 collective-permute-done.19.g2
  71.8 1.4 %shard_map.90 = (bf16[1024,512]{1,0:T(8,128)(2,1)S(1)}, bf16[528,512]{1,0:T(8,128)(2,1)S(1)}) custom-call(bf16[512,1024]{1,0:T(8,128)(2,1)S(1)} %shard_map.79.refs_0_, bf16[512,1024]{1,0:T(8,128)(2,1)S(1)} %collective-permute-done.10.refs_1_, bf16[256,1024]{1,0:T(8,128)(2,1)S(1)} %collective-permute-done.7.refs_5_.refs_2_.refs_10_, ...), custom_call_target="tpu_custom_call" | custom-call | tf_op jit(solution)/shard_map/pallas_call | solution.py:80
  73.3 2.1 %collective-permute-start.21 = (bf16[528,512]{1,0:T(8,128)(2,1)S(1)}, bf16[528,512]{1,0:T(8,128)(2,1)S(1)}, u32[]{:S(2)}, u32[]{:S(2)}) collective-permute-start(bf16[528,512]{1,0:T(8,128)(2,1)S(1)} %get-tuple-element.81), channel_id=1, source_target_pairs={{0,24},{1,97},{2,26},{3,99},{4,28},{5,101},{6,30},{7,103},{8,16},{... | collective-permute-start | bytes 1622024 | tf_op jit(solution)/shard_map/ppermute | solution.py:57
  75.3 1.4 %shard_map.88 = (bf16[1024,512]{1,0:T(8,128)(2,1)S(1)}, bf16[528,512]{1,0:T(8,128)(2,1)S(1)}) custom-call(bf16[512,1024]{1,0:T(8,128)(2,1)S(1)} %shard_map.79.refs_0_, bf16[512,1024]{1,0:T(8,128)(2,1)S(1)} %collective-permute-done.10.refs_1_, bf16[256,1024]{1,0:T(8,128)(2,1)S(1)} %collective-permute-done.6.refs_4_.refs_2_.refs_6_, ...), custom_call_target="tpu_custom_call" | custom-call | tf_op jit(solution)/shard_map/pallas_call | solution.py:80
  76.8 1.4 %shard_map.89 = (bf16[1024,512]{1,0:T(8,128)(2,1)S(1)}, bf16[528,512]{1,0:T(8,128)(2,1)S(1)}) custom-call(bf16[512,1024]{1,0:T(8,128)(2,1)S(1)} %shard_map.79.refs_0_, bf16[512,1024]{1,0:T(8,128)(2,1)S(1)} %collective-permute-done.10.refs_1_, bf16[256,1024]{1,0:T(8,128)(2,1)S(1)} %collective-permute-done.11.refs_2_.refs_8_, ...), custom_call_target="tpu_custom_call" | custom-call | tf_op jit(solution)/shard_map/pallas_call | solution.py:80
  78.2 1.4 %shard_map.87 = (bf16[1024,512]{1,0:T(8,128)(2,1)S(1)}, f32[512,512]{1,0:T(8,128)S(1)}) custom-call(bf16[512,1024]{1,0:T(8,128)(2,1)S(1)} %shard_map.79.refs_0_, bf16[512,1024]{1,0:T(8,128)(2,1)S(1)} %collective-permute-done.10.refs_1_, bf16[256,1024]{1,0:T(8,128)(2,1)S(1)} %get-tuple-element.50.refs_2_.refs_4_, ...), custom_call_target="tpu_custom_call" | custom-call | tf_op jit(solution)/shard_map/pallas_call | solution.py:80
  79.7 1.2 %shard_map.92 = bf16[528,512]{1,0:T(8,128)(2,1)S(1)} custom-call(bf16[1024,512]{1,0:T(8,128)(2,1)S(1)} %get-tuple-element.64.refs_0_, bf16[1024,512]{1,0:T(8,128)(2,1)S(1)} %get-tuple-element.70.refs_1_, bf16[1024,512]{1,0:T(8,128)(2,1)S(1)} %get-tuple-element.75.refs_2_, bf16[1024,512]{1,0:T(8,128)(2,1)S(1)} %get-tuple-element.80.refs_3_, ...), custom_call_target="tpu_custom_call" | custom-call | tf_op jit(solution)/shard_map/pallas_call | solution.py:80
  81.0 2.8 %collective-permute-start.27 = (bf16[528,512]{1,0:T(8,128)(2,1)S(1)}, bf16[528,512]{1,0:T(8,128)(2,1)S(1)}, u32[]{:S(2)}, u32[]{:S(2)}) collective-permute-start(bf16[528,512]{1,0:T(8,128)(2,1)S(1)} %get-tuple-element.89), channel_id=1, source_target_pairs={{0,16},{1,65},{2,18},{3,67},{4,20},{5,69},{6,22},{7,71},{8,24},{9,... | collective-permute-start | bytes 1622024 | tf_op jit(solution)/shard_map/ppermute | solution.py:57
  83.9 2.3 %collective-permute-done.22.refs_13_.refs_3_ = bf16[528,512]{1,0:T(8,128)(2,1)S(1)} collective-permute-done((bf16[528,512]{1,0:T(8,128)(2,1)S(1)}, bf16[528,512]{1,0:T(8,128)(2,1)S(1)}, u32[]{:S(2)}, u32[]{:S(2)}) %collective-permute-start.22) | collective-permute-done | bytes 540704 | tf_op jit(solution)/shard_map/ppermute | solution.py:57
  86.2 1.2 %shard_map.91.refs_0_ = f32[512,512]{1,0:T(8,128)S(1)} custom-call(bf16[1024,512]{1,0:T(8,128)(2,1)S(1)} %get-tuple-element.64.refs_0_, bf16[1024,512]{1,0:T(8,128)(2,1)S(1)} %get-tuple-element.70.refs_1_, bf16[1024,512]{1,0:T(8,128)(2,1)S(1)} %get-tuple-element.75.refs_2_, bf16[1024,512]{1,0:T(8,128)(2,1)S(1)} %get-tuple-element.80.refs_3_, ...), custom_call_target="tpu_custom_call" | custom-call | tf_op jit(solution)/shard_map/pallas_call | solution.py:80
  87.5 1.6 %collective-permute-start.24 = (bf16[144,512]{1,0:T(8,128)(2,1)S(1)}, bf16[144,512]{1,0:T(8,128)(2,1)S(1)}, u32[]{:S(2)}, u32[]{:S(2)}) collective-permute-start(bf16[144,512]{1,0:T(8,128)(2,1)S(1)} %get-tuple-element.85), channel_id=1, source_target_pairs={{0,6},{1,7},{2,4},{3,5},{4,2},{5,3},{6,0},{7,1},{8,14},{9,15},{10,... | collective-permute-start | bytes 442376 | tf_op jit(solution)/shard_map/ppermute | solution.py:57
  89.1 0.9 collective-permute-start.25
  90.0 1.7 %collective-permute-start.26 = (bf16[144,512]{1,0:T(8,128)(2,1)S(1)}, bf16[144,512]{1,0:T(8,128)(2,1)S(1)}, u32[]{:S(2)}, u32[]{:S(2)}) collective-permute-start(bf16[144,512]{1,0:T(8,128)(2,1)S(1)} %get-tuple-element.87), channel_id=1, source_target_pairs={{0,2},{1,3},{2,0},{3,1},{4,6},{5,7},{6,4},{7,5},{8,10},{9,11},{10,... | collective-permute-start | bytes 442376 | tf_op jit(solution)/shard_map/ppermute | solution.py:57
  91.7 0.9 collective-permute-done.27.refs_4_
  92.6 1.3 %collective-permute-done.24.refs_5_.refs_2_ = bf16[144,512]{1,0:T(8,128)(2,1)S(1)} collective-permute-done((bf16[144,512]{1,0:T(8,128)(2,1)S(1)}, bf16[144,512]{1,0:T(8,128)(2,1)S(1)}, u32[]{:S(2)}, u32[]{:S(2)}) %collective-permute-start.24) | collective-permute-done | bytes 147488 | tf_op jit(solution)/shard_map/ppermute | solution.py:57
  94.2 1.5 %collective-permute-start.28 = (bf16[144,512]{1,0:T(8,128)(2,1)S(1)}, bf16[144,512]{1,0:T(8,128)(2,1)S(1)}, u32[]{:S(2)}, u32[]{:S(2)}) collective-permute-start(bf16[144,512]{1,0:T(8,128)(2,1)S(1)} %get-tuple-element.91), channel_id=1, source_target_pairs={{0,96},{1,25},{2,98},{3,27},{4,100},{5,29},{6,102},{7,31},{8,104},... | collective-permute-start | bytes 442376 | tf_op jit(solution)/shard_map/ppermute | solution.py:57
  95.7 0.9 collective-permute-start.29
  96.6 1.8 %collective-permute-start.30 = (bf16[144,512]{1,0:T(8,128)(2,1)S(1)}, bf16[144,512]{1,0:T(8,128)(2,1)S(1)}, u32[]{:S(2)}, u32[]{:S(2)}) collective-permute-start(bf16[144,512]{1,0:T(8,128)(2,1)S(1)} %get-tuple-element.93), channel_id=1, source_target_pairs={{0,32},{1,9},{2,34},{3,11},{4,36},{5,13},{6,38},{7,15},{8,40},{9,1... | collective-permute-start | bytes 442376 | tf_op jit(solution)/shard_map/ppermute | solution.py:57
  98.4 2.3 %collective-permute-done.28.refs_7_ = bf16[144,512]{1,0:T(8,128)(2,1)S(1)} collective-permute-done((bf16[144,512]{1,0:T(8,128)(2,1)S(1)}, bf16[144,512]{1,0:T(8,128)(2,1)S(1)}, u32[]{:S(2)}, u32[]{:S(2)}) %collective-permute-start.28) | collective-permute-done | bytes 147488 | tf_op jit(solution)/shard_map/ppermute | solution.py:57
  100.6 1.7 %collective-permute-done.29.refs_8_ = bf16[144,512]{1,0:T(8,128)(2,1)S(1)} collective-permute-done((bf16[144,512]{1,0:T(8,128)(2,1)S(1)}, bf16[144,512]{1,0:T(8,128)(2,1)S(1)}, u32[]{:S(2)}, u32[]{:S(2)}) %collective-permute-start.29) | collective-permute-done | bytes 147488 | tf_op jit(solution)/shard_map/ppermute | solution.py:57
  103.1 1.1 %shard_map.95 = (f32[128,512]{1,0:T(8,128)}, f32[128,512]{1,0:T(8,128)}, f32[1,1]{1,0:T(1,128)}) custom-call(bf16[128,512]{1,0:T(8,128)(2,1)S(1)} %copy-done.2, f32[136,512]{1,0:T(8,128)S(1)} %get-tuple-element.84.refs_1_, bf16[144,512]{1,0:T(8,128)(2,1)S(1)} %collective-permute-done.24.refs_5_.refs_2_, ...), custom_call_target="tpu_custom_call" | custom-call | tf_op jit(solution)/shard_map/pallas_call | solution.py:80
  (44 shorter events, 7.0 us)
Async XLA Ops:
  0.6 9.5 %copy-start = (bf16[1280,512]{1,0:T(8,128)(2,1)S(1)}, bf16[1280,512]{1,0:T(8,128)(2,1)}, u32[]{:S(2)}) copy-start(bf16[1280,512]{1,0:T(8,128)(2,1)} %sketch_ref.1) | copy-start | bytes 3932164
  0.6 9.5 %copy-start.2 = (bf16[128,512]{1,0:T(8,128)(2,1)S(1)}, bf16[128,512]{1,0:T(8,128)(2,1)}, u32[]{:S(2)}) copy-start(bf16[128,512]{1,0:T(8,128)(2,1)} %refs_0_.1) | copy-start | bytes 393220
  0.7 9.5 %copy-start.4 = (bf16[128,1280]{1,0:T(8,128)(2,1)S(1)}, bf16[128,1280]{1,0:T(8,128)(2,1)}, u32[]{:S(2)}) copy-start(bf16[128,1280]{1,0:T(8,128)(2,1)} %teacher_ref.1) | copy-start | bytes 983044
  3.4 18.2 %copy-start.1 = (bf16[128,1024]{1,0:T(8,128)(2,1)S(1)}, bf16[128,1024]{1,0:T(8,128)(2,1)}, u32[]{:S(2)}) copy-start(bf16[128,1024]{1,0:T(8,128)(2,1)} %shard_map.76.refs_0_) | copy-start | bytes 786436
  3.4 6.7 %collective-permute-start = (bf16[128,1024]{1,0:T(8,128)(2,1)}, bf16[128,1024]{1,0:T(8,128)(2,1)S(1)}, u32[]{:S(2)}, u32[]{:S(2)}) collective-permute-start(bf16[128,1024]{1,0:T(8,128)(2,1)} %shard_map.76.refs_0_), channel_id=1, source_target_pairs={{0,32},{1,9},{2,34},{3,11},{4,36},{5,13},{6,38},{7,15},{8,40},{9,1... | collective-permute-start | bytes 786440 | tf_op jit(solution)/shard_map/ppermute | solution.py:57
  5.1 10.6 %collective-permute-start.5 = (bf16[128,1024]{1,0:T(8,128)(2,1)}, bf16[128,1024]{1,0:T(8,128)(2,1)S(1)}, u32[]{:S(2)}, u32[]{:S(2)}) collective-permute-start(bf16[128,1024]{1,0:T(8,128)(2,1)} %shard_map.76.refs_0_), channel_id=1, source_target_pairs={{0,96},{1,25},{2,98},{3,27},{4,100},{5,29},{6,102},{7,31},{8,104},... | collective-permute-start | bytes 786440 | tf_op jit(solution)/shard_map/ppermute | solution.py:57
  7.2 8.5 %collective-permute-start.4 = (bf16[128,1024]{1,0:T(8,128)(2,1)}, bf16[128,1024]{1,0:T(8,128)(2,1)S(1)}, u32[]{:S(2)}, u32[]{:S(2)}) collective-permute-start(bf16[128,1024]{1,0:T(8,128)(2,1)} %shard_map.76.refs_0_), channel_id=1, source_target_pairs={{0,64},{1,17},{2,66},{3,19},{4,68},{5,21},{6,70},{7,23},{8,72},{9,... | collective-permute-start | bytes 786440 | tf_op jit(solution)/shard_map/ppermute | solution.py:57
  10.6 9.6 %collective-permute-start.3 = (bf16[128,1024]{1,0:T(8,128)(2,1)S(1)}, bf16[128,1024]{1,0:T(8,128)(2,1)S(1)}, u32[]{:S(2)}, u32[]{:S(2)}) collective-permute-start(bf16[128,1024]{1,0:T(8,128)(2,1)S(1)} %shard_map.77.refs_0_), channel_id=1, source_target_pairs={{0,6},{1,7},{2,4},{3,5},{4,2},{5,3},{6,0},{7,1},{8,14},{9,15},{10,... | collective-permute-start | bytes 786440 | tf_op jit(solution)/shard_map/ppermute | solution.py:57
  14.8 6.9 %collective-permute-start.1 = (bf16[128,1024]{1,0:T(8,128)(2,1)S(1)}, bf16[128,1024]{1,0:T(8,128)(2,1)S(1)}, u32[]{:S(2)}, u32[]{:S(2)}) collective-permute-start(bf16[128,1024]{1,0:T(8,128)(2,1)S(1)} %shard_map.77.refs_0_), channel_id=1, source_target_pairs={{0,2},{1,3},{2,0},{3,1},{4,6},{5,7},{6,4},{7,5},{8,10},{9,11},{10,... | collective-permute-start | bytes 786440 | tf_op jit(solution)/shard_map/ppermute | solution.py:57
  21.8 13.0 %collective-permute-start.7 = (bf16[256,1024]{1,0:T(8,128)(2,1)S(1)}, bf16[256,1024]{1,0:T(8,128)(2,1)S(1)}, u32[]{:S(2)}, u32[]{:S(2)}) collective-permute-start(bf16[256,1024]{1,0:T(8,128)(2,1)S(1)} %get-tuple-element.50.refs_2_.refs_4_), channel_id=1, source_target_pairs={{0,24},{1,97},{2,26},{3,99},{4,28},{5,101},{6,30},{7,103},{8,16},{... | collective-permute-start | bytes 1572872 | tf_op jit(solution)/shard_map/ppermute | solution.py:57
  24.8 9.9 %collective-permute-start.6 = (bf16[256,1024]{1,0:T(8,128)(2,1)S(1)}, bf16[256,1024]{1,0:T(8,128)(2,1)S(1)}, u32[]{:S(2)}, u32[]{:S(2)}) collective-permute-start(bf16[256,1024]{1,0:T(8,128)(2,1)S(1)} %get-tuple-element.50.refs_2_.refs_4_), channel_id=1, source_target_pairs={{0,8},{1,33},{2,10},{3,35},{4,12},{5,37},{6,14},{7,39},{8,0},{9,41... | collective-permute-start | bytes 1572872 | tf_op jit(solution)/shard_map/ppermute | solution.py:57
  25.0 12.9 %collective-permute-start.9 = (bf16[256,1024]{1,0:T(8,128)(2,1)S(1)}, bf16[256,1024]{1,0:T(8,128)(2,1)S(1)}, u32[]{:S(2)}, u32[]{:S(2)}) collective-permute-start(bf16[256,1024]{1,0:T(8,128)(2,1)S(1)} %get-tuple-element.51.refs_3_.refs_5_), channel_id=1, source_target_pairs={{0,24},{1,97},{2,26},{3,99},{4,28},{5,101},{6,30},{7,103},{8,16},{... | collective-permute-start | bytes 1572872 | tf_op jit(solution)/shard_map/ppermute | solution.py:57
  26.0 13.6 %collective-permute-start.8 = (bf16[256,1024]{1,0:T(8,128)(2,1)S(1)}, bf16[256,1024]{1,0:T(8,128)(2,1)S(1)}, u32[]{:S(2)}, u32[]{:S(2)}) collective-permute-start(bf16[256,1024]{1,0:T(8,128)(2,1)S(1)} %get-tuple-element.51.refs_3_.refs_5_), channel_id=1, source_target_pairs={{0,8},{1,33},{2,10},{3,35},{4,12},{5,37},{6,14},{7,39},{8,0},{9,41... | collective-permute-start | bytes 1572872 | tf_op jit(solution)/shard_map/ppermute | solution.py:57
  26.9 7.9 %collective-permute-start.2 = (bf16[128,1024]{1,0:T(8,128)(2,1)S(1)}, bf16[128,1024]{1,0:T(8,128)(2,1)S(1)}, u32[]{:S(2)}, u32[]{:S(2)}) collective-permute-start(bf16[128,1024]{1,0:T(8,128)(2,1)S(1)} %shard_map.77.refs_0_), channel_id=1, source_target_pairs={{0,4},{1,5},{2,6},{3,7},{4,0},{5,1},{6,2},{7,3},{8,12},{9,13},{10,... | collective-permute-start | bytes 786440 | tf_op jit(solution)/shard_map/ppermute | solution.py:57
  39.7 2.7 %collective-permute-start.10 = (bf16[512,1024]{1,0:T(8,128)(2,1)S(1)}, bf16[512,1024]{1,0:T(8,128)(2,1)S(1)}, u32[]{:S(2)}, u32[]{:S(2)}) collective-permute-start(bf16[512,1024]{1,0:T(8,128)(2,1)S(1)} %shard_map.79.refs_0_), channel_id=1, source_target_pairs={{0,1},{1,0},{2,3},{3,2},{4,5},{5,4},{6,7},{7,6},{8,9},{9,8},{10,11... | collective-permute-start | bytes 3145736 | tf_op jit(solution)/shard_map/ppermute | solution.py:57
  39.8 9.3 %collective-permute-start.11 = (bf16[256,1024]{1,0:T(8,128)(2,1)S(1)}, bf16[256,1024]{1,0:T(8,128)(2,1)S(1)}, u32[]{:S(2)}, u32[]{:S(2)}) collective-permute-start(bf16[256,1024]{1,0:T(8,128)(2,1)S(1)} %collective-permute-done.7.refs_5_.refs_2_.refs_10_), channel_id=1, source_target_pairs={{0,8},{1,33},{2,10},{3,35},{4,12},{5,37},{6,14},{7,39},{8,0},{9,41... | collective-permute-start | bytes 1572872 | tf_op jit(solution)/shard_map/ppermute | solution.py:57
  40.0 10.4 %collective-permute-start.12 = (bf16[256,1024]{1,0:T(8,128)(2,1)S(1)}, bf16[256,1024]{1,0:T(8,128)(2,1)S(1)}, u32[]{:S(2)}, u32[]{:S(2)}) collective-permute-start(bf16[256,1024]{1,0:T(8,128)(2,1)S(1)} %collective-permute-done.8.refs_6_.refs_3_.refs_7_), channel_id=1, source_target_pairs={{0,24},{1,97},{2,26},{3,99},{4,28},{5,101},{6,30},{7,103},{8,16},{... | collective-permute-start | bytes 1572872 | tf_op jit(solution)/shard_map/ppermute | solution.py:57
  52.5 1.3 %collective-permute-start.13 = (f32[8,2048]{1,0:T(8,128)S(1)}, f32[8,2048]{1,0:T(8,128)S(1)}, u32[]{:S(2)}, u32[]{:S(2)}) collective-permute-start(f32[8,2048]{1,0:T(8,128)S(1)} %shard_map.82.own_ref), channel_id=1, source_target_pairs={{0,1},{1,0},{2,3},{3,2},{4,5},{5,4},{6,7},{7,6},{8,9},{9,8},{10,11... | collective-permute-start | bytes 196616 | tf_op jit(solution)/shard_map/ppermute | solution.py:57
  53.9 5.6 %collective-permute-start.16 = (f32[8,2048]{1,0:T(8,128)S(1)}, f32[8,2048]{1,0:T(8,128)S(1)}, u32[]{:S(2)}, u32[]{:S(2)}) collective-permute-start(f32[8,2048]{1,0:T(8,128)S(1)} %shard_map.83.own_ref), channel_id=1, source_target_pairs={{0,96},{1,7},{2,98},{3,5},{4,100},{5,3},{6,102},{7,1},{8,104},{9,1... | collective-permute-start | bytes 196616 | tf_op jit(solution)/shard_map/ppermute | solution.py:57
  56.7 5.8 %collective-permute-start.15 = (f32[8,2048]{1,0:T(8,128)S(1)}, f32[8,2048]{1,0:T(8,128)S(1)}, u32[]{:S(2)}, u32[]{:S(2)}) collective-permute-start(f32[8,2048]{1,0:T(8,128)S(1)} %shard_map.83.own_ref), channel_id=1, source_target_pairs={{0,64},{1,5},{2,66},{3,7},{4,68},{5,1},{6,70},{7,3},{8,72},{9,13},... | collective-permute-start | bytes 196616 | tf_op jit(solution)/shard_map/ppermute | solution.py:57
  57.5 5.0 %collective-permute-start.14 = (f32[8,2048]{1,0:T(8,128)S(1)}, f32[8,2048]{1,0:T(8,128)S(1)}, u32[]{:S(2)}, u32[]{:S(2)}) collective-permute-start(f32[8,2048]{1,0:T(8,128)S(1)} %shard_map.83.own_ref), channel_id=1, source_target_pairs={{0,32},{1,3},{2,34},{3,1},{4,36},{5,7},{6,38},{7,5},{8,40},{9,11},... | collective-permute-start | bytes 196616 | tf_op jit(solution)/shard_map/ppermute | solution.py:57
  62.6 1.3 %collective-permute-start.17 = (f32[8,2048]{1,0:T(8,128)S(1)}, f32[8,2048]{1,0:T(8,128)S(1)}, u32[]{:S(2)}, u32[]{:S(2)}) collective-permute-start(f32[8,2048]{1,0:T(8,128)S(1)} %shard_map.84.own_ref), channel_id=1, source_target_pairs={{0,1},{1,0},{2,3},{3,2},{4,5},{5,4},{6,7},{7,6},{8,9},{9,8},{10,11... | collective-permute-start | bytes 196616 | tf_op jit(solution)/shard_map/ppermute | solution.py:57
  64.1 6.3 %collective-permute-start.20 = (f32[8,2048]{1,0:T(8,128)S(1)}, f32[8,2048]{1,0:T(8,128)S(1)}, u32[]{:S(2)}, u32[]{:S(2)}) collective-permute-start(f32[8,2048]{1,0:T(8,128)S(1)} %get-tuple-element.57.own_ref), channel_id=1, source_target_pairs={{0,24},{1,25},{2,26},{3,27},{4,28},{5,29},{6,30},{7,31},{8,16},{9,... | collective-permute-start | bytes 196616 | tf_op jit(solution)/shard_map/ppermute | solution.py:57
  65.4 5.9 %collective-permute-start.19 = (f32[8,2048]{1,0:T(8,128)S(1)}, f32[8,2048]{1,0:T(8,128)S(1)}, u32[]{:S(2)}, u32[]{:S(2)}) collective-permute-start(f32[8,2048]{1,0:T(8,128)S(1)} %get-tuple-element.57.own_ref), channel_id=1, source_target_pairs={{0,16},{1,17},{2,18},{3,19},{4,20},{5,21},{6,22},{7,23},{8,24},{9,... | collective-permute-start | bytes 196616 | tf_op jit(solution)/shard_map/ppermute | solution.py:57
  66.9 4.4 %collective-permute-start.18 = (f32[8,2048]{1,0:T(8,128)S(1)}, f32[8,2048]{1,0:T(8,128)S(1)}, u32[]{:S(2)}, u32[]{:S(2)}) collective-permute-start(f32[8,2048]{1,0:T(8,128)S(1)} %get-tuple-element.57.own_ref), channel_id=1, source_target_pairs={{0,8},{1,9},{2,10},{3,11},{4,12},{5,13},{6,14},{7,15},{8,0},{9,1},... | collective-permute-start | bytes 196616 | tf_op jit(solution)/shard_map/ppermute | solution.py:57
  73.3 10.6 %collective-permute-start.21 = (bf16[528,512]{1,0:T(8,128)(2,1)S(1)}, bf16[528,512]{1,0:T(8,128)(2,1)S(1)}, u32[]{:S(2)}, u32[]{:S(2)}) collective-permute-start(bf16[528,512]{1,0:T(8,128)(2,1)S(1)} %get-tuple-element.81), channel_id=1, source_target_pairs={{0,24},{1,97},{2,26},{3,99},{4,28},{5,101},{6,30},{7,103},{8,16},{... | collective-permute-start | bytes 1622024 | tf_op jit(solution)/shard_map/ppermute | solution.py:57
  76.7 9.4 %collective-permute-start.22 = (bf16[528,512]{1,0:T(8,128)(2,1)S(1)}, bf16[528,512]{1,0:T(8,128)(2,1)S(1)}, u32[]{:S(2)}, u32[]{:S(2)}) collective-permute-start(bf16[528,512]{1,0:T(8,128)(2,1)S(1)} %get-tuple-element.82), channel_id=1, source_target_pairs={{0,8},{1,33},{2,10},{3,35},{4,12},{5,37},{6,14},{7,39},{8,0},{9,41... | collective-permute-start | bytes 1622024 | tf_op jit(solution)/shard_map/ppermute | solution.py:57
  80.9 6.5 %collective-permute-start.23 = (bf16[528,512]{1,0:T(8,128)(2,1)S(1)}, bf16[528,512]{1,0:T(8,128)(2,1)S(1)}, u32[]{:S(2)}, u32[]{:S(2)}) collective-permute-start(bf16[528,512]{1,0:T(8,128)(2,1)S(1)} %shard_map.92), channel_id=1, source_target_pairs={{0,1},{1,0},{2,3},{3,2},{4,5},{5,4},{6,7},{7,6},{8,9},{9,8},{10,11... | collective-permute-start | bytes 1622024 | tf_op jit(solution)/shard_map/ppermute | solution.py:57
  81.0 11.6 %collective-permute-start.27 = (bf16[528,512]{1,0:T(8,128)(2,1)S(1)}, bf16[528,512]{1,0:T(8,128)(2,1)S(1)}, u32[]{:S(2)}, u32[]{:S(2)}) collective-permute-start(bf16[528,512]{1,0:T(8,128)(2,1)S(1)} %get-tuple-element.89), channel_id=1, source_target_pairs={{0,16},{1,65},{2,18},{3,67},{4,20},{5,69},{6,22},{7,71},{8,24},{9,... | collective-permute-start | bytes 1622024 | tf_op jit(solution)/shard_map/ppermute | solution.py:57
  87.5 6.4 %collective-permute-start.24 = (bf16[144,512]{1,0:T(8,128)(2,1)S(1)}, bf16[144,512]{1,0:T(8,128)(2,1)S(1)}, u32[]{:S(2)}, u32[]{:S(2)}) collective-permute-start(bf16[144,512]{1,0:T(8,128)(2,1)S(1)} %get-tuple-element.85), channel_id=1, source_target_pairs={{0,6},{1,7},{2,4},{3,5},{4,2},{5,3},{6,0},{7,1},{8,14},{9,15},{10,... | collective-permute-start | bytes 442376 | tf_op jit(solution)/shard_map/ppermute | solution.py:57
  89.1 9.3 %collective-permute-start.25 = (bf16[144,512]{1,0:T(8,128)(2,1)S(1)}, bf16[144,512]{1,0:T(8,128)(2,1)S(1)}, u32[]{:S(2)}, u32[]{:S(2)}) collective-permute-start(bf16[144,512]{1,0:T(8,128)(2,1)S(1)} %get-tuple-element.86), channel_id=1, source_target_pairs={{0,4},{1,5},{2,6},{3,7},{4,0},{5,1},{6,2},{7,3},{8,12},{9,13},{10,... | collective-permute-start | bytes 442376 | tf_op jit(solution)/shard_map/ppermute | solution.py:57
  90.0 8.4 %collective-permute-start.26 = (bf16[144,512]{1,0:T(8,128)(2,1)S(1)}, bf16[144,512]{1,0:T(8,128)(2,1)S(1)}, u32[]{:S(2)}, u32[]{:S(2)}) collective-permute-start(bf16[144,512]{1,0:T(8,128)(2,1)S(1)} %get-tuple-element.87), channel_id=1, source_target_pairs={{0,2},{1,3},{2,0},{3,1},{4,6},{5,7},{6,4},{7,5},{8,10},{9,11},{10,... | collective-permute-start | bytes 442376 | tf_op jit(solution)/shard_map/ppermute | solution.py:57
  94.0 9.1 %copy-start.3 = (bf16[128,512]{1,0:T(8,128)(2,1)S(1)}, bf16[128,512]{1,0:T(8,128)(2,1)}, u32[]{:S(2)}) copy-start(bf16[128,512]{1,0:T(8,128)(2,1)} %refs_5_.1) | copy-start | bytes 393220
  94.2 6.4 %collective-permute-start.28 = (bf16[144,512]{1,0:T(8,128)(2,1)S(1)}, bf16[144,512]{1,0:T(8,128)(2,1)S(1)}, u32[]{:S(2)}, u32[]{:S(2)}) collective-permute-start(bf16[144,512]{1,0:T(8,128)(2,1)S(1)} %get-tuple-element.91), channel_id=1, source_target_pairs={{0,96},{1,25},{2,98},{3,27},{4,100},{5,29},{6,102},{7,31},{8,104},... | collective-permute-start | bytes 442376 | tf_op jit(solution)/shard_map/ppermute | solution.py:57
  95.7 6.6 %collective-permute-start.29 = (bf16[144,512]{1,0:T(8,128)(2,1)S(1)}, bf16[144,512]{1,0:T(8,128)(2,1)S(1)}, u32[]{:S(2)}, u32[]{:S(2)}) collective-permute-start(bf16[144,512]{1,0:T(8,128)(2,1)S(1)} %get-tuple-element.92), channel_id=1, source_target_pairs={{0,64},{1,17},{2,66},{3,19},{4,68},{5,21},{6,70},{7,23},{8,72},{9,... | collective-permute-start | bytes 442376 | tf_op jit(solution)/shard_map/ppermute | solution.py:57
  96.6 6.5 %collective-permute-start.30 = (bf16[144,512]{1,0:T(8,128)(2,1)S(1)}, bf16[144,512]{1,0:T(8,128)(2,1)S(1)}, u32[]{:S(2)}, u32[]{:S(2)}) collective-permute-start(bf16[144,512]{1,0:T(8,128)(2,1)S(1)} %get-tuple-element.93), channel_id=1, source_target_pairs={{0,32},{1,9},{2,34},{3,11},{4,36},{5,13},{6,38},{7,15},{8,40},{9,1... | collective-permute-start | bytes 442376 | tf_op jit(solution)/shard_map/ppermute | solution.py:57

commit v4 on v3

--- a/solution.py
+++ b/solution.py
@@ -660,7 +660,7 @@
     keep, *messages = combine(own_img, stats[3], [send(message, other_core())])
     image = [image_student, keep] + [send(messages[e - 1], along_z(e)) for e in (3, 2, 1)]
     keep_txt, *messages_txt = combine(own_txt, stats[2], got, image[2:3])
-    text = [text_student, keep_txt] + [send(messages_txt[e - 1], first(e)) for e in (3, 2, 1)]
+    text = [text_student, keep_txt] + [send(messages_txt[e - 1], first(e)) for e in (2, 3, 1)]
     pairs = rows * lax.axis_size("row") * lax.axis_size("col")
     grad_image, grad_text, mean_loss = finish(image, text, 0.5 / (LOG2E * pairs))
     return (grad_image, grad_text, mean_loss.reshape(()))

time: 105 us -> 105 us (level)
  transfers between devices with their start and end apart: 31 -> 31, of which waited for: 24 -> 23; matrix products, arithmetic and copies ran while one was open for 0% -> 0% of each run, Pallas kernels for 13% -> 13%
where the time goes in v4:
time: 105 us; the launch traced here: 104 us
  waiting for transfers between devices  43.6 us (42%)
  starting transfers between devices  37 us (35%)
  Pallas kernels  22.3 us (21%)
    ppermute x31, waiting for transfers between devices, send(): return lax.ppermute(x, AXES, pairs)  43.6 us
    ppermute x31, starting transfers between devices, send(): return lax.ppermute(x, AXES, pairs)  37 us
    pallas_call x20, Pallas kernels, call(): pl.pallas_call(kernel, out_shape=out_shape, in_specs=[pl.BlockSpec(memory...  22.3 us
  transfers between devices with their start and end apart: 31, of which 23 were waited for; matrix products, arithmetic and copies ran while one was open for 0% of the time, Pallas kernels for 13%

profile of v4, /device:TPU:0, one launch (start us, length us, event | category | flops | bytes accessed | tf_op | source)
XLA Modules:
  0.0 104.0 jit_solution(18388123164899815010)
XLA Ops:
  0.7 2.8 %shard_map.76.refs_0_ = bf16[128,1024]{1,0:T(8,128)(2,1)} custom-call(bf16[128,512]{1,0:T(8,128)(2,1)} %refs_5_.1, bf16[128,1280]{1,0:T(8,128)(2,1)} %teacher_hbm.1, bf16[1280,512]{1,0:T(8,128)(2,1)} %sketch_ref.1), custom_call_target="tpu_custom_call" | custom-call | flops 167772160 | bytes 2031616 | tf_op jit(solution)/shard_map/pallas_call | solution.py:80
  3.4 1.7 %collective-permute-start = (bf16[128,1024]{1,0:T(8,128)(2,1)}, bf16[128,1024]{1,0:T(8,128)(2,1)S(1)}, u32[]{:S(2)}, u32[]{:S(2)}) collective-permute-start(bf16[128,1024]{1,0:T(8,128)(2,1)} %shard_map.76.refs_0_), channel_id=1, source_target_pairs={{0,32},{1,9},{2,34},{3,11},{4,36},{5,13},{6,38},{7,15},{8,40},{9,1... | collective-permute-start | bytes 786440 | tf_op jit(solution)/shard_map/ppermute | solution.py:57
  5.1 2.1 %collective-permute-start.5 = (bf16[128,1024]{1,0:T(8,128)(2,1)}, bf16[128,1024]{1,0:T(8,128)(2,1)S(1)}, u32[]{:S(2)}, u32[]{:S(2)}) collective-permute-start(bf16[128,1024]{1,0:T(8,128)(2,1)} %shard_map.76.refs_0_), channel_id=1, source_target_pairs={{0,96},{1,25},{2,98},{3,27},{4,100},{5,29},{6,102},{7,31},{8,104},... | collective-permute-start | bytes 786440 | tf_op jit(solution)/shard_map/ppermute | solution.py:57
  7.8 2.3 %collective-permute-done.refs_0_.refs_1_ = bf16[128,1024]{1,0:T(8,128)(2,1)S(1)} collective-permute-done((bf16[128,1024]{1,0:T(8,128)(2,1)}, bf16[128,1024]{1,0:T(8,128)(2,1)S(1)}, u32[]{:S(2)}, u32[]{:S(2)}) %collective-permute-start) | collective-permute-done | bytes 262176 | tf_op jit(solution)/shard_map/ppermute | solution.py:57
  10.6 4.2 %collective-permute-start.3 = (bf16[128,1024]{1,0:T(8,128)(2,1)S(1)}, bf16[128,1024]{1,0:T(8,128)(2,1)S(1)}, u32[]{:S(2)}, u32[]{:S(2)}) collective-permute-start(bf16[128,1024]{1,0:T(8,128)(2,1)S(1)} %shard_map.77.refs_0_), channel_id=1, source_target_pairs={{0,6},{1,7},{2,4},{3,5},{4,2},{5,3},{6,0},{7,1},{8,14},{9,15},{10,... | collective-permute-start | bytes 786440 | tf_op jit(solution)/shard_map/ppermute | solution.py:57
  14.8 0.9 collective-permute-done.5.refs_3_
  15.7 4.5 %collective-permute-done.3.refs_5_.refs_3_ = bf16[128,1024]{1,0:T(8,128)(2,1)S(1)} collective-permute-done((bf16[128,1024]{1,0:T(8,128)(2,1)S(1)}, bf16[128,1024]{1,0:T(8,128)(2,1)S(1)}, u32[]{:S(2)}, u32[]{:S(2)}) %collective-permute-start.3) | collective-permute-done | bytes 262176 | tf_op jit(solution)/shard_map/ppermute | solution.py:57
  20.2 1.5 %collective-permute-done.1.refs_4_.refs_1_ = bf16[128,1024]{1,0:T(8,128)(2,1)S(1)} collective-permute-done((bf16[128,1024]{1,0:T(8,128)(2,1)S(1)}, bf16[128,1024]{1,0:T(8,128)(2,1)S(1)}, u32[]{:S(2)}, u32[]{:S(2)}) %collective-permute-start.1) | collective-permute-done | bytes 262176 | tf_op jit(solution)/shard_map/ppermute | solution.py:57
  21.8 3.1 %collective-permute-start.7 = (bf16[256,1024]{1,0:T(8,128)(2,1)S(1)}, bf16[256,1024]{1,0:T(8,128)(2,1)S(1)}, u32[]{:S(2)}, u32[]{:S(2)}) collective-permute-start(bf16[256,1024]{1,0:T(8,128)(2,1)S(1)} %get-tuple-element.50.refs_2_.refs_4_), channel_id=1, source_target_pairs={{0,24},{1,97},{2,26},{3,99},{4,28},{5,101},{6,30},{7,103},{8,16},{... | collective-permute-start | bytes 1572872 | tf_op jit(solution)/shard_map/ppermute | solution.py:57
  25.0 1.1 %collective-permute-start.9 = (bf16[256,1024]{1,0:T(8,128)(2,1)S(1)}, bf16[256,1024]{1,0:T(8,128)(2,1)S(1)}, u32[]{:S(2)}, u32[]{:S(2)}) collective-permute-start(bf16[256,1024]{1,0:T(8,128)(2,1)S(1)} %get-tuple-element.51.refs_3_.refs_5_), channel_id=1, source_target_pairs={{0,24},{1,97},{2,26},{3,99},{4,28},{5,101},{6,30},{7,103},{8,16},{... | collective-permute-start | bytes 1572872 | tf_op jit(solution)/shard_map/ppermute | solution.py:57
  26.0 0.8 collective-permute-start.8
  27.1 7.7 %collective-permute-done.2.refs_2_ = bf16[128,1024]{1,0:T(8,128)(2,1)S(1)} collective-permute-done((bf16[128,1024]{1,0:T(8,128)(2,1)S(1)}, bf16[128,1024]{1,0:T(8,128)(2,1)S(1)}, u32[]{:S(2)}, u32[]{:S(2)}) %collective-permute-start.2) | collective-permute-done | bytes 262176 | tf_op jit(solution)/shard_map/ppermute | solution.py:57
  34.8 3.1 %collective-permute-done.9.refs_7_.refs_3_.refs_11_ = bf16[256,1024]{1,0:T(8,128)(2,1)S(1)} collective-permute-done((bf16[256,1024]{1,0:T(8,128)(2,1)S(1)}, bf16[256,1024]{1,0:T(8,128)(2,1)S(1)}, u32[]{:S(2)}, u32[]{:S(2)}) %collective-permute-start.9) | collective-permute-done | bytes 524320 | tf_op jit(solution)/shard_map/ppermute | solution.py:57
  37.8 1.8 %collective-permute-done.8.refs_6_.refs_3_.refs_7_ = bf16[256,1024]{1,0:T(8,128)(2,1)S(1)} collective-permute-done((bf16[256,1024]{1,0:T(8,128)(2,1)S(1)}, bf16[256,1024]{1,0:T(8,128)(2,1)S(1)}, u32[]{:S(2)}, u32[]{:S(2)}) %collective-permute-start.8) | collective-permute-done | bytes 524320 | tf_op jit(solution)/shard_map/ppermute | solution.py:57
  40.0 1.2 %collective-permute-start.12 = (bf16[256,1024]{1,0:T(8,128)(2,1)S(1)}, bf16[256,1024]{1,0:T(8,128)(2,1)S(1)}, u32[]{:S(2)}, u32[]{:S(2)}) collective-permute-start(bf16[256,1024]{1,0:T(8,128)(2,1)S(1)} %collective-permute-done.8.refs_6_.refs_3_.refs_7_), channel_id=1, source_target_pairs={{0,24},{1,97},{2,26},{3,99},{4,28},{5,101},{6,30},{7,103},{8,16},{... | collective-permute-start | bytes 1572872 | tf_op jit(solution)/shard_map/ppermute | solution.py:57
  41.2 1.3 %collective-permute-done.10.refs_1_ = bf16[512,1024]{1,0:T(8,128)(2,1)S(1)} collective-permute-done((bf16[512,1024]{1,0:T(8,128)(2,1)S(1)}, bf16[512,1024]{1,0:T(8,128)(2,1)S(1)}, u32[]{:S(2)}, u32[]{:S(2)}) %collective-permute-start.10) | collective-permute-done | bytes 1048608 | tf_op jit(solution)/shard_map/ppermute | solution.py:57
  42.5 6.5 %shard_map.80 = (f32[8,1024]{1,0:T(8,128)S(1)}, f32[8,1536]{1,0:T(8,128)S(1)}, f32[1024,256]{1,0:T(8,128)S(1)}, f32[1024,256]{1,0:T(8,128)S(1)}, f32[1024,256]{1...) custom-call(bf16[512,1024]{1,0:T(8,128)(2,1)S(1)} %shard_map.79.refs, ...), custom_call_target="tpu_custom_call" | custom-call | flops 3221225472 | bytes 17907712 | tf_op jit(solution)/shard_map/pallas_call | solution.py:80
  49.1 1.3 %collective-permute-done.12.refs_3_.refs_9_ = bf16[256,1024]{1,0:T(8,128)(2,1)S(1)} collective-permute-done((bf16[256,1024]{1,0:T(8,128)(2,1)S(1)}, bf16[256,1024]{1,0:T(8,128)(2,1)S(1)}, u32[]{:S(2)}, u32[]{:S(2)}) %collective-permute-start.12) | collective-permute-done | bytes 524320 | tf_op jit(solution)/shard_map/ppermute | solution.py:57
  50.4 2.0 %shard_map.81 = (f32[8,1024]{1,0:T(8,128)S(1)}, f32[8,512]{1,0:T(8,128)S(1)}, f32[1024,256]{1,0:T(8,128)S(1)}, f32[1024,256]{1,0:T(8,128)S(1)}, f32[1024,256]{1,0:T(8,128)S(1)}, /*index=5*/f32[1024,256]{1,0:T(8,128)S(1)}) custom-call(bf16[512,1024]{1,0:T(8,128)(2,1)S(1)} %shard_map.79.refs_0_, bf16[512,1024]{1,0:T(8,128)(2,1)S(1)} %collective-permute-done.10.refs_1_, ...), custom_call_target="tpu_custom_call" | custom-call | flops 1073741824 | bytes 7421952 | tf_op jit(solution)/shard_map/pallas_call | solution.py:80
  52.9 0.9 collective-permute-done.13.got_ref
  53.9 2.8 %collective-permute-start.16 = (f32[8,2048]{1,0:T(8,128)S(1)}, f32[8,2048]{1,0:T(8,128)S(1)}, u32[]{:S(2)}, u32[]{:S(2)}) collective-permute-start(f32[8,2048]{1,0:T(8,128)S(1)} %shard_map.83.own_ref), channel_id=1, source_target_pairs={{0,96},{1,7},{2,98},{3,5},{4,100},{5,3},{6,102},{7,1},{8,104},{9,1... | collective-permute-start | bytes 196616 | tf_op jit(solution)/shard_map/ppermute | solution.py:57
  58.0 1.4 %collective-permute-done.16.g3 = f32[8,2048]{1,0:T(8,128)S(1)} collective-permute-done((f32[8,2048]{1,0:T(8,128)S(1)}, f32[8,2048]{1,0:T(8,128)S(1)}, u32[]{:S(2)}, u32[]{:S(2)}) %collective-permute-start.16) | collective-permute-done | bytes 65568 | tf_op jit(solution)/shard_map/ppermute | solution.py:57
  59.4 3.1 %collective-permute-done.15.g2 = f32[8,2048]{1,0:T(8,128)S(1)} collective-permute-done((f32[8,2048]{1,0:T(8,128)S(1)}, f32[8,2048]{1,0:T(8,128)S(1)}, u32[]{:S(2)}, u32[]{:S(2)}) %collective-permute-start.15) | collective-permute-done | bytes 65568 | tf_op jit(solution)/shard_map/ppermute | solution.py:57
  62.7 1.2 %collective-permute-done.17.got_ref = f32[8,2048]{1,0:T(8,128)S(1)} collective-permute-done((f32[8,2048]{1,0:T(8,128)S(1)}, f32[8,2048]{1,0:T(8,128)S(1)}, u32[]{:S(2)}, u32[]{:S(2)}) %collective-permute-start.17) | collective-permute-done | bytes 65568 | tf_op jit(solution)/shard_map/ppermute | solution.py:57
  64.1 1.3 %collective-permute-start.20 = (f32[8,2048]{1,0:T(8,128)S(1)}, f32[8,2048]{1,0:T(8,128)S(1)}, u32[]{:S(2)}, u32[]{:S(2)}) collective-permute-start(f32[8,2048]{1,0:T(8,128)S(1)} %get-tuple-element.57.own_ref), channel_id=1, source_target_pairs={{0,24},{1,25},{2,26},{3,27},{4,28},{5,29},{6,30},{7,31},{8,16},{9,... | collective-permute-start | bytes 196616 | tf_op jit(solution)/shard_map/ppermute | solution.py:57
  65.4 1.6 %collective-permute-start.19 = (f32[8,2048]{1,0:T(8,128)S(1)}, f32[8,2048]{1,0:T(8,128)S(1)}, u32[]{:S(2)}, u32[]{:S(2)}) collective-permute-start(f32[8,2048]{1,0:T(8,128)S(1)} %get-tuple-element.57.own_ref), channel_id=1, source_target_pairs={{0,16},{1,17},{2,18},{3,19},{4,20},{5,21},{6,22},{7,23},{8,24},{9,... | collective-permute-start | bytes 196616 | tf_op jit(solution)/shard_map/ppermute | solution.py:57
  66.9 1.4 %collective-permute-start.18 = (f32[8,2048]{1,0:T(8,128)S(1)}, f32[8,2048]{1,0:T(8,128)S(1)}, u32[]{:S(2)}, u32[]{:S(2)}) collective-permute-start(f32[8,2048]{1,0:T(8,128)S(1)} %get-tuple-element.57.own_ref), channel_id=1, source_target_pairs={{0,8},{1,9},{2,10},{3,11},{4,12},{5,13},{6,14},{7,15},{8,0},{9,1},... | collective-permute-start | bytes 196616 | tf_op jit(solution)/shard_map/ppermute | solution.py:57
  68.3 2.1 %collective-permute-done.20.g3 = f32[8,2048]{1,0:T(8,128)S(1)} collective-permute-done((f32[8,2048]{1,0:T(8,128)S(1)}, f32[8,2048]{1,0:T(8,128)S(1)}, u32[]{:S(2)}, u32[]{:S(2)}) %collective-permute-start.20) | collective-permute-done | bytes 65568 | tf_op jit(solution)/shard_map/ppermute | solution.py:57
  70.4 0.9 collective-permute-done.19.g2
  71.8 1.4 %shard_map.90 = (bf16[1024,512]{1,0:T(8,128)(2,1)S(1)}, bf16[528,512]{1,0:T(8,128)(2,1)S(1)}) custom-call(bf16[512,1024]{1,0:T(8,128)(2,1)S(1)} %shard_map.79.refs_0_, bf16[512,1024]{1,0:T(8,128)(2,1)S(1)} %collective-permute-done.10.refs_1_, bf16[256,1024]{1,0:T(8,128)(2,1)S(1)} %collective-permute-done.7.refs_5_.refs_2_.refs_10_, ...), custom_call_target="tpu_custom_call" | custom-call | tf_op jit(solution)/shard_map/pallas_call | solution.py:80
  73.3 2.1 %collective-permute-start.21 = (bf16[528,512]{1,0:T(8,128)(2,1)S(1)}, bf16[528,512]{1,0:T(8,128)(2,1)S(1)}, u32[]{:S(2)}, u32[]{:S(2)}) collective-permute-start(bf16[528,512]{1,0:T(8,128)(2,1)S(1)} %get-tuple-element.81), channel_id=1, source_target_pairs={{0,24},{1,97},{2,26},{3,99},{4,28},{5,101},{6,30},{7,103},{8,16},{... | collective-permute-start | bytes 1622024 | tf_op jit(solution)/shard_map/ppermute | solution.py:57
  75.3 1.4 %shard_map.88 = (bf16[1024,512]{1,0:T(8,128)(2,1)S(1)}, bf16[528,512]{1,0:T(8,128)(2,1)S(1)}) custom-call(bf16[512,1024]{1,0:T(8,128)(2,1)S(1)} %shard_map.79.refs_0_, bf16[512,1024]{1,0:T(8,128)(2,1)S(1)} %collective-permute-done.10.refs_1_, bf16[256,1024]{1,0:T(8,128)(2,1)S(1)} %collective-permute-done.6.refs_4_.refs_2_.refs_6_, ...), custom_call_target="tpu_custom_call" | custom-call | tf_op jit(solution)/shard_map/pallas_call | solution.py:80
  76.8 1.4 %shard_map.89 = (bf16[1024,512]{1,0:T(8,128)(2,1)S(1)}, bf16[528,512]{1,0:T(8,128)(2,1)S(1)}) custom-call(bf16[512,1024]{1,0:T(8,128)(2,1)S(1)} %shard_map.79.refs_0_, bf16[512,1024]{1,0:T(8,128)(2,1)S(1)} %collective-permute-done.10.refs_1_, bf16[256,1024]{1,0:T(8,128)(2,1)S(1)} %collective-permute-done.11.refs_2_.refs_8_, ...), custom_call_target="tpu_custom_call" | custom-call | tf_op jit(solution)/shard_map/pallas_call | solution.py:80
  78.2 1.4 %shard_map.87 = (bf16[1024,512]{1,0:T(8,128)(2,1)S(1)}, f32[512,512]{1,0:T(8,128)S(1)}) custom-call(bf16[512,1024]{1,0:T(8,128)(2,1)S(1)} %shard_map.79.refs_0_, bf16[512,1024]{1,0:T(8,128)(2,1)S(1)} %collective-permute-done.10.refs_1_, bf16[256,1024]{1,0:T(8,128)(2,1)S(1)} %get-tuple-element.50.refs_2_.refs_4_, ...), custom_call_target="tpu_custom_call" | custom-call | tf_op jit(solution)/shard_map/pallas_call | solution.py:80
  79.7 1.2 %shard_map.92 = bf16[528,512]{1,0:T(8,128)(2,1)S(1)} custom-call(bf16[1024,512]{1,0:T(8,128)(2,1)S(1)} %get-tuple-element.64.refs_0_, bf16[1024,512]{1,0:T(8,128)(2,1)S(1)} %get-tuple-element.70.refs_1_, bf16[1024,512]{1,0:T(8,128)(2,1)S(1)} %get-tuple-element.75.refs_2_, bf16[1024,512]{1,0:T(8,128)(2,1)S(1)} %get-tuple-element.80.refs_3_, ...), custom_call_target="tpu_custom_call" | custom-call | tf_op jit(solution)/shard_map/pallas_call | solution.py:80
  81.0 2.8 %collective-permute-start.27 = (bf16[528,512]{1,0:T(8,128)(2,1)S(1)}, bf16[528,512]{1,0:T(8,128)(2,1)S(1)}, u32[]{:S(2)}, u32[]{:S(2)}) collective-permute-start(bf16[528,512]{1,0:T(8,128)(2,1)S(1)} %get-tuple-element.89), channel_id=1, source_target_pairs={{0,16},{1,65},{2,18},{3,67},{4,20},{5,69},{6,22},{7,71},{8,24},{9,... | collective-permute-start | bytes 1622024 | tf_op jit(solution)/shard_map/ppermute | solution.py:57
  83.9 2.3 %collective-permute-done.22.refs_13_.refs_3_ = bf16[528,512]{1,0:T(8,128)(2,1)S(1)} collective-permute-done((bf16[528,512]{1,0:T(8,128)(2,1)S(1)}, bf16[528,512]{1,0:T(8,128)(2,1)S(1)}, u32[]{:S(2)}, u32[]{:S(2)}) %collective-permute-start.22) | collective-permute-done | bytes 540704 | tf_op jit(solution)/shard_map/ppermute | solution.py:57
  86.2 1.2 %shard_map.91.refs_0_ = f32[512,512]{1,0:T(8,128)S(1)} custom-call(bf16[1024,512]{1,0:T(8,128)(2,1)S(1)} %get-tuple-element.64.refs_0_, bf16[1024,512]{1,0:T(8,128)(2,1)S(1)} %get-tuple-element.70.refs_1_, bf16[1024,512]{1,0:T(8,128)(2,1)S(1)} %get-tuple-element.75.refs_2_, bf16[1024,512]{1,0:T(8,128)(2,1)S(1)} %get-tuple-element.80.refs_3_, ...), custom_call_target="tpu_custom_call" | custom-call | tf_op jit(solution)/shard_map/pallas_call | solution.py:80
  87.5 1.6 %collective-permute-start.24 = (bf16[144,512]{1,0:T(8,128)(2,1)S(1)}, bf16[144,512]{1,0:T(8,128)(2,1)S(1)}, u32[]{:S(2)}, u32[]{:S(2)}) collective-permute-start(bf16[144,512]{1,0:T(8,128)(2,1)S(1)} %get-tuple-element.85), channel_id=1, source_target_pairs={{0,6},{1,7},{2,4},{3,5},{4,2},{5,3},{6,0},{7,1},{8,14},{9,15},{10,... | collective-permute-start | bytes 442376 | tf_op jit(solution)/shard_map/ppermute | solution.py:57
  89.1 0.9 collective-permute-start.25
  90.0 1.7 %collective-permute-start.26 = (bf16[144,512]{1,0:T(8,128)(2,1)S(1)}, bf16[144,512]{1,0:T(8,128)(2,1)S(1)}, u32[]{:S(2)}, u32[]{:S(2)}) collective-permute-start(bf16[144,512]{1,0:T(8,128)(2,1)S(1)} %get-tuple-element.87), channel_id=1, source_target_pairs={{0,2},{1,3},{2,0},{3,1},{4,6},{5,7},{6,4},{7,5},{8,10},{9,11},{10,... | collective-permute-start | bytes 442376 | tf_op jit(solution)/shard_map/ppermute | solution.py:57
  91.7 0.9 collective-permute-done.27.refs_4_
  92.6 1.3 %collective-permute-done.24.refs_5_.refs_2_ = bf16[144,512]{1,0:T(8,128)(2,1)S(1)} collective-permute-done((bf16[144,512]{1,0:T(8,128)(2,1)S(1)}, bf16[144,512]{1,0:T(8,128)(2,1)S(1)}, u32[]{:S(2)}, u32[]{:S(2)}) %collective-permute-start.24) | collective-permute-done | bytes 147488 | tf_op jit(solution)/shard_map/ppermute | solution.py:57
  94.2 2.1 %collective-permute-start.28 = (bf16[144,512]{1,0:T(8,128)(2,1)S(1)}, bf16[144,512]{1,0:T(8,128)(2,1)S(1)}, u32[]{:S(2)}, u32[]{:S(2)}) collective-permute-start(bf16[144,512]{1,0:T(8,128)(2,1)S(1)} %get-tuple-element.91), channel_id=1, source_target_pairs={{0,64},{1,17},{2,66},{3,19},{4,68},{5,21},{6,70},{7,23},{8,72},{9,... | collective-permute-start | bytes 442376 | tf_op jit(solution)/shard_map/ppermute | solution.py:57
  96.3 0.9 collective-permute-start.29
  97.8 3.2 %collective-permute-done.28.refs_7_ = bf16[144,512]{1,0:T(8,128)(2,1)S(1)} collective-permute-done((bf16[144,512]{1,0:T(8,128)(2,1)S(1)}, bf16[144,512]{1,0:T(8,128)(2,1)S(1)}, u32[]{:S(2)}, u32[]{:S(2)}) %collective-permute-start.28) | collective-permute-done | bytes 147488 | tf_op jit(solution)/shard_map/ppermute | solution.py:57
  100.9 1.7 %collective-permute-done.29.refs_8_ = bf16[144,512]{1,0:T(8,128)(2,1)S(1)} collective-permute-done((bf16[144,512]{1,0:T(8,128)(2,1)S(1)}, bf16[144,512]{1,0:T(8,128)(2,1)S(1)}, u32[]{:S(2)}, u32[]{:S(2)}) %collective-permute-start.29) | collective-permute-done | bytes 147488 | tf_op jit(solution)/shard_map/ppermute | solution.py:57
  102.7 1.1 %shard_map.95 = (f32[128,512]{1,0:T(8,128)}, f32[128,512]{1,0:T(8,128)}, f32[1,1]{1,0:T(1,128)}) custom-call(bf16[128,512]{1,0:T(8,128)(2,1)S(1)} %copy-done.2, f32[136,512]{1,0:T(8,128)S(1)} %get-tuple-element.84.refs_1_, bf16[144,512]{1,0:T(8,128)(2,1)S(1)} %collective-permute-done.24.refs_5_.refs_2_, ...), custom_call_target="tpu_custom_call" | custom-call | tf_op jit(solution)/shard_map/pallas_call | solution.py:80
  (44 shorter events, 6.0 us)
Async XLA Ops:
  0.6 9.5 %copy-start = (bf16[1280,512]{1,0:T(8,128)(2,1)S(1)}, bf16[1280,512]{1,0:T(8,128)(2,1)}, u32[]{:S(2)}) copy-start(bf16[1280,512]{1,0:T(8,128)(2,1)} %sketch_ref.1) | copy-start | bytes 3932164
  0.6 9.5 %copy-start.2 = (bf16[128,512]{1,0:T(8,128)(2,1)S(1)}, bf16[128,512]{1,0:T(8,128)(2,1)}, u32[]{:S(2)}) copy-start(bf16[128,512]{1,0:T(8,128)(2,1)} %refs_0_.1) | copy-start | bytes 393220
  0.7 9.5 %copy-start.4 = (bf16[128,1280]{1,0:T(8,128)(2,1)S(1)}, bf16[128,1280]{1,0:T(8,128)(2,1)}, u32[]{:S(2)}) copy-start(bf16[128,1280]{1,0:T(8,128)(2,1)} %teacher_ref.1) | copy-start | bytes 983044
  3.4 18.2 %copy-start.1 = (bf16[128,1024]{1,0:T(8,128)(2,1)S(1)}, bf16[128,1024]{1,0:T(8,128)(2,1)}, u32[]{:S(2)}) copy-start(bf16[128,1024]{1,0:T(8,128)(2,1)} %shard_map.76.refs_0_) | copy-start | bytes 786436
  3.4 6.7 %collective-permute-start = (bf16[128,1024]{1,0:T(8,128)(2,1)}, bf16[128,1024]{1,0:T(8,128)(2,1)S(1)}, u32[]{:S(2)}, u32[]{:S(2)}) collective-permute-start(bf16[128,1024]{1,0:T(8,128)(2,1)} %shard_map.76.refs_0_), channel_id=1, source_target_pairs={{0,32},{1,9},{2,34},{3,11},{4,36},{5,13},{6,38},{7,15},{8,40},{9,1... | collective-permute-start | bytes 786440 | tf_op jit(solution)/shard_map/ppermute | solution.py:57
  5.1 10.6 %collective-permute-start.5 = (bf16[128,1024]{1,0:T(8,128)(2,1)}, bf16[128,1024]{1,0:T(8,128)(2,1)S(1)}, u32[]{:S(2)}, u32[]{:S(2)}) collective-permute-start(bf16[128,1024]{1,0:T(8,128)(2,1)} %shard_map.76.refs_0_), channel_id=1, source_target_pairs={{0,96},{1,25},{2,98},{3,27},{4,100},{5,29},{6,102},{7,31},{8,104},... | collective-permute-start | bytes 786440 | tf_op jit(solution)/shard_map/ppermute | solution.py:57
  7.2 8.5 %collective-permute-start.4 = (bf16[128,1024]{1,0:T(8,128)(2,1)}, bf16[128,1024]{1,0:T(8,128)(2,1)S(1)}, u32[]{:S(2)}, u32[]{:S(2)}) collective-permute-start(bf16[128,1024]{1,0:T(8,128)(2,1)} %shard_map.76.refs_0_), channel_id=1, source_target_pairs={{0,64},{1,17},{2,66},{3,19},{4,68},{5,21},{6,70},{7,23},{8,72},{9,... | collective-permute-start | bytes 786440 | tf_op jit(solution)/shard_map/ppermute | solution.py:57
  10.6 9.6 %collective-permute-start.3 = (bf16[128,1024]{1,0:T(8,128)(2,1)S(1)}, bf16[128,1024]{1,0:T(8,128)(2,1)S(1)}, u32[]{:S(2)}, u32[]{:S(2)}) collective-permute-start(bf16[128,1024]{1,0:T(8,128)(2,1)S(1)} %shard_map.77.refs_0_), channel_id=1, source_target_pairs={{0,6},{1,7},{2,4},{3,5},{4,2},{5,3},{6,0},{7,1},{8,14},{9,15},{10,... | collective-permute-start | bytes 786440 | tf_op jit(solution)/shard_map/ppermute | solution.py:57
  14.8 6.9 %collective-permute-start.1 = (bf16[128,1024]{1,0:T(8,128)(2,1)S(1)}, bf16[128,1024]{1,0:T(8,128)(2,1)S(1)}, u32[]{:S(2)}, u32[]{:S(2)}) collective-permute-start(bf16[128,1024]{1,0:T(8,128)(2,1)S(1)} %shard_map.77.refs_0_), channel_id=1, source_target_pairs={{0,2},{1,3},{2,0},{3,1},{4,6},{5,7},{6,4},{7,5},{8,10},{9,11},{10,... | collective-permute-start | bytes 786440 | tf_op jit(solution)/shard_map/ppermute | solution.py:57
  21.8 13.0 %collective-permute-start.7 = (bf16[256,1024]{1,0:T(8,128)(2,1)S(1)}, bf16[256,1024]{1,0:T(8,128)(2,1)S(1)}, u32[]{:S(2)}, u32[]{:S(2)}) collective-permute-start(bf16[256,1024]{1,0:T(8,128)(2,1)S(1)} %get-tuple-element.50.refs_2_.refs_4_), channel_id=1, source_target_pairs={{0,24},{1,97},{2,26},{3,99},{4,28},{5,101},{6,30},{7,103},{8,16},{... | collective-permute-start | bytes 1572872 | tf_op jit(solution)/shard_map/ppermute | solution.py:57
  24.8 9.9 %collective-permute-start.6 = (bf16[256,1024]{1,0:T(8,128)(2,1)S(1)}, bf16[256,1024]{1,0:T(8,128)(2,1)S(1)}, u32[]{:S(2)}, u32[]{:S(2)}) collective-permute-start(bf16[256,1024]{1,0:T(8,128)(2,1)S(1)} %get-tuple-element.50.refs_2_.refs_4_), channel_id=1, source_target_pairs={{0,8},{1,33},{2,10},{3,35},{4,12},{5,37},{6,14},{7,39},{8,0},{9,41... | collective-permute-start | bytes 1572872 | tf_op jit(solution)/shard_map/ppermute | solution.py:57
  25.0 12.9 %collective-permute-start.9 = (bf16[256,1024]{1,0:T(8,128)(2,1)S(1)}, bf16[256,1024]{1,0:T(8,128)(2,1)S(1)}, u32[]{:S(2)}, u32[]{:S(2)}) collective-permute-start(bf16[256,1024]{1,0:T(8,128)(2,1)S(1)} %get-tuple-element.51.refs_3_.refs_5_), channel_id=1, source_target_pairs={{0,24},{1,97},{2,26},{3,99},{4,28},{5,101},{6,30},{7,103},{8,16},{... | collective-permute-start | bytes 1572872 | tf_op jit(solution)/shard_map/ppermute | solution.py:57
  26.0 13.6 %collective-permute-start.8 = (bf16[256,1024]{1,0:T(8,128)(2,1)S(1)}, bf16[256,1024]{1,0:T(8,128)(2,1)S(1)}, u32[]{:S(2)}, u32[]{:S(2)}) collective-permute-start(bf16[256,1024]{1,0:T(8,128)(2,1)S(1)} %get-tuple-element.51.refs_3_.refs_5_), channel_id=1, source_target_pairs={{0,8},{1,33},{2,10},{3,35},{4,12},{5,37},{6,14},{7,39},{8,0},{9,41... | collective-permute-start | bytes 1572872 | tf_op jit(solution)/shard_map/ppermute | solution.py:57
  26.9 7.9 %collective-permute-start.2 = (bf16[128,1024]{1,0:T(8,128)(2,1)S(1)}, bf16[128,1024]{1,0:T(8,128)(2,1)S(1)}, u32[]{:S(2)}, u32[]{:S(2)}) collective-permute-start(bf16[128,1024]{1,0:T(8,128)(2,1)S(1)} %shard_map.77.refs_0_), channel_id=1, source_target_pairs={{0,4},{1,5},{2,6},{3,7},{4,0},{5,1},{6,2},{7,3},{8,12},{9,13},{10,... | collective-permute-start | bytes 786440 | tf_op jit(solution)/shard_map/ppermute | solution.py:57
  39.7 2.7 %collective-permute-start.10 = (bf16[512,1024]{1,0:T(8,128)(2,1)S(1)}, bf16[512,1024]{1,0:T(8,128)(2,1)S(1)}, u32[]{:S(2)}, u32[]{:S(2)}) collective-permute-start(bf16[512,1024]{1,0:T(8,128)(2,1)S(1)} %shard_map.79.refs_0_), channel_id=1, source_target_pairs={{0,1},{1,0},{2,3},{3,2},{4,5},{5,4},{6,7},{7,6},{8,9},{9,8},{10,11... | collective-permute-start | bytes 3145736 | tf_op jit(solution)/shard_map/ppermute | solution.py:57
  39.8 9.3 %collective-permute-start.11 = (bf16[256,1024]{1,0:T(8,128)(2,1)S(1)}, bf16[256,1024]{1,0:T(8,128)(2,1)S(1)}, u32[]{:S(2)}, u32[]{:S(2)}) collective-permute-start(bf16[256,1024]{1,0:T(8,128)(2,1)S(1)} %collective-permute-done.7.refs_5_.refs_2_.refs_10_), channel_id=1, source_target_pairs={{0,8},{1,33},{2,10},{3,35},{4,12},{5,37},{6,14},{7,39},{8,0},{9,41... | collective-permute-start | bytes 1572872 | tf_op jit(solution)/shard_map/ppermute | solution.py:57
  40.0 10.4 %collective-permute-start.12 = (bf16[256,1024]{1,0:T(8,128)(2,1)S(1)}, bf16[256,1024]{1,0:T(8,128)(2,1)S(1)}, u32[]{:S(2)}, u32[]{:S(2)}) collective-permute-start(bf16[256,1024]{1,0:T(8,128)(2,1)S(1)} %collective-permute-done.8.refs_6_.refs_3_.refs_7_), channel_id=1, source_target_pairs={{0,24},{1,97},{2,26},{3,99},{4,28},{5,101},{6,30},{7,103},{8,16},{... | collective-permute-start | bytes 1572872 | tf_op jit(solution)/shard_map/ppermute | solution.py:57
  52.5 1.3 %collective-permute-start.13 = (f32[8,2048]{1,0:T(8,128)S(1)}, f32[8,2048]{1,0:T(8,128)S(1)}, u32[]{:S(2)}, u32[]{:S(2)}) collective-permute-start(f32[8,2048]{1,0:T(8,128)S(1)} %shard_map.82.own_ref), channel_id=1, source_target_pairs={{0,1},{1,0},{2,3},{3,2},{4,5},{5,4},{6,7},{7,6},{8,9},{9,8},{10,11... | collective-permute-start | bytes 196616 | tf_op jit(solution)/shard_map/ppermute | solution.py:57
  53.9 5.6 %collective-permute-start.16 = (f32[8,2048]{1,0:T(8,128)S(1)}, f32[8,2048]{1,0:T(8,128)S(1)}, u32[]{:S(2)}, u32[]{:S(2)}) collective-permute-start(f32[8,2048]{1,0:T(8,128)S(1)} %shard_map.83.own_ref), channel_id=1, source_target_pairs={{0,96},{1,7},{2,98},{3,5},{4,100},{5,3},{6,102},{7,1},{8,104},{9,1... | collective-permute-start | bytes 196616 | tf_op jit(solution)/shard_map/ppermute | solution.py:57
  56.7 5.8 %collective-permute-start.15 = (f32[8,2048]{1,0:T(8,128)S(1)}, f32[8,2048]{1,0:T(8,128)S(1)}, u32[]{:S(2)}, u32[]{:S(2)}) collective-permute-start(f32[8,2048]{1,0:T(8,128)S(1)} %shard_map.83.own_ref), channel_id=1, source_target_pairs={{0,64},{1,5},{2,66},{3,7},{4,68},{5,1},{6,70},{7,3},{8,72},{9,13},... | collective-permute-start | bytes 196616 | tf_op jit(solution)/shard_map/ppermute | solution.py:57
  57.5 5.0 %collective-permute-start.14 = (f32[8,2048]{1,0:T(8,128)S(1)}, f32[8,2048]{1,0:T(8,128)S(1)}, u32[]{:S(2)}, u32[]{:S(2)}) collective-permute-start(f32[8,2048]{1,0:T(8,128)S(1)} %shard_map.83.own_ref), channel_id=1, source_target_pairs={{0,32},{1,3},{2,34},{3,1},{4,36},{5,7},{6,38},{7,5},{8,40},{9,11},... | collective-permute-start | bytes 196616 | tf_op jit(solution)/shard_map/ppermute | solution.py:57
  62.6 1.3 %collective-permute-start.17 = (f32[8,2048]{1,0:T(8,128)S(1)}, f32[8,2048]{1,0:T(8,128)S(1)}, u32[]{:S(2)}, u32[]{:S(2)}) collective-permute-start(f32[8,2048]{1,0:T(8,128)S(1)} %shard_map.84.own_ref), channel_id=1, source_target_pairs={{0,1},{1,0},{2,3},{3,2},{4,5},{5,4},{6,7},{7,6},{8,9},{9,8},{10,11... | collective-permute-start | bytes 196616 | tf_op jit(solution)/shard_map/ppermute | solution.py:57
  64.1 6.3 %collective-permute-start.20 = (f32[8,2048]{1,0:T(8,128)S(1)}, f32[8,2048]{1,0:T(8,128)S(1)}, u32[]{:S(2)}, u32[]{:S(2)}) collective-permute-start(f32[8,2048]{1,0:T(8,128)S(1)} %get-tuple-element.57.own_ref), channel_id=1, source_target_pairs={{0,24},{1,25},{2,26},{3,27},{4,28},{5,29},{6,30},{7,31},{8,16},{9,... | collective-permute-start | bytes 196616 | tf_op jit(solution)/shard_map/ppermute | solution.py:57
  65.4 5.9 %collective-permute-start.19 = (f32[8,2048]{1,0:T(8,128)S(1)}, f32[8,2048]{1,0:T(8,128)S(1)}, u32[]{:S(2)}, u32[]{:S(2)}) collective-permute-start(f32[8,2048]{1,0:T(8,128)S(1)} %get-tuple-element.57.own_ref), channel_id=1, source_target_pairs={{0,16},{1,17},{2,18},{3,19},{4,20},{5,21},{6,22},{7,23},{8,24},{9,... | collective-permute-start | bytes 196616 | tf_op jit(solution)/shard_map/ppermute | solution.py:57
  66.9 4.4 %collective-permute-start.18 = (f32[8,2048]{1,0:T(8,128)S(1)}, f32[8,2048]{1,0:T(8,128)S(1)}, u32[]{:S(2)}, u32[]{:S(2)}) collective-permute-start(f32[8,2048]{1,0:T(8,128)S(1)} %get-tuple-element.57.own_ref), channel_id=1, source_target_pairs={{0,8},{1,9},{2,10},{3,11},{4,12},{5,13},{6,14},{7,15},{8,0},{9,1},... | collective-permute-start | bytes 196616 | tf_op jit(solution)/shard_map/ppermute | solution.py:57
  73.3 10.6 %collective-permute-start.21 = (bf16[528,512]{1,0:T(8,128)(2,1)S(1)}, bf16[528,512]{1,0:T(8,128)(2,1)S(1)}, u32[]{:S(2)}, u32[]{:S(2)}) collective-permute-start(bf16[528,512]{1,0:T(8,128)(2,1)S(1)} %get-tuple-element.81), channel_id=1, source_target_pairs={{0,24},{1,97},{2,26},{3,99},{4,28},{5,101},{6,30},{7,103},{8,16},{... | collective-permute-start | bytes 1622024 | tf_op jit(solution)/shard_map/ppermute | solution.py:57
  76.7 9.4 %collective-permute-start.22 = (bf16[528,512]{1,0:T(8,128)(2,1)S(1)}, bf16[528,512]{1,0:T(8,128)(2,1)S(1)}, u32[]{:S(2)}, u32[]{:S(2)}) collective-permute-start(bf16[528,512]{1,0:T(8,128)(2,1)S(1)} %get-tuple-element.82), channel_id=1, source_target_pairs={{0,8},{1,33},{2,10},{3,35},{4,12},{5,37},{6,14},{7,39},{8,0},{9,41... | collective-permute-start | bytes 1622024 | tf_op jit(solution)/shard_map/ppermute | solution.py:57
  80.9 6.5 %collective-permute-start.23 = (bf16[528,512]{1,0:T(8,128)(2,1)S(1)}, bf16[528,512]{1,0:T(8,128)(2,1)S(1)}, u32[]{:S(2)}, u32[]{:S(2)}) collective-permute-start(bf16[528,512]{1,0:T(8,128)(2,1)S(1)} %shard_map.92), channel_id=1, source_target_pairs={{0,1},{1,0},{2,3},{3,2},{4,5},{5,4},{6,7},{7,6},{8,9},{9,8},{10,11... | collective-permute-start | bytes 1622024 | tf_op jit(solution)/shard_map/ppermute | solution.py:57
  81.0 11.6 %collective-permute-start.27 = (bf16[528,512]{1,0:T(8,128)(2,1)S(1)}, bf16[528,512]{1,0:T(8,128)(2,1)S(1)}, u32[]{:S(2)}, u32[]{:S(2)}) collective-permute-start(bf16[528,512]{1,0:T(8,128)(2,1)S(1)} %get-tuple-element.89), channel_id=1, source_target_pairs={{0,16},{1,65},{2,18},{3,67},{4,20},{5,69},{6,22},{7,71},{8,24},{9,... | collective-permute-start | bytes 1622024 | tf_op jit(solution)/shard_map/ppermute | solution.py:57
  87.5 6.4 %collective-permute-start.24 = (bf16[144,512]{1,0:T(8,128)(2,1)S(1)}, bf16[144,512]{1,0:T(8,128)(2,1)S(1)}, u32[]{:S(2)}, u32[]{:S(2)}) collective-permute-start(bf16[144,512]{1,0:T(8,128)(2,1)S(1)} %get-tuple-element.85), channel_id=1, source_target_pairs={{0,6},{1,7},{2,4},{3,5},{4,2},{5,3},{6,0},{7,1},{8,14},{9,15},{10,... | collective-permute-start | bytes 442376 | tf_op jit(solution)/shard_map/ppermute | solution.py:57
  89.1 8.7 %collective-permute-start.25 = (bf16[144,512]{1,0:T(8,128)(2,1)S(1)}, bf16[144,512]{1,0:T(8,128)(2,1)S(1)}, u32[]{:S(2)}, u32[]{:S(2)}) collective-permute-start(bf16[144,512]{1,0:T(8,128)(2,1)S(1)} %get-tuple-element.86), channel_id=1, source_target_pairs={{0,4},{1,5},{2,6},{3,7},{4,0},{5,1},{6,2},{7,3},{8,12},{9,13},{10,... | collective-permute-start | bytes 442376 | tf_op jit(solution)/shard_map/ppermute | solution.py:57
  90.0 7.8 %collective-permute-start.26 = (bf16[144,512]{1,0:T(8,128)(2,1)S(1)}, bf16[144,512]{1,0:T(8,128)(2,1)S(1)}, u32[]{:S(2)}, u32[]{:S(2)}) collective-permute-start(bf16[144,512]{1,0:T(8,128)(2,1)S(1)} %get-tuple-element.87), channel_id=1, source_target_pairs={{0,2},{1,3},{2,0},{3,1},{4,6},{5,7},{6,4},{7,5},{8,10},{9,11},{10,... | collective-permute-start | bytes 442376 | tf_op jit(solution)/shard_map/ppermute | solution.py:57
  94.0 8.7 %copy-start.3 = (bf16[128,512]{1,0:T(8,128)(2,1)S(1)}, bf16[128,512]{1,0:T(8,128)(2,1)}, u32[]{:S(2)}) copy-start(bf16[128,512]{1,0:T(8,128)(2,1)} %refs_5_.1) | copy-start | bytes 393220
  94.2 6.7 %collective-permute-start.28 = (bf16[144,512]{1,0:T(8,128)(2,1)S(1)}, bf16[144,512]{1,0:T(8,128)(2,1)S(1)}, u32[]{:S(2)}, u32[]{:S(2)}) collective-permute-start(bf16[144,512]{1,0:T(8,128)(2,1)S(1)} %get-tuple-element.91), channel_id=1, source_target_pairs={{0,64},{1,17},{2,66},{3,19},{4,68},{5,21},{6,70},{7,23},{8,72},{9,... | collective-permute-start | bytes 442376 | tf_op jit(solution)/shard_map/ppermute | solution.py:57
  96.3 6.4 %collective-permute-start.29 = (bf16[144,512]{1,0:T(8,128)(2,1)S(1)}, bf16[144,512]{1,0:T(8,128)(2,1)S(1)}, u32[]{:S(2)}, u32[]{:S(2)}) collective-permute-start(bf16[144,512]{1,0:T(8,128)(2,1)S(1)} %get-tuple-element.92), channel_id=1, source_target_pairs={{0,96},{1,25},{2,98},{3,27},{4,100},{5,29},{6,102},{7,31},{8,104},... | collective-permute-start | bytes 442376 | tf_op jit(solution)/shard_map/ppermute | solution.py:57
  97.2 5.5 %collective-permute-start.30 = (bf16[144,512]{1,0:T(8,128)(2,1)S(1)}, bf16[144,512]{1,0:T(8,128)(2,1)S(1)}, u32[]{:S(2)}, u32[]{:S(2)}) collective-permute-start(bf16[144,512]{1,0:T(8,128)(2,1)S(1)} %get-tuple-element.93), channel_id=1, source_target_pairs={{0,32},{1,9},{2,34},{3,11},{4,36},{5,13},{6,38},{7,15},{8,40},{9,1... | collective-permute-start | bytes 442376 | tf_op jit(solution)/shard_map/ppermute | solution.py:57
